TPU v7x, 32 devices: a whole 2x2x4 slice. The times are simulated.
32 devices in a mesh: dp: 2 (over core), seq: 4 (over y, x), expert: 4 (over z).
Axes of the slice: x: 2, y: 2, z: 4, core: 2. Of those that a mesh axis runs over, the one named last changes fastest.
Arguments:
- query_in: bfloat16 [2, 512, 4096], P('dp', 'seq', 'expert'), may hold values from -21 to 21
- key_in: bfloat16 [2, 512, 1024], P('dp', 'seq', 'expert'), may hold values from -6 to 6
- value_in: bfloat16 [2, 512, 1024], P('dp', 'seq', 'expert'), may hold values from -6 to 6
- resid_in: bfloat16 [2, 512, 4096], P('dp', 'seq', 'expert'), may hold values from -6 to 6
- out_grad: bfloat16 [2, 512, 4096], P('dp', 'seq', 'expert'), may hold values from -6 to 6
- o_weight: bfloat16 [4096, 4096], P('expert', 'seq'), may hold values from -0.09375 to 0.09375
- router_weight: bfloat16 [4096, 4], P('expert'), may hold values from -0.09375 to 0.09375
- route_ids: int32 [2, 512, 2], P('dp', 'seq'), may hold values from 0 to 3, all different within a row; in each aligned block of 128 rows (0 to 127, 128 to 255, ..., all dimensions but the last counted through in order) at most 128 rows name the same one
- expert_out: bfloat16 [2, 2048, 4096], P('dp', ('seq', 'expert')), may hold values from -6 to 6
Outputs:
- query_grad: bfloat16 [2, 512, 4096], P('dp', 'seq', 'expert')
- key_grad: bfloat16 [2, 512, 1024], P('dp', 'seq', 'expert')
- value_grad: bfloat16 [2, 512, 1024], P('dp', 'seq', 'expert')
- router_grad: float32 [4096, 4], P('expert')
- expert_grad: bfloat16 [2, 2048, 4096], P('dp', ('seq', 'expert'))
Inputs may be any that keep to these rules, and one draw needn't show every extreme that they name: `route_ids`: the two experts of a token differ; among the 128 tokens of one index of seq at most 128 name one expert, and some such group in every draw has exactly 128 naming one expert.
All inputs are finite; a program needn't handle non-finite values.
Results may differ from a plain program's by a relative error of at most 0.0078.
Values may be sent and summed in bfloat16 or wider, within the bound.
No kernel may reach another device: no remote copies, remote signals or barrier semaphores. Data moves between devices by JAX's collectives and lax.ppermute only.
A program may use at most 64 MiB of HBM per device.

v0:
```python
import math

import jax
import jax.numpy as jnp
from jax import lax
from jax.sharding import PartitionSpec as P

HEADS = 32
KV_HEADS = 8
HEAD_DIM = 128
D = 4096


NEG_FILL = -1e30
NORM_EPS = 1e-05


def head_rows(matrix, kv_count):
    tok_rows = matrix.shape[0]
    group_size = HEADS // KV_HEADS
    split_view = matrix.reshape(tok_rows, kv_count, group_size, HEAD_DIM)
    return jnp.transpose(split_view, (1, 2, 0, 3)).reshape(
        kv_count, group_size * tok_rows, HEAD_DIM
    )


def token_cols(matrix, tok_rows):
    kv_count = matrix.shape[0]
    group_size = matrix.shape[1] // tok_rows
    split_view = matrix.reshape(kv_count, group_size, tok_rows, HEAD_DIM)
    return jnp.transpose(split_view, (2, 0, 1, 3)).reshape(
        tok_rows, kv_count * group_size * HEAD_DIM
    )


def key_blocks(key_part, value_part):
    key_count = key_part.shape[0]
    block_len = math.gcd(key_count, 512)
    kv_count = key_part.shape[1] // HEAD_DIM
    steps_count = key_count // block_len
    key_stack = key_part.reshape(steps_count, block_len, kv_count, HEAD_DIM)
    value_stack = value_part.reshape(steps_count, block_len, kv_count, HEAD_DIM)
    offsets = block_len * jnp.arange(steps_count, dtype=jnp.int32)
    return (key_stack, value_stack, offsets, block_len)


def forward_fold(query_heads, query_pos):
    score_scale = HEAD_DIM ** (-0.5)

    def forward_fold_keys(carry_in, key_piece, start_row):
        key_stack, value_stack, offsets, block_len = key_blocks(key_piece[0], key_piece[1])

        def forward_one_block(carry_state, blocks):
            run_max, run_sum, run_out = carry_state
            key_block, value_block, block_start = blocks
            scores = (
                jnp.einsum(
                    "hrd,khd->hrk", query_heads, key_block, preferred_element_type=jnp.float32
                )
                * score_scale
            )
            key_pos = block_start + jnp.arange(block_len, dtype=jnp.int32)
            allowed = (key_pos[None, :] <= query_pos[:, None])[None]
            row_top = jnp.maximum(run_max, jnp.max(jnp.where(allowed, scores, NEG_FILL), axis=-1))
            weights = jnp.exp(jnp.where(allowed, scores - row_top[..., None], NEG_FILL))
            shrink = jnp.exp(run_max - row_top)
            run_sum = run_sum * shrink + jnp.sum(weights, axis=-1)
            run_out = run_out * shrink[..., None] + jnp.einsum(
                "hrk,khd->hrd",
                weights.astype(jnp.bfloat16),
                value_block,
                preferred_element_type=jnp.float32,
            )
            return ((row_top, run_sum, run_out), None)

        result, _ = lax.scan(forward_one_block, carry_in, (key_stack, value_stack, offsets))
        return result

    return forward_fold_keys


def backward_fold(query_heads, grad_heads, log_norm, delta_row, query_pos):
    score_scale = HEAD_DIM ** (-0.5)

    def backward_fold_keys(carry_in, key_piece, start_row):
        key_stack, value_stack, offsets, block_len = key_blocks(key_piece[0], key_piece[1])

        def backward_one_block(dq_acc, blocks):
            key_block, value_block, block_start = blocks
            scores = (
                jnp.einsum(
                    "hrd,khd->hrk", query_heads, key_block, preferred_element_type=jnp.float32
                )
                * score_scale
            )
            key_pos = block_start + jnp.arange(block_len, dtype=jnp.int32)
            allowed = (key_pos[None, :] <= query_pos[:, None])[None]
            probs = jnp.exp(jnp.where(allowed, scores - log_norm[..., None], NEG_FILL))
            dprobs = jnp.einsum(
                "hrd,khd->hrk", grad_heads, value_block, preferred_element_type=jnp.float32
            )
            dscores = (probs * (dprobs - delta_row[..., None])).astype(jnp.bfloat16)
            dq_acc = (
                dq_acc
                + jnp.einsum("hrk,khd->hrd", dscores, key_block, preferred_element_type=jnp.float32)
                * score_scale
            )
            dk_block = (
                jnp.einsum("hrk,hrd->khd", dscores, query_heads, preferred_element_type=jnp.float32)
                * score_scale
            )
            dv_block = jnp.einsum(
                "hrk,hrd->khd",
                probs.astype(jnp.bfloat16),
                grad_heads,
                preferred_element_type=jnp.float32,
            )
            return (dq_acc, (dk_block, dv_block))

        dq_acc, key_terms = lax.scan(
            backward_one_block, carry_in[0], (key_stack, value_stack, offsets)
        )
        key_count = key_piece[0].shape[0]
        dk_rows = key_terms[0].reshape(key_count, -1)
        dv_rows = key_terms[1].reshape(key_count, -1)
        return (dq_acc, dk_rows, dv_rows)

    return backward_fold_keys


def local(
    query_in, key_in, value_in, resid_in, out_grad, o_weight, router_weight, route_ids, expert_out
):
    query_loc = query_in[0]
    key_loc = key_in[0]
    value_loc = value_in[0]
    resid_loc = resid_in[0]
    grad_in = out_grad[0]
    route_loc = route_ids[0]
    tok_rows = query_loc.shape[0]
    expert_count = router_weight.shape[1]
    capacity = expert_out.shape[1]
    my_expert = lax.axis_index("expert")
    resid_f32 = resid_loc.astype(jnp.float32)
    raw_part = jnp.dot(resid_loc, router_weight, preferred_element_type=jnp.float32)
    square_part = jnp.sum(resid_f32 * resid_f32, axis=1)
    raw_logits, square_sums = lax.psum((raw_part, square_part), "expert")
    inv_rms = lax.rsqrt(square_sums / D + NORM_EPS)
    logits = inv_rms[:, None] * raw_logits
    expert_iota = jnp.arange(expert_count, dtype=jnp.int32)
    first_mask = route_loc[:, 0:1] == expert_iota[None, :]
    second_mask = route_loc[:, 1:2] == expert_iota[None, :]
    choose_a = first_mask.astype(jnp.float32)
    choose_b = second_mask.astype(jnp.float32)
    logit_a = jnp.sum(logits * choose_a, axis=1)
    logit_b = jnp.sum(logits * choose_b, axis=1)
    gate_a = jax.nn.sigmoid(logit_a - logit_b)
    gate_b = jax.nn.sigmoid(logit_b - logit_a)
    gate_table = gate_a[:, None] * choose_a + gate_b[:, None] * choose_b
    member = (first_mask | second_mask).astype(jnp.int32)
    slot_index = jnp.cumsum(member, axis=0) - member
    slot_iota = jnp.arange(capacity, dtype=jnp.int32)
    dispatch_mask = (member.T[:, None, :] == 1) & (
        slot_index.T[:, None, :] == slot_iota[None, :, None]
    )
    dispatch_f32 = dispatch_mask.astype(jnp.float32)
    outgoing = jnp.einsum(
        "ect,td->ecd",
        dispatch_mask.astype(jnp.bfloat16),
        grad_in,
        preferred_element_type=jnp.float32,
    ).astype(jnp.bfloat16)
    arrived = lax.all_to_all(outgoing, "expert", split_axis=0, concat_axis=2, tiled=True)
    slot_grads = arrived[0]
    saved_rows = expert_out[0]
    dgate_mine = jnp.einsum("cd,cd->c", slot_grads, saved_rows, preferred_element_type=jnp.float32)
    onehot_mine = (expert_iota == my_expert).astype(jnp.float32)
    place_mine = jnp.sum(dispatch_f32 * onehot_mine[:, None, None], axis=0)
    gate_column = jnp.sum(gate_table * onehot_mine[None, :], axis=1)
    gate_slot = jnp.sum(place_mine * gate_column[None, :], axis=1)
    expert_grad = (gate_slot[:, None] * slot_grads.astype(jnp.float32)).astype(jnp.bfloat16)
    dgate_all = lax.all_gather(dgate_mine, "expert", axis=0, tiled=True)
    dgate_tok = jnp.einsum(
        "ect,ec->te",
        dispatch_f32,
        dgate_all.reshape(expert_count, capacity),
        precision=lax.Precision.HIGHEST,
    )
    dgate_a = jnp.sum(dgate_tok * choose_a, axis=1)
    dgate_b = jnp.sum(dgate_tok * choose_b, axis=1)
    dlogit_a = gate_a * gate_b * (dgate_a - dgate_b)
    dlogits = dlogit_a[:, None] * (choose_a - choose_b)
    back_proj = jnp.dot(
        dlogits, router_weight.astype(jnp.float32).T, precision=lax.Precision.HIGHEST
    )
    along_raw = jnp.sum(raw_logits * dlogits, axis=1)
    resid_grad = (
        grad_in.astype(jnp.float32)
        + inv_rms[:, None] * back_proj
        - (along_raw * inv_rms**3 / D)[:, None] * resid_f32
    )
    resid_grad = resid_grad.astype(jnp.bfloat16)
    token_total = lax.axis_size("dp") * lax.axis_size("seq") * tok_rows
    router_part = (
        jnp.dot(resid_f32.T, inv_rms[:, None] * dlogits, precision=lax.Precision.HIGHEST)
        / token_total
    )
    router_grad = lax.psum(router_part, ("dp", "seq"))
    resid_whole = lax.all_gather(resid_grad, "expert", axis=1, tiled=True)
    attn_grad = lax.dot_general(
        resid_whole,
        lax.all_gather(o_weight, "seq", axis=1, tiled=True),
        (((1,), (1,)), ((), ())),
        preferred_element_type=jnp.float32,
    ).astype(jnp.bfloat16)
    kv_count = key_loc.shape[1] // HEAD_DIM
    group_size = HEADS // KV_HEADS
    query_heads = head_rows(query_loc, kv_count)
    grad_heads = head_rows(attn_grad, kv_count)
    seq_base = lax.axis_index("seq") * tok_rows
    query_pos = jnp.tile(seq_base + jnp.arange(tok_rows, dtype=jnp.int32), group_size)
    head_count = group_size * tok_rows
    initial = (
        jnp.full((kv_count, head_count), NEG_FILL, jnp.float32),
        jnp.zeros((kv_count, head_count), jnp.float32),
        jnp.zeros((kv_count, head_count, HEAD_DIM), jnp.float32),
    )
    fold_forward = forward_fold(query_heads, query_pos)
    every_key, every_value = (
        lax.all_gather(key_loc, "seq", axis=0, tiled=True),
        lax.all_gather(value_loc, "seq", axis=0, tiled=True),
    )
    run_max, run_sum, run_out = fold_forward(initial, (every_key, every_value), jnp.int32(0))
    log_norm = run_max + jnp.log(run_sum)
    attn_out = run_out / run_sum[..., None]
    delta_row = jnp.sum(grad_heads.astype(jnp.float32) * attn_out, axis=-1)
    zero_dq = jnp.zeros((kv_count, head_count, HEAD_DIM), jnp.float32)
    full_len = tok_rows * lax.axis_size("seq")
    zero_terms = jnp.zeros((full_len, kv_count * HEAD_DIM), jnp.float32)
    back_init = (zero_dq, zero_terms, zero_terms)
    fold_backward = backward_fold(query_heads, grad_heads, log_norm, delta_row, query_pos)
    back_out = fold_backward(back_init, (every_key, every_value), jnp.int32(0))
    query_grad = token_cols(back_out[0], tok_rows).astype(jnp.bfloat16)
    dk_rows, dv_rows = (
        lax.psum_scatter(back_out[1], "seq", scatter_dimension=0, tiled=True),
        lax.psum_scatter(back_out[2], "seq", scatter_dimension=0, tiled=True),
    )
    key_grad = dk_rows.astype(jnp.bfloat16)
    value_grad = dv_rows.astype(jnp.bfloat16)
    return (query_grad[None], key_grad[None], value_grad[None], router_grad, expert_grad[None])


def solution(mesh):
    placed = (
        P("dp", "seq", "expert"),
        P("dp", "seq", "expert"),
        P("dp", "seq", "expert"),
        P("dp", "seq", "expert"),
        P("dp", "seq", "expert"),
        P("expert", "seq"),
        P("expert", None),
        P("dp", "seq", None),
        P("dp", ("seq", "expert"), None),
    )
    return jax.shard_map(
        local,
        mesh=mesh,
        in_specs=placed,
        out_specs=(
            P("dp", "seq", "expert"),
            P("dp", "seq", "expert"),
            P("dp", "seq", "expert"),
            P("expert", None),
            P("dp", ("seq", "expert"), None),
        ),
        check_vma=False,
    )
```

profile of v0, /device:TPU:8, one launch (start us, length us, event | category | flops | bytes accessed | tf_op | source)
XLA Modules:
  0.0 257.0 jit_solution(2441352669457672481)
XLA Ops:
  8.3 2.4 convolution_convert_fusion
  10.7 5.3 %all-to-all-start = ((bf16[4,128,1024]{2,1,0:T(8,128)(2,1)}), bf16[4,128,1024]{2,1,0:T(8,128)(2,1)S(1)}, u32[]{:S(2)}, u32[]{:S(2)}) async-start(bf16[4,128,1024]{2,1,0:T(8,128)(2,1)} %convolution_convert_fusion), calls=%async_computation | async-start | bytes 2097152 | tf_op jit(solution)/shard_map/all_to_all | solution.py:173
  16.3 25.6 %all-reduce = (f32[128,4]{0,1:T(4,128)S(1)}, f32[128]{0:T(128)S(1)}) all-reduce(f32[128,4]{0,1:T(4,128)S(1)} %fusion.27, f32[128]{0:T(128)S(1)} %fusion.24), channel_id=1, replica_groups=mesh['dp'=2,'seq'=4,'expert'=4] {'expert'}, use_global_device_ids=true, to_apply=%region_4.0 | all-reduce | flops 640 | bytes 5120 | tf_op jit(solution)/shard_map/psum | solution.py:147
  41.9 1.3 copy.111
  43.2 1.4 bitcast_convert_fusion
  44.6 1.9 copy.134
  46.5 2.2 multiply_reduce_fusion
  48.7 9.0 %all-gather.2 = f32[4,1,128]{2,1,0:T(1,128)S(1)} all-gather(f32[1,1,128]{2,1,0:T(1,128)S(1)} %bitcast.92), channel_id=1, replica_groups=mesh['dp'=2,'seq'=4,'expert'=4] {'expert'}, dimensions={0}, use_global_device_ids=true | all-gather | bytes 2560 | tf_op jit(solution)/shard_map/all_gather | solution.py:182
  58.0 1.2 fusion.10
  61.6 9.0 %all-gather = bf16[1,512,256]{1,2,0:T(8,128)(2,1)S(1)} all-gather(bf16[1,128,256]{1,2,0:T(8,128)(2,1)S(1)} %copy.106), channel_id=2, replica_groups=mesh['dp'=2,'seq'=4,'expert'=4] {'seq'}, dimensions={1}, use_global_device_ids=true | all-gather | bytes 327680 | tf_op jit(solution)/shard_map/all_gather | solution.py:230
  70.6 9.6 %all-gather.1 = bf16[1,512,256]{1,2,0:T(8,128)(2,1)} all-gather(bf16[1,128,256]{1,2,0:T(8,128)(2,1)S(1)} %copy.113), channel_id=3, replica_groups=mesh['dp'=2,'seq'=4,'expert'=4] {'seq'}, dimensions={1}, use_global_device_ids=true | all-gather | bytes 327680 | tf_op jit(solution)/shard_map/all_gather | solution.py:231
  80.4 1.7 select_reduce_fusion
  82.6 4.7 %all-gather.6.cloned.1.call-done = bf16[128,4096]{1,0:T(8,128)(2,1)} async-done(((bf16[128,1024]{1,0:T(8,128)(2,1)}), bf16[128,4096]{1,0:T(8,128)(2,1)}) %all-gather.6.cloned.1.call-update) | async-done | bytes 1048592 | tf_op jit(solution)/shard_map/all_gather | solution.py:209
  87.3 89.0 %all-gather.8.cloned.1.call-done = bf16[1024,4096]{1,0:T(8,128)(2,1)} async-done(((bf16[1024,1024]{1,0:T(8,128)(2,1)}), bf16[1024,4096]{1,0:T(8,128)(2,1)}) %all-gather.8.cloned.1.call-update) | async-done | bytes 8388624 | tf_op jit(solution)/shard_map/all_gather | solution.py:212
  176.3 7.3 %convolution_convert_fusion.1 = bf16[128,1024]{1,0:T(8,128)(2,1)} fusion(bf16[128,4096]{1,0:T(8,128)(2,1)} %all-gather.6.cloned.1.call-done, bf16[1024,4096]{1,0:T(8,128)(2,1)} %all-gather.8.cloned.1.call-done), kind=kOutput, calls=%fused_computation.22 | convolution fusion | flops 1073872896 | bytes 9699328 | tf_op jit(solution)/shard_map/dot_general | solution.py:210
  183.6 1.8 reshape.222
  185.4 1.9 copy.112
  187.3 1.8 reshape.223
  189.1 2.0 fusion.11
  192.0 1.0 copy-done.1
  192.9 1.2 fusion.4
  194.2 2.0 copy.123
  196.4 1.5 bitcast_convert_fusion.1
  197.9 3.0 %copy.126 = f32[1,128,4,1024]{1,3,2,0:T(8,128)} copy(f32[1,128,4,1024]{3,1,2,0:T(8,128)} %bitcast_convert_fusion.1) | data formatting | bytes 4194304 | tf_op jit(solution)/shard_map/convert_element_type | solution.py:181
  201.8 1.0 copy.125
  202.9 1.8 fusion
  204.7 1.3 copy.128
  206.2 27.0 %psum.23 = f32[1024,4]{0,1:T(4,128)} all-reduce(f32[1024,4]{0,1:T(4,128)S(1)} %fusion.12), channel_id=1, replica_groups=mesh['dp'=2,'seq'=4,'expert'=4] {'dp','seq'}, use_global_device_ids=true, to_apply=%region_14.15 | all-reduce | flops 4096 | bytes 32768 | tf_op jit(solution)/shard_map/psum | solution.py:208
  234.0 0.9 convert_element_type.124
  234.9 0.9 convert_bitcast_fusion.1
  236.5 12.4 %reduce-scatter.5.cloned.1.call-done = f32[128,256]{1,0:T(8,128)} async-done(((f32[512,256]{1,0:T(8,128)}), f32[128,256]{1,0:T(8,128)}) %reduce-scatter.5.cloned.1.call-update) | async-done | bytes 131088 | tf_op jit(solution)/shard_map/reduce_scatter | solution.py:246
  249.0 1.5 convert_bitcast_fusion
  (80 shorter events, 8.4 us)
Async XLA Ops:
  7.2 9.0 %copy-start = (bf16[1024,4]{0,1:T(4,128)(2,1)S(1)}, bf16[1024,4]{0,1:T(4,128)(2,1)}, u32[]{:S(2)}) copy-start(bf16[1024,4]{0,1:T(4,128)(2,1)} %param.15) | copy-start | bytes 24580
  7.2 8.8 %copy-start.3 = (bf16[1,128,1024]{2,1,0:T(8,128)(2,1)S(1)}, bf16[1,128,1024]{2,1,0:T(8,128)(2,1)}, u32[]{:S(2)}) copy-start(bf16[1,128,1024]{2,1,0:T(8,128)(2,1)} %param.12) | copy-start | bytes 786436
  10.7 31.2 %all-to-all-start = ((bf16[4,128,1024]{2,1,0:T(8,128)(2,1)}), bf16[4,128,1024]{2,1,0:T(8,128)(2,1)S(1)}, u32[]{:S(2)}, u32[]{:S(2)}) async-start(bf16[4,128,1024]{2,1,0:T(8,128)(2,1)} %convolution_convert_fusion), calls=%async_computation | async-start | bytes 2097152 | tf_op jit(solution)/shard_map/all_to_all | solution.py:173
  16.0 71.3 %all-gather.6.cloned.1.call-start = ((), (), s32[]{:S(2)}) async-start(), calls=%async_computation.3 | async-start | bytes 1310720 | tf_op jit(solution)/shard_map/all_gather | solution.py:209
  46.5 11.6 %copy-start.10 = (bf16[1,128,1024]{2,1,0:T(8,128)(2,1)S(1)}, bf16[1,128,1024]{2,1,0:T(8,128)(2,1)}, u32[]{:S(2)}) copy-start(bf16[1,128,1024]{2,1,0:T(8,128)(2,1)} %param.13) | copy-start | bytes 786436
  48.7 11.4 %copy-start.12 = (bf16[1,128,1024]{2,1,0:T(8,128)(2,1)S(1)}, bf16[1,128,1024]{2,1,0:T(8,128)(2,1)}, u32[]{:S(2)}) copy-start(bf16[1,128,1024]{2,1,0:T(8,128)(2,1)} %param.9) | copy-start | bytes 786436
  59.2 2.1 copy-start.15
  59.2 2.2 copy-start.16
  59.3 117.0 %all-gather.8.cloned.1.call-start = ((), (), s32[]{:S(2)}) async-start(), calls=%async_computation.4 | async-start | bytes 10485760 | tf_op jit(solution)/shard_map/all_gather | solution.py:212
  60.0 174.8 %reduce-scatter.3.cloned.1.call-start = ((), (), s32[]{:S(2)}) async-start(), calls=%async_computation.5 | async-start | bytes 655360 | tf_op jit(solution)/shard_map/reduce_scatter | solution.py:245
  70.6 9.8 %copy-start.8 = (bf16[1,512,256]{1,2,0:T(8,128)(2,1)}, bf16[1,512,256]{1,2,0:T(8,128)(2,1)S(1)}, u32[]{:S(2)}) copy-start(bf16[1,512,256]{1,2,0:T(8,128)(2,1)S(1)} %all-gather) | copy-start | bytes 786436
  80.4 2.2 copy-start.4
  189.1 2.0 copy-start.5
  189.1 2.0 copy-start.11
  189.1 2.0 copy-start.13
  191.1 1.8 copy-start.7
  192.0 1.0 copy-start.1
  196.2 52.7 %reduce-scatter.5.cloned.1.call-start = ((), (), s32[]{:S(2)}) async-start(), calls=%async_computation.6 | async-start | bytes 655360 | tf_op jit(solution)/shard_map/reduce_scatter | solution.py:246
  197.9 3.1 %copy-start.6 = (pred[512,512]{0,1:T(8,128)(4,1)S(1)}, pred[512,512]{0,1:T(8,128)(4,1)}, u32[]{:S(2)}) copy-start(pred[512,512]{0,1:T(8,128)(4,1)} %copy-done.4) | copy-start | bytes 786436
  197.9 3.1 %copy-start.14 = (bf16[2,512,128]{1,2,0:T(8,128)(2,1)S(1)}, bf16[2,512,128]{1,2,0:T(8,128)(2,1)}, u32[]{:S(2)}) copy-start(bf16[2,512,128]{1,2,0:T(8,128)(2,1)} %reshape.223) | copy-start | bytes 786436
  202.8 30.4 %copy-start.2 = (bf16[2,512,512]{1,2,0:T(8,128)(2,1)S(1)}, bf16[2,512,512]{1,2,0:T(8,128)(2,1)}, u32[]{:S(2)}) copy-start(bf16[2,512,512]{1,2,0:T(8,128)(2,1)} %copy-done.1) | copy-start | bytes 3145732
  202.8 30.4 %copy-start.9 = (bf16[1,512,256]{1,2,0:T(8,128)(2,1)S(1)}, bf16[1,512,256]{1,2,0:T(8,128)(2,1)}, u32[]{:S(2)}) copy-start(bf16[1,512,256]{1,2,0:T(8,128)(2,1)} %copy-done.8) | copy-start | bytes 786436
Sparse Core Ops, SparseCore 0:
  59.4 27.8 all-gather.5
  89.1 87.1 all-gather.7
  196.4 24.8 reduce-scatter.2
  224.1 24.7 reduce-scatter.4
where the time goes:
time: 259 us; the launch traced here: 257 us
  waiting for transfers between devices  107 us (41%)
  blocking collectives  80.2 us (31%)
  local copies, waits for them, and re-layouts  21.2 us (8%)
  matrix products  18.5 us (7%)
  between operations  14 us (5%)
  other arithmetic  10.7 us (4%)
  starting transfers between devices  5.44 us (2%)
    all_gather x1, waiting for transfers between devices, local(): lax.all_gather(o_weight, 'seq', axis=1, tiled=True)  89 us
    psum x1, blocking collectives, local(): router_grad = lax.psum(router_part, ('dp', 'seq'))  27 us
    psum x1, blocking collectives, local(): raw_logits, square_sums = lax.psum((raw_part, square_part), 'expert')  25.6 us
    reduce_scatter x1, waiting for transfers between devices, local(): lax.psum_scatter(back_out[2], 'seq', scatter_dimension=0, tiled=True)  12.4 us
    all_gather x1, blocking collectives, local(): lax.all_gather(value_loc, 'seq', axis=0, tiled=True)  9.6 us
    all_gather x1, blocking collectives, local(): dgate_all = lax.all_gather(dgate_mine, 'expert', axis=0, tiled=True)  9.01 us
    all_gather x1, blocking collectives, local(): lax.all_gather(key_loc, 'seq', axis=0, tiled=True)  9 us
    dot_general x1, matrix products, local(): lax.dot_general(resid_whole, lax.all_gather(o_weight, 'seq', axis=1, tile...  7.33 us
  transfers between devices with their start and end apart: 5, of which 3 were waited for; matrix products, arithmetic and copies ran while one was open for 7% of the time, Pallas kernels for 0%

commit v1 on v0

--- a/solution.py
+++ b/solution.py
@@ -3,6 +3,8 @@
 import jax
 import jax.numpy as jnp
 from jax import lax
+from jax.experimental import pallas as pl
+from jax.experimental.pallas import tpu as pltpu
 from jax.sharding import PartitionSpec as P
 
 HEADS = 32
@@ -250,6 +252,421 @@
     return (query_grad[None], key_grad[None], value_grad[None], router_grad, expert_grad[None])
 
 
+ANY_VMEM = pltpu.VMEM
+VMEM_LIMIT = 56 * 1024 * 1024
+NT = (((1,), (1,)), ((), ()))
+TN = (((0,), (0,)), ((), ()))
+LANES = 128
+
+
+def params():
+    return pltpu.CompilerParams(vmem_limit_bytes=VMEM_LIMIT)
+
+
+def partner(array, axis, count, distance):
+    return lax.ppermute(array, axis, [(i, i ^ distance) for i in range(count)])
+
+
+def iota(shape, axis):
+    return lax.broadcasted_iota(jnp.int32, shape, axis)
+
+
+def whole(shape):
+    return pl.BlockSpec(shape, lambda *_: (0,) * len(shape))
+
+
+def column(matrix, lane):
+    lanes = iota(matrix.shape, 1)
+    return jnp.sum(jnp.where(lanes == lane, matrix, 0.0), axis=1, keepdims=True)
+
+
+def as_rows(matrix):
+    return jnp.transpose(matrix)[0:8]
+
+
+def as_columns(rows):
+    count = rows.shape[1]
+    return jnp.transpose(
+        jnp.concatenate([rows, jnp.zeros((LANES - rows.shape[0], count), rows.dtype)], axis=0)
+    )
+
+
+def prepare_kernel(meta, route, router_pad, resid, saved, pack, place, saved_tok):
+    my_expert = meta[2]
+    tok_rows, feats = resid.shape
+    capacity = saved.shape[0]
+    experts = EXPERTS_ROW
+    member = (route[:, 0:1] == my_expert) | (route[:, 1:2] == my_expert)
+    earlier = (iota((tok_rows, tok_rows), 1) < iota((tok_rows, tok_rows), 0)).astype(
+        jnp.float32
+    ).astype(jnp.bfloat16)
+    member_wide = jnp.broadcast_to(member.astype(jnp.float32), (tok_rows, capacity))
+    slot = jnp.dot(earlier, member_wide.astype(jnp.bfloat16), preferred_element_type=jnp.float32)
+    slot_lane = iota((tok_rows, capacity), 1).astype(jnp.float32)
+    placed = jnp.where(slot == slot_lane, member_wide, 0.0).astype(jnp.bfloat16)
+    place[...] = placed
+    saved_tok[...] = jnp.dot(placed, saved[...], preferred_element_type=jnp.float32).astype(
+        jnp.bfloat16
+    )
+    resid_f32 = resid[...].astype(jnp.float32)
+    raw = jnp.dot(resid[...], router_pad[...], preferred_element_type=jnp.float32)
+    square = jnp.sum(resid_f32 * resid_f32, axis=1, keepdims=True)
+    lanes = iota(raw.shape, 1)
+    pack[:, 0:feats] = as_rows(router_pad[...].astype(jnp.float32))
+    pack[:, feats : feats + tok_rows] = as_rows(jnp.where(lanes == experts, square, raw))
+
+
+def gate_grad_kernel(meta, route, saved_tok, g0, g1, g2, g3, terms):
+    my_expert = meta[2]
+    tok_rows, feats = g0.shape
+    total = jnp.zeros((tok_rows, 1), jnp.float32)
+    for k, grad in enumerate((g0, g1, g2, g3)):
+        start = pl.multiple_of((my_expert ^ k) * feats, LANES)
+        saved = saved_tok[:, pl.ds(start, feats)].astype(jnp.float32)
+        total = total + jnp.sum(grad[...].astype(jnp.float32) * saved, axis=1, keepdims=True)
+    first = (route[:, 0:1] == my_expert).astype(jnp.float32)
+    second = (route[:, 1:2] == my_expert).astype(jnp.float32)
+    terms[...] = as_rows(jnp.broadcast_to((first - second) * total, (tok_rows, LANES)))
+
+
+def expert_grad_kernel(
+    meta, route, p0, p1, p2, p3, place, g0, g1, g2, g3, expert_grad, columns
+):
+    my_expert = meta[2]
+    tok_rows, feats = g0.shape
+    experts = EXPERTS_ROW
+    here = slice(feats, feats + tok_rows)
+    sums = as_columns((p0[:, here] + p1[:, here]) + (p2[:, here] + p3[:, here]))
+    lanes = iota(sums.shape, 1)
+    inv_rms = lax.rsqrt(column(sums, experts) / D + NORM_EPS)
+    logits = jnp.where(lanes < experts, sums * inv_rms, 0.0)
+    first = route[:, 0:1]
+    second = route[:, 1:2]
+    logit_a = jnp.sum(jnp.where(lanes == first, logits, 0.0), axis=1, keepdims=True)
+    logit_b = jnp.sum(jnp.where(lanes == second, logits, 0.0), axis=1, keepdims=True)
+    gate_a = jax.nn.sigmoid(logit_a - logit_b)
+    gate_b = jax.nn.sigmoid(logit_b - logit_a)
+    gate = jnp.where(first == my_expert, gate_a, 0.0) + jnp.where(second == my_expert, gate_b, 0.0)
+    columns[...] = jnp.where(
+        lanes < experts, sums, jnp.where(lanes == experts, inv_rms, gate_a * gate_b)
+    )
+    for k, grad in enumerate((g0, g1, g2, g3)):
+        start = pl.multiple_of((my_expert ^ k) * feats, LANES)
+        value = (gate * grad[...].astype(jnp.float32)).astype(jnp.bfloat16)
+        expert_grad[:, pl.ds(start, feats)] = lax.dot_general(
+            place[...], value, TN, preferred_element_type=jnp.float32
+        ).astype(jnp.bfloat16)
+
+
+def router_kernel(total_tokens, route, t0, t1, t2, t3, columns, resid, dcolumns, router_part):
+    experts = EXPERTS_ROW
+    rows = (t0[...] + t1[...]) + (t2[...] + t3[...])
+    delta = column(as_columns(rows), 0)
+    cols = columns[...]
+    lanes = iota(cols.shape, 1)
+    inv_rms = column(cols, experts)
+    dlogit_a = column(cols, experts + 1) * delta
+    dlogits = jnp.where(lanes == route[:, 0:1], dlogit_a, 0.0) - jnp.where(
+        lanes == route[:, 1:2], dlogit_a, 0.0
+    )
+    along_raw = jnp.sum(jnp.where(lanes < experts, cols, 0.0) * dlogits, axis=1, keepdims=True)
+    scaled = inv_rms * dlogits
+    dcolumns[...] = jnp.where(lanes == experts, along_raw * inv_rms * inv_rms * inv_rms / D, scaled)
+    router_part[...] = (
+        jnp.dot(
+            as_rows(scaled),
+            resid[...].astype(jnp.float32),
+            precision=lax.Precision.HIGHEST,
+            preferred_element_type=jnp.float32,
+        )
+        / total_tokens
+    )
+
+
+def resid_grad_kernel(
+    meta, dcolumns, p0, p1, p2, p3, g0, g1, g2, g3, r0, r1, r2, r3, resid_grad
+):
+    my_expert = meta[2]
+    tok_rows, feats = g0.shape
+    cols = dcolumns[...]
+    weights = [column(cols, e) for e in range(EXPERTS_ROW)]
+    along = column(cols, EXPERTS_ROW)
+    groups = ((p0, g0, r0), (p1, g1, r1), (p2, g2, r2), (p3, g3, r3))
+    for k, (pack, grad, resid) in enumerate(groups):
+        start = pl.multiple_of((my_expert ^ k) * feats, LANES)
+        back = weights[0] * pack[0:1, 0:feats]
+        for e in range(1, EXPERTS_ROW):
+            back = back + weights[e] * pack[e : e + 1, 0:feats]
+        resid_grad[:, pl.ds(start, feats)] = (
+            grad[...].astype(jnp.float32) + back - along * resid[...].astype(jnp.float32)
+        ).astype(jnp.bfloat16)
+
+
+def stacked(matrix, heads):
+    return jnp.concatenate(
+        [matrix[:, h * HEAD_DIM : (h + 1) * HEAD_DIM] for h in range(heads)], axis=0
+    )
+
+
+def forward_kernel(meta, query, v0, v1, v2, v3, probs, attn_out):
+    my_seq = meta[1]
+    tok_rows = query.shape[0]
+    kv_count = v0.shape[1] // (2 * HEAD_DIM)
+    group = query.shape[1] // (kv_count * HEAD_DIM)
+    rows = group * tok_rows
+    position = lax.rem(iota((rows, tok_rows), 0), tok_rows)
+    key_at = iota((rows, tok_rows), 1)
+    allowed = jnp.concatenate(
+        [key_at + ((my_seq ^ k) - my_seq) * tok_rows <= position for k in range(4)], axis=1
+    )
+    for kv in range(kv_count):
+        heads = stacked(query[:, kv * group * HEAD_DIM : (kv + 1) * group * HEAD_DIM], group)
+        key_cols = slice(kv * HEAD_DIM, (kv + 1) * HEAD_DIM)
+        value_cols = slice((kv_count + kv) * HEAD_DIM, (kv_count + kv + 1) * HEAD_DIM)
+        keys = jnp.concatenate([v[:, key_cols] for v in (v0, v1, v2, v3)], axis=0)
+        values = jnp.concatenate([v[:, value_cols] for v in (v0, v1, v2, v3)], axis=0)
+        scores = lax.dot_general(heads, keys, NT, preferred_element_type=jnp.float32) * (
+            HEAD_DIM ** (-0.5)
+        )
+        row_max = jnp.max(jnp.where(allowed, scores, NEG_FILL), axis=1, keepdims=True)
+        weights = jnp.exp(jnp.where(allowed, scores - row_max, NEG_FILL))
+        row_total = jnp.sum(weights, axis=1, keepdims=True)
+        mixed = (
+            jnp.dot(weights.astype(jnp.bfloat16), values, preferred_element_type=jnp.float32)
+            / row_total
+        )
+        log_norm = row_max + jnp.log(row_total)
+        probs[kv] = jnp.exp(jnp.where(allowed, scores - log_norm, NEG_FILL))
+        for h in range(group):
+            at = (kv * group + h) * HEAD_DIM
+            attn_out[:, at : at + HEAD_DIM] = mixed[h * tok_rows : (h + 1) * tok_rows]
+
+
+def backward_kernel(
+    meta, resid_grad, w0, w1, w2, w3, query, probs, attn_out, *rest
+):
+    key_refs, value_refs, (dquery, d0, d1, d2, d3, total) = rest[0:4], rest[4:8], rest[8:]
+    step = pl.program_id(0)
+    my_seq = meta[1]
+    tok_rows = query.shape[0]
+    group = query.shape[1] // HEAD_DIM
+    width = w0.shape[1]
+    feats = width * pl.num_programs(0)
+
+    @pl.when(step == 0)
+    def _():
+        total[...] = jnp.zeros_like(total)
+
+    for k, weight in enumerate((w0, w1, w2, w3)):
+        start = pl.multiple_of((my_seq ^ k) * feats + step * width, LANES)
+        total[...] += lax.dot_general(
+            resid_grad[:, pl.ds(start, width)], weight[...], NT, preferred_element_type=jnp.float32
+        )
+
+    @pl.when(step == pl.num_programs(0) - 1)
+    def _():
+        score_scale = HEAD_DIM ** (-0.5)
+        attn_grad = total[...].astype(jnp.bfloat16)
+        grads = stacked(attn_grad, group)
+        heads = stacked(query[...], group)
+        mixed = stacked(attn_out[...], group)
+        keys = jnp.concatenate([ref[...] for ref in key_refs], axis=0)
+        values = jnp.concatenate([ref[...] for ref in value_refs], axis=0)
+        delta = jnp.sum(grads.astype(jnp.float32) * mixed, axis=1, keepdims=True)
+        dprobs = lax.dot_general(grads, values, NT, preferred_element_type=jnp.float32)
+        chances = probs[0]
+        dscores = (chances * (dprobs - delta)).astype(jnp.bfloat16)
+        dheads = (
+            jnp.dot(dscores, keys, preferred_element_type=jnp.float32) * score_scale
+        ).astype(jnp.bfloat16)
+        for h in range(group):
+            dquery[:, h * HEAD_DIM : (h + 1) * HEAD_DIM] = dheads[h * tok_rows : (h + 1) * tok_rows]
+        dkeys = lax.dot_general(dscores, heads, TN, preferred_element_type=jnp.float32) * score_scale
+        dvalues = lax.dot_general(
+            chances.astype(jnp.bfloat16), grads, TN, preferred_element_type=jnp.float32
+        )
+        for k, out in enumerate((d0, d1, d2, d3)):
+            here = slice(k * tok_rows, (k + 1) * tok_rows)
+            out[:, 0:HEAD_DIM] = dkeys[here].astype(out.dtype)
+            out[:, HEAD_DIM : 2 * HEAD_DIM] = dvalues[here].astype(out.dtype)
+
+
+def finish_kernel(meta, a0, a1, a2, a3, b0, b1, b2, b3, qa, qb, key_grad, value_grad, query_grad):
+    my_core = meta[0]
+    wide = qa.shape[1]
+    for half, parts, dquery in ((0, (a0, a1, a2, a3), qa), (1, (b0, b1, b2, b3), qb)):
+        total = parts[0][...]
+        for part in parts[1:]:
+            total = total + part[...].astype(jnp.float32)
+        total = total.astype(jnp.bfloat16)
+        head = my_core ^ half
+        start = pl.multiple_of(head * HEAD_DIM, LANES)
+        key_grad[:, pl.ds(start, HEAD_DIM)] = total[:, 0:HEAD_DIM]
+        value_grad[:, pl.ds(start, HEAD_DIM)] = total[:, HEAD_DIM : 2 * HEAD_DIM]
+        query_grad[:, pl.ds(pl.multiple_of(head * wide, LANES), wide)] = dquery[...]
+
+
+EXPERTS_ROW = 4
+
+
+def call(kernel, meta, args, outs):
+    shapes = [jax.ShapeDtypeStruct(s, t) for s, t in outs]
+    return pl.pallas_call(
+        kernel,
+        out_shape=shapes,
+        grid_spec=pltpu.PrefetchScalarGridSpec(
+            num_scalar_prefetch=1,
+            grid=(1,),
+            in_specs=[whole(a.shape) for a in args],
+            out_specs=[whole(s.shape) for s in shapes],
+        ),
+        compiler_params=params(),
+    )(meta, *args)
+
+
+def local_fast(
+    query_in, key_in, value_in, resid_in, out_grad, o_weight, router_weight, route_ids, expert_out
+):
+    query = query_in[0]
+    resid = resid_in[0]
+    grad = out_grad[0]
+    route = route_ids[0]
+    saved = expert_out[0]
+    tok_rows, feats = resid.shape
+    capacity, width = saved.shape
+    seq_n, expert_n, dp_n = lax.axis_size("seq"), lax.axis_size("expert"), lax.axis_size("dp")
+    core = lax.axis_index("dp")
+    meta = jnp.stack([core, lax.axis_index("seq"), lax.axis_index("expert")]).astype(jnp.int32)
+    f32, bf16 = jnp.float32, jnp.bfloat16
+
+    def over_expert(array):
+        return [array] + [partner(array, "expert", expert_n, k) for k in range(1, expert_n)]
+
+    def over_seq(array):
+        return [partner(array, "seq", seq_n, k) for k in range(1, seq_n)]
+
+    half_rows = o_weight.shape[0] // dp_n
+    mine = lax.dynamic_slice_in_dim(o_weight, core * half_rows, half_rows, axis=0)
+    weight_mine = over_seq(mine)
+    weight_other = [partner(w, "dp", dp_n, 1) for w in weight_mine]
+
+    grads = over_expert(grad)
+    resids = over_expert(resid)
+    pair = jnp.concatenate([key_in[0], value_in[0]], axis=1)
+    pairs = [pair] + over_seq(pair)
+
+    router_pad = jnp.pad(router_weight, ((0, 0), (0, LANES - router_weight.shape[1])))
+    pack, place, saved_tok = call(
+        prepare_kernel,
+        meta,
+        (route, router_pad, resid, saved),
+        (
+            ((8, feats + tok_rows), f32),
+            ((tok_rows, capacity), bf16),
+            ((tok_rows, width), bf16),
+        ),
+    )
+    packs = over_expert(pack)
+    (terms,) = call(
+        gate_grad_kernel, meta, (route, saved_tok, *grads), (((8, tok_rows), f32),)
+    )
+    all_terms = over_expert(terms)
+    expert_grad, columns = call(
+        expert_grad_kernel,
+        meta,
+        (route, *packs, place, *grads),
+        (((capacity, width), bf16), ((tok_rows, LANES), f32)),
+    )
+    total_tokens = dp_n * seq_n * tok_rows
+    dcolumns, router_part = call(
+        lambda meta, *refs: router_kernel(total_tokens, *refs),
+        meta,
+        (route, *all_terms, columns, resid),
+        (((tok_rows, LANES), f32), ((8, feats), f32)),
+    )
+    router_pair = router_part + partner(router_part, "dp", dp_n, 1)
+    r1, r2, r3 = over_seq(router_pair)
+    router_sum = (router_pair + r1) + (r2 + r3)
+    router_grad = router_sum[0 : router_weight.shape[1]].T
+
+    kv_width = key_in.shape[2]
+    kv_count = kv_width // HEAD_DIM
+    group = query.shape[1] // kv_width
+    probs, attn_out = call(
+        forward_kernel,
+        meta,
+        (query, *pairs),
+        (
+            ((kv_count, group * tok_rows, seq_n * tok_rows), f32),
+            (query.shape, f32),
+        ),
+    )
+    (resid_grad,) = call(
+        resid_grad_kernel,
+        meta,
+        (dcolumns, *packs, *grads, *resids),
+        (((tok_rows, width), bf16),),
+    )
+
+    def backward(half, weights):
+        steps = 4
+        wide = group * HEAD_DIM
+        head = lambda i, m: m[0] ^ half
+        in_specs = [
+            whole(resid_grad.shape),
+            pl.BlockSpec((half_rows, feats // steps), lambda i, m: (head(i, m), i)),
+        ]
+        in_specs += [pl.BlockSpec((half_rows, feats // steps), lambda i, m: (0, i))] * 3
+        in_specs += [
+            pl.BlockSpec((tok_rows, wide), lambda i, m: (0, head(i, m))),
+            pl.BlockSpec((1, group * tok_rows, seq_n * tok_rows), lambda i, m: (head(i, m), 0, 0)),
+            pl.BlockSpec((tok_rows, wide), lambda i, m: (0, head(i, m))),
+        ]
+        in_specs += [pl.BlockSpec((tok_rows, HEAD_DIM), lambda i, m: (0, head(i, m)))] * 4
+        in_specs += [
+            pl.BlockSpec((tok_rows, HEAD_DIM), lambda i, m: (0, kv_count + head(i, m)))
+        ] * 4
+        term = (tok_rows, 2 * HEAD_DIM)
+        shapes = [jax.ShapeDtypeStruct((tok_rows, wide), bf16), jax.ShapeDtypeStruct(term, f32)]
+        shapes += [jax.ShapeDtypeStruct(term, bf16)] * 3
+        return pl.pallas_call(
+            backward_kernel,
+            out_shape=shapes,
+            grid_spec=pltpu.PrefetchScalarGridSpec(
+                num_scalar_prefetch=1,
+                grid=(steps,),
+                in_specs=in_specs,
+                out_specs=[whole(s.shape) for s in shapes],
+                scratch_shapes=[pltpu.VMEM((tok_rows, wide), f32)],
+            ),
+            compiler_params=params(),
+        )(meta, resid_grad, o_weight, *weights, query, probs, attn_out, *pairs, *pairs)
+
+    def send_back(terms):
+        return [
+            lax.ppermute(
+                terms[k - 1], "seq", [(i, i ^ k) for i in range(seq_n) if i > i ^ k]
+            )
+            for k in range(1, seq_n)
+        ]
+
+    dquery_a, own_a, *terms_a = backward(0, weight_mine)
+    back_a = send_back(terms_a)
+    dquery_b, own_b, *terms_b = backward(1, weight_other)
+    back_b = send_back(terms_b)
+    key_grad, value_grad, query_grad = call(
+        finish_kernel,
+        meta,
+        (own_a, *back_a, own_b, *back_b, dquery_a, dquery_b),
+        (
+            ((tok_rows, kv_width), bf16),
+            ((tok_rows, kv_width), bf16),
+            ((tok_rows, query.shape[1]), bf16),
+        ),
+    )
+    return (query_grad[None], key_grad[None], value_grad[None], router_grad, expert_grad[None])
+
+
 def solution(mesh):
     placed = (
         P("dp", "seq", "expert"),
@@ -262,8 +679,9 @@
         P("dp", "seq", None),
         P("dp", ("seq", "expert"), None),
     )
+    four = mesh.shape["dp"] == 2 and mesh.shape["seq"] == 4 and mesh.shape["expert"] == 4
     return jax.shard_map(
-        local,
+        local_fast if four else local,
         mesh=mesh,
         in_specs=placed,
         out_specs=(

time: 259 us -> 174 us (0.67)
  blocking collectives: 80.2 us -> 0 us
  starting transfers between devices: 5.44 us -> 47.4 us
  Pallas kernels: 0 us -> 40.8 us
  waiting for transfers between devices: 107 us -> 75 us
  matrix products: 18.5 us -> 0 us
  local copies, waits for them, and re-layouts: 21.2 us -> 5.54 us
  between operations: 14 us -> 1.02 us
  other arithmetic: 10.7 us -> 1.25 us
    all_gather x2 -> x0, waiting for transfers between devices: 93.7 us -> none  [the longest x1 89 us: local(): lax.all_gather(o_weight, 'seq', axis=1, tiled=True)]
    ppermute x0 -> x31, waiting for transfers between devices: none -> 75 us  [the longest x25 67.1 us: partner(): return lax.ppermute(array, axis, [(i, i ^ distance) for i in range(count)])]
    psum x2 -> x0, blocking collectives: 52.6 us -> none  [the longest x1 27 us: local(): router_grad = lax.psum(router_part, ('dp', 'seq'))]
    ppermute x0 -> x31, starting transfers between devices: none -> 47.4 us  [the longest x25 39.5 us: partner(): return lax.ppermute(array, axis, [(i, i ^ distance) for i in range(count)])]
    pallas_call x0 -> x9, Pallas kernels: none -> 40.8 us  [the longest x7 26 us: call(): pl.pallas_call(kernel, out_shape=shapes, grid_spec=pltpu.PrefetchScalarGr...]
    all_gather x3 -> x0, blocking collectives: 27.6 us -> none  [the longest x1 9.6 us: local(): lax.all_gather(value_loc, 'seq', axis=0, tiled=True)]
    dot_general x12 -> x0, matrix products: 18.5 us -> none  [the longest x1 7.33 us: local(): lax.dot_general(resid_whole, lax.all_gather(o_weight, 'seq', axis=1, tile...]
    reduce_scatter x2 -> x0, waiting for transfers between devices: 12.4 us -> none  [the longest x1 12.4 us: local(): lax.psum_scatter(back_out[2], 'seq', scatter_dimension=0, tiled=True)]
  transfers between devices with their start and end apart: 5 -> 31, of which waited for: 3 -> 14; matrix products, arithmetic and copies ran while one was open for 7% -> 2% of each run, Pallas kernels for 0% -> 22%
where the time goes in v1:
time: 174 us; the launch traced here: 171 us
  waiting for transfers between devices  75 us (43%)
  starting transfers between devices  47.4 us (27%)
  Pallas kernels  40.8 us (23%)
  local copies, waits for them, and re-layouts  5.54 us (3%)
    ppermute x25, waiting for transfers between devices, partner(): return lax.ppermute(array, axis, [(i, i ^ distance) for i in range(count)])  67.1 us
    ppermute x25, starting transfers between devices, partner(): return lax.ppermute(array, axis, [(i, i ^ distance) for i in range(count)])  39.5 us
    pallas_call x7, Pallas kernels, call(): pl.pallas_call(kernel, out_shape=shapes, grid_spec=pltpu.PrefetchScalarGr...  26 us
    pallas_call x2, Pallas kernels, backward(): pl.pallas_call(backward_kernel, out_shape=shapes, grid_spec=pltpu.Prefetc...  14.9 us
    ppermute x6, waiting for transfers between devices, send_back(): lax.ppermute(terms[k - 1], 'seq', [(i, i ^ k) for i in range(seq_n) if i...  7.94 us
    ppermute x6, starting transfers between devices, send_back(): lax.ppermute(terms[k - 1], 'seq', [(i, i ^ k) for i in range(seq_n) if i...  7.88 us
  transfers between devices with their start and end apart: 31, of which 14 were waited for; matrix products, arithmetic and copies ran while one was open for 2% of the time, Pallas kernels for 22%

profile of v1, /device:TPU:8, one launch (start us, length us, event | category | flops | bytes accessed | tf_op | source)
XLA Modules:
  0.0 171.1 jit_solution(8000382896521111318)
XLA Ops:
  0.7 2.4 %constant_dynamic-slice_fusion = bf16[512,1024]{1,0:T(8,128)(2,1)} fusion(bf16[1024,1024]{1,0:T(8,128)(2,1)} %w0.3, s32[]{:T(128)S(6)} %select_n.3), kind=kLoop, calls=%fused_computation.6 | loop fusion | bytes 2097156 | tf_op jit(solution)/shard_map/dynamic_slice | solution.py:549
  4.6 1.5 collective-permute-start.13
  6.6 1.6 collective-permute-start.15
  10.5 3.7 %shard_map.128 = (f32[8,1152]{1,0:T(8,128)}, bf16[128,128]{1,0:T(8,128)(2,1)}, bf16[128,4096]{1,0:T(8,128)(2,1)}) custom-call(s32[3]{0:T(128)} %pad_add_fusion.meta, s32[128,2]{1,0:T(8,128)} %bitcast.31, bf16[1024,128]{1,0:T(8,128)(2,1)} %pad.4.router_pad, bf16[128,1024]{1,0:T(8,128)(2,1)} %bitcast.19, bf16[128,4096]{1,0:T(8,128)(2,1)} %bitcast.35), custom_call_target="tpu_custom_call" | custom-call | tf_op jit(solution)/shard_map/pallas_call | solution.py:514
  14.7 14.8 %collective-permute-done.12.w1 = bf16[512,1024]{1,0:T(8,128)(2,1)} collective-permute-done((bf16[512,1024]{1,0:T(8,128)(2,1)}, bf16[512,1024]{1,0:T(8,128)(2,1)}, u32[]{:S(2)}, u32[]{:S(2)}) %collective-permute-start.12) | collective-permute-done | bytes 1048608 | tf_op jit(solution)/shard_map/ppermute | solution.py:267
  29.4 21.5 %collective-permute-done.13.w2 = bf16[512,1024]{1,0:T(8,128)(2,1)S(1)} collective-permute-done((bf16[512,1024]{1,0:T(8,128)(2,1)}, bf16[512,1024]{1,0:T(8,128)(2,1)S(1)}, u32[]{:S(2)}, u32[]{:S(2)}) %collective-permute-start.13) | collective-permute-done | bytes 1048608 | tf_op jit(solution)/shard_map/ppermute | solution.py:267
  51.0 2.7 %collective-permute-start.7 = (f32[8,1152]{1,0:T(8,128)}, f32[8,1152]{1,0:T(8,128)S(1)}, u32[]{:S(2)}, u32[]{:S(2)}) collective-permute-start(f32[8,1152]{1,0:T(8,128)} %get-tuple-element.28.p0), channel_id=1, source_target_pairs={{0,2},{1,3},{2,0},{3,1},{4,6},{5,7},{6,4},{7,5},{8,10},{9,11},{10,... | collective-permute-start | bytes 110600 | tf_op jit(solution)/shard_map/ppermute | solution.py:267
  53.8 2.3 %collective-permute-done.7.p2 = f32[8,1152]{1,0:T(8,128)S(1)} collective-permute-done((f32[8,1152]{1,0:T(8,128)}, f32[8,1152]{1,0:T(8,128)S(1)}, u32[]{:S(2)}, u32[]{:S(2)}) %collective-permute-start.7) | collective-permute-done | bytes 36896 | tf_op jit(solution)/shard_map/ppermute | solution.py:267
  56.1 1.6 collective-permute-start.8
  57.7 2.6 %collective-permute-done.8.p3 = f32[8,1152]{1,0:T(8,128)S(1)} collective-permute-done((f32[8,1152]{1,0:T(8,128)}, f32[8,1152]{1,0:T(8,128)S(1)}, u32[]{:S(2)}, u32[]{:S(2)}) %collective-permute-start.8) | collective-permute-done | bytes 36896 | tf_op jit(solution)/shard_map/ppermute | solution.py:267
  60.3 2.6 %collective-permute-start = (bf16[128,1024]{1,0:T(8,128)(2,1)S(1)}, bf16[128,1024]{1,0:T(8,128)(2,1)S(1)}, u32[]{:S(2)}, u32[]{:S(2)}) collective-permute-start(bf16[128,1024]{1,0:T(8,128)(2,1)S(1)} %bitcast.28), channel_id=1, source_target_pairs={{0,1},{1,0},{2,3},{3,2},{4,5},{5,4},{6,7},{7,6},{8,9},{9,8},{10,11... | collective-permute-start | bytes 786440 | tf_op jit(solution)/shard_map/ppermute | solution.py:267
  62.8 2.5 %collective-permute-start.16 = (bf16[128,512]{1,0:T(8,128)(2,1)S(1)}, bf16[128,512]{1,0:T(8,128)(2,1)S(1)}, u32[]{:S(2)}, u32[]{:S(2)}) collective-permute-start(bf16[128,512]{1,0:T(8,128)(2,1)S(1)} %pad_maximum_fusion.v0.rest_0_.rest_4_), channel_id=1, source_target_pairs={{0,8},{4,12},{8,0},{12,4},{1,9},{5,13},{9,1},{13,5},{2,10},{6,14},... | collective-permute-start | bytes 393224 | tf_op jit(solution)/shard_map/ppermute | solution.py:267
  65.3 2.9 %collective-permute-done.16.v2.rest_2_.rest_6_ = bf16[128,512]{1,0:T(8,128)(2,1)S(1)} collective-permute-done((bf16[128,512]{1,0:T(8,128)(2,1)S(1)}, bf16[128,512]{1,0:T(8,128)(2,1)S(1)}, u32[]{:S(2)}, u32[]{:S(2)}) %collective-permute-start.16) | collective-permute-done | bytes 131104 | tf_op jit(solution)/shard_map/ppermute | solution.py:267
  68.3 2.6 %collective-permute-start.1 = (bf16[128,1024]{1,0:T(8,128)(2,1)S(1)}, bf16[128,1024]{1,0:T(8,128)(2,1)S(1)}, u32[]{:S(2)}, u32[]{:S(2)}) collective-permute-start(bf16[128,1024]{1,0:T(8,128)(2,1)S(1)} %bitcast.29), channel_id=1, source_target_pairs={{0,2},{1,3},{2,0},{3,1},{4,6},{5,7},{6,4},{7,5},{8,10},{9,11},{10,... | collective-permute-start | bytes 786440 | tf_op jit(solution)/shard_map/ppermute | solution.py:267
  71.5 15.7 %collective-permute-done.1.g2 = bf16[128,1024]{1,0:T(8,128)(2,1)S(1)} collective-permute-done((bf16[128,1024]{1,0:T(8,128)(2,1)S(1)}, bf16[128,1024]{1,0:T(8,128)(2,1)S(1)}, u32[]{:S(2)}, u32[]{:S(2)}) %collective-permute-start.1) | collective-permute-done | bytes 262176 | tf_op jit(solution)/shard_map/ppermute | solution.py:267
  87.2 1.8 %collective-permute-start.9 = (bf16[128,1024]{1,0:T(8,128)(2,1)S(1)}, bf16[128,1024]{1,0:T(8,128)(2,1)S(1)}, u32[]{:S(2)}, u32[]{:S(2)}) collective-permute-start(bf16[128,1024]{1,0:T(8,128)(2,1)S(1)} %bitcast.22), channel_id=1, source_target_pairs={{0,1},{1,0},{2,3},{3,2},{4,5},{5,4},{6,7},{7,6},{8,9},{9,8},{10,11... | collective-permute-start | bytes 786440 | tf_op jit(solution)/shard_map/ppermute | solution.py:267
  89.0 3.5 %collective-permute-done.2.g3 = bf16[128,1024]{1,0:T(8,128)(2,1)S(1)} collective-permute-done((bf16[128,1024]{1,0:T(8,128)(2,1)S(1)}, bf16[128,1024]{1,0:T(8,128)(2,1)S(1)}, u32[]{:S(2)}, u32[]{:S(2)}) %collective-permute-start.2) | collective-permute-done | bytes 262176 | tf_op jit(solution)/shard_map/ppermute | solution.py:267
  93.3 3.3 %shard_map.129.refs_1_ = f32[8,128]{1,0:T(8,128)} custom-call(s32[3]{0:T(128)} %pad_add_fusion.meta, s32[128,2]{1,0:T(8,128)} %bitcast.32, bf16[128,4096]{1,0:T(8,128)(2,1)} %get-tuple-element.27.saved_tok, bf16[128,1024]{1,0:T(8,128)(2,1)} %bitcast.25, bf16[128,1024]{1,0:T(8,128)(2,1)} %copy-done.6, bf16[128,1024]{1,0:T(8,128)(2,1)} %copy-done.7, ...), custom_call_target="tpu_custom_call" | custom-call | tf_op jit(solution)/shard_map/pallas_call | solution.py:514
  96.6 1.8 %collective-permute-done.17.v3.rest_3_.rest_7_ = bf16[128,512]{1,0:T(8,128)(2,1)S(1)} collective-permute-done((bf16[128,512]{1,0:T(8,128)(2,1)S(1)}, bf16[128,512]{1,0:T(8,128)(2,1)S(1)}, u32[]{:S(2)}, u32[]{:S(2)}) %collective-permute-start.17) | collective-permute-done | bytes 131104 | tf_op jit(solution)/shard_map/ppermute | solution.py:267
  98.4 2.7 %collective-permute-start.4 = (f32[8,128]{1,0:T(8,128)}, f32[8,128]{1,0:T(8,128)S(1)}, u32[]{:S(2)}, u32[]{:S(2)}) collective-permute-start(f32[8,128]{1,0:T(8,128)} %shard_map.129.refs_1_), channel_id=1, source_target_pairs={{0,2},{1,3},{2,0},{3,1},{4,6},{5,7},{6,4},{7,5},{8,10},{9,11},{10,... | collective-permute-start | bytes 12296 | tf_op jit(solution)/shard_map/ppermute | solution.py:267
  103.5 10.6 %collective-permute-start.10 = (bf16[128,1024]{1,0:T(8,128)(2,1)S(1)}, bf16[128,1024]{1,0:T(8,128)(2,1)S(1)}, u32[]{:S(2)}, u32[]{:S(2)}) collective-permute-start(bf16[128,1024]{1,0:T(8,128)(2,1)S(1)} %bitcast.23), channel_id=1, source_target_pairs={{0,2},{1,3},{2,0},{3,1},{4,6},{5,7},{6,4},{7,5},{8,10},{9,11},{10,... | collective-permute-start | bytes 786440 | tf_op jit(solution)/shard_map/ppermute | solution.py:267
  114.1 3.8 %shard_map.130 = (bf16[128,4096]{1,0:T(8,128)(2,1)}, f32[128,128]{1,0:T(8,128)}) custom-call(s32[3]{0:T(128)} %pad_add_fusion.meta, s32[128,2]{1,0:T(8,128)} %bitcast.33, f32[8,1152]{1,0:T(8,128)} %get-tuple-element.28.p0, f32[8,1152]{1,0:T(8,128)} %copy-done.17, f32[8,1152]{1,0:T(8,128)} %copy-done.18, f32[8,1152]{1,0:T(8,128)} %copy-done.19, ...), custom_call_target="tpu_custom_call" | custom-call | tf_op jit(solution)/shard_map/pallas_call | solution.py:514
  117.9 3.0 %shard_map.131 = (f32[128,128]{1,0:T(8,128)}, f32[8,1024]{1,0:T(8,128)}) custom-call(s32[3]{0:T(128)} %pad_add_fusion.meta, s32[128,2]{1,0:T(8,128)} %bitcast.34, f32[8,128]{1,0:T(8,128)} %shard_map.129.refs_1_, f32[8,128]{1,0:T(8,128)} %copy-done.30, f32[8,128]{1,0:T(8,128)} %copy-done.31, f32[8,128]{1,0:T(8,128)} %copy-done.32, ...), custom_call_target="tpu_custom_call" | custom-call | tf_op jit(solution)/shard_map/pallas_call | solution.py:514
  121.8 5.1 %shard_map.133 = (f32[2,512,512]{2,1,0:T(8,128)}, f32[128,1024]{1,0:T(8,128)}) custom-call(s32[3]{0:T(128)} %pad_add_fusion.meta, bf16[128,1024]{1,0:T(8,128)(2,1)} %bitcast.16, bf16[128,512]{1,0:T(8,128)(2,1)} %copy-done, bf16[128,512]{1,0:T(8,128)(2,1)} %copy-done.1, bf16[128,512]{1,0:T(8,128)(2,1)} %copy-done.2, bf16[128,512]{1,0:T(8,128)(2,1)} %copy-done.3), custom_call_target="tpu_custom_call" | custom-call | tf_op jit(solution)/shard_map/pallas_call | solution.py:514
  127.6 4.4 %shard_map.132.resid_grad = bf16[128,4096]{1,0:T(8,128)(2,1)} custom-call(s32[3]{0:T(128)} %pad_add_fusion.meta, f32[128,128]{1,0:T(8,128)} %get-tuple-element.31.dcolumns, f32[8,1152]{1,0:T(8,128)} %get-tuple-element.28.p0, f32[8,1152]{1,0:T(8,128)} %copy-done.17, f32[8,1152]{1,0:T(8,128)} %copy-done.18, f32[8,1152]{1,0:T(8,128)} %copy-done.19, ...), custom_call_target="tpu_custom_call" | custom-call | tf_op jit(solution)/shard_map/pallas_call | solution.py:514
  132.0 7.4 %shard_map.134 = (bf16[128,512]{1,0:T(8,128)(2,1)}, f32[128,256]{1,0:T(8,128)}, bf16[128,256]{1,0:T(8,128)(2,1)}, bf16[128,256]{1,0:T(8,128)(2,1)}, bf16[128,256]{1,0:T(8,128)(2,1)}) custom-call(s32[3]{0:T(128)} %pad_add_fusion.meta, bf16[128,4096]{1,0:T(8,128)(2,1)} %shard_map.132.resid_grad, bf16[1024,1024]{1,0:T(8,128)(2,1)} %w0.3, ...), custom_call_target="tpu_custom_call" | custom-call | tf_op jit(solution)/shard_map/pallas_call | solution.py:632
  140.7 2.7 %collective-permute-start.30 = (f32[8,1024]{1,0:T(8,128)S(1)}, f32[8,1024]{1,0:T(8,128)S(1)}, u32[]{:S(2)}, u32[]{:S(2)}) collective-permute-start(f32[8,1024]{1,0:T(8,128)S(1)} %add.18), channel_id=1, source_target_pairs={{0,12},{4,8},{8,4},{12,0},{1,13},{5,9},{9,5},{13,1},{2,14},{6,10},... | collective-permute-start | bytes 98312 | tf_op jit(solution)/shard_map/ppermute | solution.py:267
  146.4 7.5 %shard_map.135 = (bf16[128,512]{1,0:T(8,128)(2,1)}, f32[128,256]{1,0:T(8,128)}, bf16[128,256]{1,0:T(8,128)(2,1)}, bf16[128,256]{1,0:T(8,128)(2,1)}, bf16[128,256]{1,0:T(8,128)(2,1)}) custom-call(s32[3]{0:T(128)} %pad_add_fusion.meta, bf16[128,4096]{1,0:T(8,128)(2,1)} %shard_map.132.resid_grad, bf16[1024,1024]{1,0:T(8,128)(2,1)} %w0.3, ...), custom_call_target="tpu_custom_call" | custom-call | tf_op jit(solution)/shard_map/pallas_call | solution.py:632
  159.8 1.7 %collective-permute-done.20.a3 = bf16[128,256]{1,0:T(8,128)(2,1)S(1)} collective-permute-done((bf16[128,256]{1,0:T(8,128)(2,1)S(1)}, bf16[128,256]{1,0:T(8,128)(2,1)S(1)}, u32[]{:S(2)}, u32[]{:S(2)}) %collective-permute-start.20) | collective-permute-done | bytes 65568 | tf_op jit(solution)/shard_map/ppermute | solution.py:647
  161.6 2.7 %collective-permute-done.25.b2 = bf16[128,256]{1,0:T(8,128)(2,1)S(1)} collective-permute-done((bf16[128,256]{1,0:T(8,128)(2,1)}, bf16[128,256]{1,0:T(8,128)(2,1)S(1)}, u32[]{:S(2)}, u32[]{:S(2)}) %collective-permute-start.25) | collective-permute-done | bytes 65568 | tf_op jit(solution)/shard_map/ppermute | solution.py:647
  164.3 3.4 %collective-permute-done.26.b3 = bf16[128,256]{1,0:T(8,128)(2,1)S(1)} collective-permute-done((bf16[128,256]{1,0:T(8,128)(2,1)}, bf16[128,256]{1,0:T(8,128)(2,1)S(1)}, u32[]{:S(2)}, u32[]{:S(2)}) %collective-permute-start.26) | collective-permute-done | bytes 65568 | tf_op jit(solution)/shard_map/ppermute | solution.py:647
  168.3 2.7 %shard_map.136 = (bf16[128,256]{1,0:T(8,128)(2,1)}, bf16[128,256]{1,0:T(8,128)(2,1)}, bf16[128,1024]{1,0:T(8,128)(2,1)}) custom-call(s32[3]{0:T(128)} %pad_add_fusion.meta, f32[128,256]{1,0:T(8,128)} %get-tuple-element.34.a0, bf16[128,256]{1,0:T(8,128)(2,1)} %copy-done.20, bf16[128,256]{1,0:T(8,128)(2,1)} %copy-done.21, bf16[128,256]{1,0:T(8,128)(2,1)} %copy-done.22, ...), custom_call_target="tpu_custom_call" | custom-call | tf_op jit(solution)/shard_map/pallas_call | solution.py:514
  (117 shorter events, 21.2 us)
Async XLA Ops:
  3.1 26.4 %collective-permute-start.12 = (bf16[512,1024]{1,0:T(8,128)(2,1)}, bf16[512,1024]{1,0:T(8,128)(2,1)}, u32[]{:S(2)}, u32[]{:S(2)}) collective-permute-start(bf16[512,1024]{1,0:T(8,128)(2,1)} %constant_dynamic-slice_fusion), channel_id=1, source_target_pairs={{0,4},{4,0},{8,12},{12,8},{1,5},{5,1},{9,13},{13,9},{2,6},{6,2},{1... | collective-permute-start | bytes 3145736 | tf_op jit(solution)/shard_map/ppermute | solution.py:267
  4.6 46.4 %collective-permute-start.13 = (bf16[512,1024]{1,0:T(8,128)(2,1)}, bf16[512,1024]{1,0:T(8,128)(2,1)S(1)}, u32[]{:S(2)}, u32[]{:S(2)}) collective-permute-start(bf16[512,1024]{1,0:T(8,128)(2,1)} %constant_dynamic-slice_fusion), channel_id=1, source_target_pairs={{0,8},{4,12},{8,0},{12,4},{1,9},{5,13},{9,1},{13,5},{2,10},{6,14},... | collective-permute-start | bytes 3145736 | tf_op jit(solution)/shard_map/ppermute | solution.py:267
  6.1 47.5 %collective-permute-start.14 = (bf16[512,1024]{1,0:T(8,128)(2,1)}, bf16[512,1024]{1,0:T(8,128)(2,1)S(1)}, u32[]{:S(2)}, u32[]{:S(2)}) collective-permute-start(bf16[512,1024]{1,0:T(8,128)(2,1)} %constant_dynamic-slice_fusion), channel_id=1, source_target_pairs={{0,12},{4,8},{8,4},{12,0},{1,13},{5,9},{9,5},{13,1},{2,14},{6,10},... | collective-permute-start | bytes 3145736 | tf_op jit(solution)/shard_map/ppermute | solution.py:267
  6.6 90.0 %copy-start = (bf16[128,512]{1,0:T(8,128)(2,1)}, bf16[128,512]{1,0:T(8,128)(2,1)S(1)}, u32[]{:S(2)}) copy-start(bf16[128,512]{1,0:T(8,128)(2,1)S(1)} %pad_maximum_fusion.v0.rest_0_.rest_4_) | copy-start | bytes 393220
  6.6 56.2 %collective-permute-start.15 = (bf16[128,512]{1,0:T(8,128)(2,1)S(1)}, bf16[128,512]{1,0:T(8,128)(2,1)S(1)}, u32[]{:S(2)}, u32[]{:S(2)}) collective-permute-start(bf16[128,512]{1,0:T(8,128)(2,1)S(1)} %pad_maximum_fusion.v0.rest_0_.rest_4_), channel_id=1, source_target_pairs={{0,4},{4,0},{8,12},{12,8},{1,5},{5,1},{9,13},{13,9},{2,6},{6,2},{1... | collective-permute-start | bytes 393224 | tf_op jit(solution)/shard_map/ppermute | solution.py:267
  14.2 36.7 %collective-permute-start.6 = (f32[8,1152]{1,0:T(8,128)}, f32[8,1152]{1,0:T(8,128)S(1)}, u32[]{:S(2)}, u32[]{:S(2)}) collective-permute-start(f32[8,1152]{1,0:T(8,128)} %get-tuple-element.28.p0), channel_id=1, source_target_pairs={{0,1},{1,0},{2,3},{3,2},{4,5},{5,4},{6,7},{7,6},{8,9},{9,8},{10,11... | collective-permute-start | bytes 110600 | tf_op jit(solution)/shard_map/ppermute | solution.py:267
  29.4 114.0 %collective-permute-start.21 = (bf16[512,1024]{1,0:T(8,128)(2,1)}, bf16[512,1024]{1,0:T(8,128)(2,1)S(1)}, u32[]{:S(2)}, u32[]{:S(2)}) collective-permute-start(bf16[512,1024]{1,0:T(8,128)(2,1)} %collective-permute-done.12.w1), channel_id=1, source_target_pairs={{0,16},{16,0},{1,17},{17,1},{2,18},{18,2},{3,19},{19,3},{4,20},{20... | collective-permute-start | bytes 3145736 | tf_op jit(solution)/shard_map/ppermute | solution.py:267
  51.0 93.9 %collective-permute-start.22 = (bf16[512,1024]{1,0:T(8,128)(2,1)S(1)}, bf16[512,1024]{1,0:T(8,128)(2,1)S(1)}, u32[]{:S(2)}, u32[]{:S(2)}) collective-permute-start(bf16[512,1024]{1,0:T(8,128)(2,1)S(1)} %collective-permute-done.13.w2), channel_id=1, source_target_pairs={{0,16},{16,0},{1,17},{17,1},{2,18},{18,2},{3,19},{19,3},{4,20},{20... | collective-permute-start | bytes 3145736 | tf_op jit(solution)/shard_map/ppermute | solution.py:267
  51.0 5.1 %collective-permute-start.7 = (f32[8,1152]{1,0:T(8,128)}, f32[8,1152]{1,0:T(8,128)S(1)}, u32[]{:S(2)}, u32[]{:S(2)}) collective-permute-start(f32[8,1152]{1,0:T(8,128)} %get-tuple-element.28.p0), channel_id=1, source_target_pairs={{0,2},{1,3},{2,0},{3,1},{4,6},{5,7},{6,4},{7,5},{8,10},{9,11},{10,... | collective-permute-start | bytes 110600 | tf_op jit(solution)/shard_map/ppermute | solution.py:267
  53.6 91.3 %collective-permute-start.23 = (bf16[512,1024]{1,0:T(8,128)(2,1)S(1)}, bf16[512,1024]{1,0:T(8,128)(2,1)S(1)}, u32[]{:S(2)}, u32[]{:S(2)}) collective-permute-start(bf16[512,1024]{1,0:T(8,128)(2,1)S(1)} %collective-permute-done.14.w3), channel_id=1, source_target_pairs={{0,16},{16,0},{1,17},{17,1},{2,18},{18,2},{3,19},{19,3},{4,20},{20... | collective-permute-start | bytes 3145736 | tf_op jit(solution)/shard_map/ppermute | solution.py:267
  56.1 4.2 %collective-permute-start.8 = (f32[8,1152]{1,0:T(8,128)}, f32[8,1152]{1,0:T(8,128)S(1)}, u32[]{:S(2)}, u32[]{:S(2)}) collective-permute-start(f32[8,1152]{1,0:T(8,128)} %get-tuple-element.28.p0), channel_id=1, source_target_pairs={{0,3},{1,2},{2,1},{3,0},{4,7},{5,6},{6,5},{7,4},{8,11},{9,10},{10,... | collective-permute-start | bytes 110600 | tf_op jit(solution)/shard_map/ppermute | solution.py:267
  60.3 10.5 %collective-permute-start = (bf16[128,1024]{1,0:T(8,128)(2,1)S(1)}, bf16[128,1024]{1,0:T(8,128)(2,1)S(1)}, u32[]{:S(2)}, u32[]{:S(2)}) collective-permute-start(bf16[128,1024]{1,0:T(8,128)(2,1)S(1)} %bitcast.28), channel_id=1, source_target_pairs={{0,1},{1,0},{2,3},{3,2},{4,5},{5,4},{6,7},{7,6},{8,9},{9,8},{10,11... | collective-permute-start | bytes 786440 | tf_op jit(solution)/shard_map/ppermute | solution.py:267
  62.8 5.4 %collective-permute-start.16 = (bf16[128,512]{1,0:T(8,128)(2,1)S(1)}, bf16[128,512]{1,0:T(8,128)(2,1)S(1)}, u32[]{:S(2)}, u32[]{:S(2)}) collective-permute-start(bf16[128,512]{1,0:T(8,128)(2,1)S(1)} %pad_maximum_fusion.v0.rest_0_.rest_4_), channel_id=1, source_target_pairs={{0,8},{4,12},{8,0},{12,4},{1,9},{5,13},{9,1},{13,5},{2,10},{6,14},... | collective-permute-start | bytes 393224 | tf_op jit(solution)/shard_map/ppermute | solution.py:267
  68.3 18.9 %collective-permute-start.1 = (bf16[128,1024]{1,0:T(8,128)(2,1)S(1)}, bf16[128,1024]{1,0:T(8,128)(2,1)S(1)}, u32[]{:S(2)}, u32[]{:S(2)}) collective-permute-start(bf16[128,1024]{1,0:T(8,128)(2,1)S(1)} %bitcast.29), channel_id=1, source_target_pairs={{0,2},{1,3},{2,0},{3,1},{4,6},{5,7},{6,4},{7,5},{8,10},{9,11},{10,... | collective-permute-start | bytes 786440 | tf_op jit(solution)/shard_map/ppermute | solution.py:267
  70.8 21.7 %collective-permute-start.2 = (bf16[128,1024]{1,0:T(8,128)(2,1)S(1)}, bf16[128,1024]{1,0:T(8,128)(2,1)S(1)}, u32[]{:S(2)}, u32[]{:S(2)}) collective-permute-start(bf16[128,1024]{1,0:T(8,128)(2,1)S(1)} %bitcast.30), channel_id=1, source_target_pairs={{0,3},{1,2},{2,1},{3,0},{4,7},{5,6},{6,5},{7,4},{8,11},{9,10},{10,... | collective-permute-start | bytes 786440 | tf_op jit(solution)/shard_map/ppermute | solution.py:267
  87.2 11.2 %collective-permute-start.9 = (bf16[128,1024]{1,0:T(8,128)(2,1)S(1)}, bf16[128,1024]{1,0:T(8,128)(2,1)S(1)}, u32[]{:S(2)}, u32[]{:S(2)}) collective-permute-start(bf16[128,1024]{1,0:T(8,128)(2,1)S(1)} %bitcast.22), channel_id=1, source_target_pairs={{0,1},{1,0},{2,3},{3,2},{4,5},{5,4},{6,7},{7,6},{8,9},{9,8},{10,11... | collective-permute-start | bytes 786440 | tf_op jit(solution)/shard_map/ppermute | solution.py:267
  92.5 5.9 %collective-permute-start.17 = (bf16[128,512]{1,0:T(8,128)(2,1)S(1)}, bf16[128,512]{1,0:T(8,128)(2,1)S(1)}, u32[]{:S(2)}, u32[]{:S(2)}) collective-permute-start(bf16[128,512]{1,0:T(8,128)(2,1)S(1)} %pad_maximum_fusion.v0.rest_0_.rest_4_), channel_id=1, source_target_pairs={{0,12},{4,8},{8,4},{12,0},{1,13},{5,9},{9,5},{13,1},{2,14},{6,10},... | collective-permute-start | bytes 393224 | tf_op jit(solution)/shard_map/ppermute | solution.py:267
  98.4 3.8 %collective-permute-start.3 = (f32[8,128]{1,0:T(8,128)}, f32[8,128]{1,0:T(8,128)S(1)}, u32[]{:S(2)}, u32[]{:S(2)}) collective-permute-start(f32[8,128]{1,0:T(8,128)} %shard_map.129.refs_1_), channel_id=1, source_target_pairs={{0,1},{1,0},{2,3},{3,2},{4,5},{5,4},{6,7},{7,6},{8,9},{9,8},{10,11... | collective-permute-start | bytes 12296 | tf_op jit(solution)/shard_map/ppermute | solution.py:267
  98.4 5.1 %collective-permute-start.4 = (f32[8,128]{1,0:T(8,128)}, f32[8,128]{1,0:T(8,128)S(1)}, u32[]{:S(2)}, u32[]{:S(2)}) collective-permute-start(f32[8,128]{1,0:T(8,128)} %shard_map.129.refs_1_), channel_id=1, source_target_pairs={{0,2},{1,3},{2,0},{3,1},{4,6},{5,7},{6,4},{7,5},{8,10},{9,11},{10,... | collective-permute-start | bytes 12296 | tf_op jit(solution)/shard_map/ppermute | solution.py:267
  102.2 11.9 %collective-permute-start.5 = (f32[8,128]{1,0:T(8,128)}, f32[8,128]{1,0:T(8,128)S(1)}, u32[]{:S(2)}, u32[]{:S(2)}) collective-permute-start(f32[8,128]{1,0:T(8,128)} %shard_map.129.refs_1_), channel_id=1, source_target_pairs={{0,3},{1,2},{2,1},{3,0},{4,7},{5,6},{6,5},{7,4},{8,11},{9,10},{10,... | collective-permute-start | bytes 12296 | tf_op jit(solution)/shard_map/ppermute | solution.py:267
  103.5 18.3 %collective-permute-start.10 = (bf16[128,1024]{1,0:T(8,128)(2,1)S(1)}, bf16[128,1024]{1,0:T(8,128)(2,1)S(1)}, u32[]{:S(2)}, u32[]{:S(2)}) collective-permute-start(bf16[128,1024]{1,0:T(8,128)(2,1)S(1)} %bitcast.23), channel_id=1, source_target_pairs={{0,2},{1,3},{2,0},{3,1},{4,6},{5,7},{6,4},{7,5},{8,10},{9,11},{10,... | collective-permute-start | bytes 786440 | tf_op jit(solution)/shard_map/ppermute | solution.py:267
  114.0 12.8 %collective-permute-start.11 = (bf16[128,1024]{1,0:T(8,128)(2,1)S(1)}, bf16[128,1024]{1,0:T(8,128)(2,1)S(1)}, u32[]{:S(2)}, u32[]{:S(2)}) collective-permute-start(bf16[128,1024]{1,0:T(8,128)(2,1)S(1)} %bitcast.24), channel_id=1, source_target_pairs={{0,3},{1,2},{2,1},{3,0},{4,7},{5,6},{6,5},{7,4},{8,11},{9,10},{10,... | collective-permute-start | bytes 786440 | tf_op jit(solution)/shard_map/ppermute | solution.py:267
  121.7 18.9 %collective-permute-start.27 = (f32[8,1024]{1,0:T(8,128)}, f32[8,1024]{1,0:T(8,128)S(1)}, u32[]{:S(2)}, u32[]{:S(2)}) collective-permute-start(f32[8,1024]{1,0:T(8,128)} %get-tuple-element.47), channel_id=1, source_target_pairs={{0,16},{16,0},{1,17},{17,1},{2,18},{18,2},{3,19},{19,3},{4,20},{20... | collective-permute-start | bytes 98312 | tf_op jit(solution)/shard_map/ppermute | solution.py:267
  139.4 18.4 %collective-permute-start.18 = (bf16[128,256]{1,0:T(8,128)(2,1)}, bf16[128,256]{1,0:T(8,128)(2,1)S(1)}, u32[]{:S(2)}, u32[]{:S(2)}) collective-permute-start(bf16[128,256]{1,0:T(8,128)(2,1)} %get-tuple-element.35), channel_id=1, source_target_pairs={{4,0},{12,8},{5,1},{13,9},{6,2},{14,10},{7,3},{15,11},{20,16},{28,... | collective-permute-start | bytes 196616 | tf_op jit(solution)/shard_map/ppermute | solution.py:647
  140.7 13.2 %collective-permute-start.30 = (f32[8,1024]{1,0:T(8,128)S(1)}, f32[8,1024]{1,0:T(8,128)S(1)}, u32[]{:S(2)}, u32[]{:S(2)}) collective-permute-start(f32[8,1024]{1,0:T(8,128)S(1)} %add.18), channel_id=1, source_target_pairs={{0,12},{4,8},{8,4},{12,0},{1,13},{5,9},{9,5},{13,1},{2,14},{6,10},... | collective-permute-start | bytes 98312 | tf_op jit(solution)/shard_map/ppermute | solution.py:267
  143.5 11.7 %collective-permute-start.29 = (f32[8,1024]{1,0:T(8,128)S(1)}, f32[8,1024]{1,0:T(8,128)S(1)}, u32[]{:S(2)}, u32[]{:S(2)}) collective-permute-start(f32[8,1024]{1,0:T(8,128)S(1)} %add.18), channel_id=1, source_target_pairs={{0,8},{4,12},{8,0},{12,4},{1,9},{5,13},{9,1},{13,5},{2,10},{6,14},... | collective-permute-start | bytes 98312 | tf_op jit(solution)/shard_map/ppermute | solution.py:267
  144.9 11.6 %collective-permute-start.28 = (f32[8,1024]{1,0:T(8,128)S(1)}, f32[8,1024]{1,0:T(8,128)S(1)}, u32[]{:S(2)}, u32[]{:S(2)}) collective-permute-start(f32[8,1024]{1,0:T(8,128)S(1)} %add.18), channel_id=1, source_target_pairs={{0,4},{4,0},{8,12},{12,8},{1,5},{5,1},{9,13},{13,9},{2,6},{6,2},{1... | collective-permute-start | bytes 98312 | tf_op jit(solution)/shard_map/ppermute | solution.py:267
  144.9 14.8 %collective-permute-start.19 = (bf16[128,256]{1,0:T(8,128)(2,1)}, bf16[128,256]{1,0:T(8,128)(2,1)S(1)}, u32[]{:S(2)}, u32[]{:S(2)}) collective-permute-start(bf16[128,256]{1,0:T(8,128)(2,1)} %get-tuple-element.36), channel_id=1, source_target_pairs={{8,0},{12,4},{9,1},{13,5},{10,2},{14,6},{11,3},{15,7},{24,16},{28,... | collective-permute-start | bytes 196616 | tf_op jit(solution)/shard_map/ppermute | solution.py:647
  153.9 7.6 %collective-permute-start.20 = (bf16[128,256]{1,0:T(8,128)(2,1)S(1)}, bf16[128,256]{1,0:T(8,128)(2,1)S(1)}, u32[]{:S(2)}, u32[]{:S(2)}) collective-permute-start(bf16[128,256]{1,0:T(8,128)(2,1)S(1)} %copy-done.34), channel_id=1, source_target_pairs={{8,4},{12,0},{9,5},{13,1},{10,6},{14,2},{11,7},{15,3},{24,20},{28,... | collective-permute-start | bytes 196616 | tf_op jit(solution)/shard_map/ppermute | solution.py:647
  155.2 6.4 %collective-permute-start.24 = (bf16[128,256]{1,0:T(8,128)(2,1)}, bf16[128,256]{1,0:T(8,128)(2,1)S(1)}, u32[]{:S(2)}, u32[]{:S(2)}) collective-permute-start(bf16[128,256]{1,0:T(8,128)(2,1)} %get-tuple-element.39), channel_id=1, source_target_pairs={{4,0},{12,8},{5,1},{13,9},{6,2},{14,10},{7,3},{15,11},{20,16},{28,... | collective-permute-start | bytes 196616 | tf_op jit(solution)/shard_map/ppermute | solution.py:647
  156.5 7.8 %collective-permute-start.25 = (bf16[128,256]{1,0:T(8,128)(2,1)}, bf16[128,256]{1,0:T(8,128)(2,1)S(1)}, u32[]{:S(2)}, u32[]{:S(2)}) collective-permute-start(bf16[128,256]{1,0:T(8,128)(2,1)} %get-tuple-element.40), channel_id=1, source_target_pairs={{8,0},{12,4},{9,1},{13,5},{10,2},{14,6},{11,3},{15,7},{24,16},{28,... | collective-permute-start | bytes 196616 | tf_op jit(solution)/shard_map/ppermute | solution.py:647
  157.8 9.9 %collective-permute-start.26 = (bf16[128,256]{1,0:T(8,128)(2,1)}, bf16[128,256]{1,0:T(8,128)(2,1)S(1)}, u32[]{:S(2)}, u32[]{:S(2)}) collective-permute-start(bf16[128,256]{1,0:T(8,128)(2,1)} %get-tuple-element.41), channel_id=1, source_target_pairs={{8,4},{12,0},{9,5},{13,1},{10,6},{14,2},{11,7},{15,3},{24,20},{28,... | collective-permute-start | bytes 196616 | tf_op jit(solution)/shard_map/ppermute | solution.py:647
  (34 other events, 800.7 us)

commit v2 on v1

--- a/solution.py
+++ b/solution.py
@@ -252,8 +252,7 @@
     return (query_grad[None], key_grad[None], value_grad[None], router_grad, expert_grad[None])
 
 
-ANY_VMEM = pltpu.VMEM
-VMEM_LIMIT = 56 * 1024 * 1024
+VMEM_LIMIT = 16 * 1024 * 1024
 NT = (((1,), (1,)), ((), ()))
 TN = (((0,), (0,)), ((), ()))
 LANES = 128
@@ -291,11 +290,10 @@
     )
 
 
-def prepare_kernel(meta, route, router_pad, resid, saved, pack, place, saved_tok):
+def prepare_kernel(meta, route, router_pad, resid, saved, rows, place, saved_tok):
     my_expert = meta[2]
-    tok_rows, feats = resid.shape
+    tok_rows = resid.shape[0]
     capacity = saved.shape[0]
-    experts = EXPERTS_ROW
     member = (route[:, 0:1] == my_expert) | (route[:, 1:2] == my_expert)
     earlier = (iota((tok_rows, tok_rows), 1) < iota((tok_rows, tok_rows), 0)).astype(
         jnp.float32
@@ -312,11 +310,10 @@
     raw = jnp.dot(resid[...], router_pad[...], preferred_element_type=jnp.float32)
     square = jnp.sum(resid_f32 * resid_f32, axis=1, keepdims=True)
     lanes = iota(raw.shape, 1)
-    pack[:, 0:feats] = as_rows(router_pad[...].astype(jnp.float32))
-    pack[:, feats : feats + tok_rows] = as_rows(jnp.where(lanes == experts, square, raw))
-
-
-def gate_grad_kernel(meta, route, saved_tok, g0, g1, g2, g3, terms):
+    rows[...] = as_rows(jnp.where(lanes == EXPERTS_ROW, square, raw))
+
+
+def gate_grad_kernel(meta, route, rows, saved_tok, g0, g1, g2, g3, terms):
     my_expert = meta[2]
     tok_rows, feats = g0.shape
     total = jnp.zeros((tok_rows, 1), jnp.float32)
@@ -326,20 +323,19 @@
         total = total + jnp.sum(grad[...].astype(jnp.float32) * saved, axis=1, keepdims=True)
     first = (route[:, 0:1] == my_expert).astype(jnp.float32)
     second = (route[:, 1:2] == my_expert).astype(jnp.float32)
-    terms[...] = as_rows(jnp.broadcast_to((first - second) * total, (tok_rows, LANES)))
-
-
-def expert_grad_kernel(
-    meta, route, p0, p1, p2, p3, place, g0, g1, g2, g3, expert_grad, columns
-):
+    signed = as_rows(jnp.broadcast_to((first - second) * total, (tok_rows, LANES)))
+    terms[...] = jnp.where(iota(signed.shape, 0) == EXPERTS_ROW + 1, signed, rows[...])
+
+
+def router_kernel(meta, total_tokens, route, t0, t1, t2, t3, resid, columns, router_part):
     my_expert = meta[2]
-    tok_rows, feats = g0.shape
     experts = EXPERTS_ROW
-    here = slice(feats, feats + tok_rows)
-    sums = as_columns((p0[:, here] + p1[:, here]) + (p2[:, here] + p3[:, here]))
+    sums = as_columns((t0[...] + t1[...]) + (t2[...] + t3[...]))
     lanes = iota(sums.shape, 1)
     inv_rms = lax.rsqrt(column(sums, experts) / D + NORM_EPS)
-    logits = jnp.where(lanes < experts, sums * inv_rms, 0.0)
+    delta = column(sums, experts + 1)
+    raw = jnp.where(lanes < experts, sums, 0.0)
+    logits = raw * inv_rms
     first = route[:, 0:1]
     second = route[:, 1:2]
     logit_a = jnp.sum(jnp.where(lanes == first, logits, 0.0), axis=1, keepdims=True)
@@ -347,31 +343,14 @@
     gate_a = jax.nn.sigmoid(logit_a - logit_b)
     gate_b = jax.nn.sigmoid(logit_b - logit_a)
     gate = jnp.where(first == my_expert, gate_a, 0.0) + jnp.where(second == my_expert, gate_b, 0.0)
+    dlogit_a = gate_a * gate_b * delta
+    dlogits = jnp.where(lanes == first, dlogit_a, 0.0) - jnp.where(lanes == second, dlogit_a, 0.0)
+    along_raw = jnp.sum(raw * dlogits, axis=1, keepdims=True)
+    scaled = inv_rms * dlogits
+    along = along_raw * inv_rms * inv_rms * inv_rms / D
     columns[...] = jnp.where(
-        lanes < experts, sums, jnp.where(lanes == experts, inv_rms, gate_a * gate_b)
-    )
-    for k, grad in enumerate((g0, g1, g2, g3)):
-        start = pl.multiple_of((my_expert ^ k) * feats, LANES)
-        value = (gate * grad[...].astype(jnp.float32)).astype(jnp.bfloat16)
-        expert_grad[:, pl.ds(start, feats)] = lax.dot_general(
-            place[...], value, TN, preferred_element_type=jnp.float32
-        ).astype(jnp.bfloat16)
-
-
-def router_kernel(total_tokens, route, t0, t1, t2, t3, columns, resid, dcolumns, router_part):
-    experts = EXPERTS_ROW
-    rows = (t0[...] + t1[...]) + (t2[...] + t3[...])
-    delta = column(as_columns(rows), 0)
-    cols = columns[...]
-    lanes = iota(cols.shape, 1)
-    inv_rms = column(cols, experts)
-    dlogit_a = column(cols, experts + 1) * delta
-    dlogits = jnp.where(lanes == route[:, 0:1], dlogit_a, 0.0) - jnp.where(
-        lanes == route[:, 1:2], dlogit_a, 0.0
-    )
-    along_raw = jnp.sum(jnp.where(lanes < experts, cols, 0.0) * dlogits, axis=1, keepdims=True)
-    scaled = inv_rms * dlogits
-    dcolumns[...] = jnp.where(lanes == experts, along_raw * inv_rms * inv_rms * inv_rms / D, scaled)
+        lanes < experts, scaled, jnp.where(lanes == experts, along, gate)
+    )
     router_part[...] = (
         jnp.dot(
             as_rows(scaled),
@@ -383,22 +362,32 @@
     )
 
 
-def resid_grad_kernel(
-    meta, dcolumns, p0, p1, p2, p3, g0, g1, g2, g3, r0, r1, r2, r3, resid_grad
-):
+def expert_grad_kernel(meta, columns, place, g0, g1, g2, g3, expert_grad):
+    my_expert = meta[2]
+    feats = g0.shape[1]
+    gate = column(columns[...], EXPERTS_ROW + 1)
+    for k, grad in enumerate((g0, g1, g2, g3)):
+        start = pl.multiple_of((my_expert ^ k) * feats, LANES)
+        value = (gate * grad[...].astype(jnp.float32)).astype(jnp.bfloat16)
+        expert_grad[:, pl.ds(start, feats)] = lax.dot_general(
+            place[...], value, TN, preferred_element_type=jnp.float32
+        ).astype(jnp.bfloat16)
+
+
+def resid_grad_kernel(meta, columns, g0, g1, g2, g3, r0, r1, r2, r3, resid_grad):
     my_expert = meta[2]
     tok_rows, feats = g0.shape
-    cols = dcolumns[...]
+    cols = columns[...]
     weights = [column(cols, e) for e in range(EXPERTS_ROW)]
     along = column(cols, EXPERTS_ROW)
-    groups = ((p0, g0, r0), (p1, g1, r1), (p2, g2, r2), (p3, g3, r3))
-    for k, (pack, grad, resid) in enumerate(groups):
+    for k, (grad, resid) in enumerate(((g0, r0), (g1, r1), (g2, r2), (g3, r3))):
         start = pl.multiple_of((my_expert ^ k) * feats, LANES)
-        back = weights[0] * pack[0:1, 0:feats]
+        router = resid[tok_rows : tok_rows + ROW_TILE].astype(jnp.float32)
+        back = weights[0] * router[0:1]
         for e in range(1, EXPERTS_ROW):
-            back = back + weights[e] * pack[e : e + 1, 0:feats]
+            back = back + weights[e] * router[e : e + 1]
         resid_grad[:, pl.ds(start, feats)] = (
-            grad[...].astype(jnp.float32) + back - along * resid[...].astype(jnp.float32)
+            grad[...].astype(jnp.float32) + back - along * resid[0:tok_rows].astype(jnp.float32)
         ).astype(jnp.bfloat16)
 
 
@@ -447,6 +436,7 @@
 ):
     key_refs, value_refs, (dquery, d0, d1, d2, d3, total) = rest[0:4], rest[4:8], rest[8:]
     step = pl.program_id(0)
+    my_core = meta[0]
     my_seq = meta[1]
     tok_rows = query.shape[0]
     group = query.shape[1] // HEAD_DIM
@@ -457,7 +447,7 @@
     def _():
         total[...] = jnp.zeros_like(total)
 
-    for k, weight in enumerate((w0, w1, w2, w3)):
+    for k, weight in ((0, w0), (1 + my_core, w1), (2 - my_core, w2), (3, w3)):
         start = pl.multiple_of((my_seq ^ k) * feats + step * width, LANES)
         total[...] += lax.dot_general(
             resid_grad[:, pl.ds(start, width)], weight[...], NT, preferred_element_type=jnp.float32
@@ -507,6 +497,7 @@
 
 
 EXPERTS_ROW = 4
+ROW_TILE = 16
 
 
 def call(kernel, meta, args, outs):
@@ -514,12 +505,9 @@
     return pl.pallas_call(
         kernel,
         out_shape=shapes,
-        grid_spec=pltpu.PrefetchScalarGridSpec(
-            num_scalar_prefetch=1,
-            grid=(1,),
-            in_specs=[whole(a.shape) for a in args],
-            out_specs=[whole(s.shape) for s in shapes],
-        ),
+        in_specs=[pl.BlockSpec(memory_space=pltpu.SMEM)]
+        + [pl.BlockSpec(memory_space=pltpu.VMEM)] * len(args),
+        out_specs=[pl.BlockSpec(memory_space=pltpu.VMEM)] * len(shapes),
         compiler_params=params(),
     )(meta, *args)
 
@@ -545,49 +533,55 @@
     def over_seq(array):
         return [partner(array, "seq", seq_n, k) for k in range(1, seq_n)]
 
+    def over_both(array, step):
+        pairs = [
+            (c * seq_n + i, c * seq_n + (i ^ step(c))) for c in range(dp_n) for i in range(seq_n)
+        ]
+        return lax.ppermute(array, ("dp", "seq"), pairs)
+
     half_rows = o_weight.shape[0] // dp_n
-    mine = lax.dynamic_slice_in_dim(o_weight, core * half_rows, half_rows, axis=0)
-    weight_mine = over_seq(mine)
-    weight_other = [partner(w, "dp", dp_n, 1) for w in weight_mine]
-
     grads = over_expert(grad)
-    resids = over_expert(resid)
+    weight_near = over_both(o_weight, lambda c: 1 + c)
     pair = jnp.concatenate([key_in[0], value_in[0]], axis=1)
     pairs = [pair] + over_seq(pair)
-
+    resid_rows = jnp.concatenate(
+        [resid, jnp.pad(router_weight.T, ((0, ROW_TILE - EXPERTS_ROW), (0, 0)))], axis=0
+    )
+    resids = over_expert(resid_rows)
     router_pad = jnp.pad(router_weight, ((0, 0), (0, LANES - router_weight.shape[1])))
-    pack, place, saved_tok = call(
+    rows, place, saved_tok = call(
         prepare_kernel,
         meta,
         (route, router_pad, resid, saved),
         (
-            ((8, feats + tok_rows), f32),
+            ((8, tok_rows), f32),
             ((tok_rows, capacity), bf16),
             ((tok_rows, width), bf16),
         ),
     )
-    packs = over_expert(pack)
+    weight_near, grads[1:], pairs[1:], resids[1], rows, place, saved_tok = lax.optimization_barrier(
+        (weight_near, grads[1:], pairs[1:], resids[1], rows, place, saved_tok)
+    )
+    weight_far = partner(weight_near, "dp", dp_n, 1)
+    across = lax.dynamic_slice_in_dim(weight_near, core * half_rows, half_rows, axis=0)
+    across_mine = over_both(across, lambda c: 2 - c)
+
     (terms,) = call(
-        gate_grad_kernel, meta, (route, saved_tok, *grads), (((8, tok_rows), f32),)
-    )
-    all_terms = over_expert(terms)
-    expert_grad, columns = call(
-        expert_grad_kernel,
+        gate_grad_kernel, meta, (route, rows, saved_tok, *grads), (((8, tok_rows), f32),)
+    )
+    total_tokens = dp_n * seq_n * tok_rows
+    columns, router_part = call(
+        lambda meta, *refs: router_kernel(meta, total_tokens, *refs),
         meta,
-        (route, *packs, place, *grads),
-        (((capacity, width), bf16), ((tok_rows, LANES), f32)),
-    )
-    total_tokens = dp_n * seq_n * tok_rows
-    dcolumns, router_part = call(
-        lambda meta, *refs: router_kernel(total_tokens, *refs),
-        meta,
-        (route, *all_terms, columns, resid),
+        (route, *over_expert(terms), resid),
         (((tok_rows, LANES), f32), ((8, feats), f32)),
+    )
+    (expert_grad,) = call(
+        expert_grad_kernel, meta, (columns, place, *grads), (((capacity, width), bf16),)
     )
     router_pair = router_part + partner(router_part, "dp", dp_n, 1)
     r1, r2, r3 = over_seq(router_pair)
     router_sum = (router_pair + r1) + (r2 + r3)
-    router_grad = router_sum[0 : router_weight.shape[1]].T
 
     kv_width = key_in.shape[2]
     kv_count = kv_width // HEAD_DIM
@@ -601,10 +595,17 @@
             (query.shape, f32),
         ),
     )
+    across_mine, weight_far, resids[2:], columns, expert_grad, probs, attn_out = (
+        lax.optimization_barrier(
+            (across_mine, weight_far, resids[2:], columns, expert_grad, probs, attn_out)
+        )
+    )
+    across_other = partner(across_mine, "dp", dp_n, 1)
+    router_grad = router_sum[0 : router_weight.shape[1]].T
     (resid_grad,) = call(
         resid_grad_kernel,
         meta,
-        (dcolumns, *packs, *grads, *resids),
+        (columns, *grads, *resids),
         (((tok_rows, width), bf16),),
     )
 
@@ -616,7 +617,8 @@
             whole(resid_grad.shape),
             pl.BlockSpec((half_rows, feats // steps), lambda i, m: (head(i, m), i)),
         ]
-        in_specs += [pl.BlockSpec((half_rows, feats // steps), lambda i, m: (0, i))] * 3
+        in_specs += [pl.BlockSpec((half_rows, feats // steps), lambda i, m: (head(i, m), i))] * 2
+        in_specs += [pl.BlockSpec((half_rows, feats // steps), lambda i, m: (0, i))]
         in_specs += [
             pl.BlockSpec((tok_rows, wide), lambda i, m: (0, head(i, m))),
             pl.BlockSpec((1, group * tok_rows, seq_n * tok_rows), lambda i, m: (head(i, m), 0, 0)),
@@ -650,9 +652,9 @@
             for k in range(1, seq_n)
         ]
 
-    dquery_a, own_a, *terms_a = backward(0, weight_mine)
+    dquery_a, own_a, *terms_a = backward(0, (weight_near, weight_far, across_mine))
     back_a = send_back(terms_a)
-    dquery_b, own_b, *terms_b = backward(1, weight_other)
+    dquery_b, own_b, *terms_b = backward(1, (weight_near, weight_far, across_other))
     back_b = send_back(terms_b)
     key_grad, value_grad, query_grad = call(
         finish_kernel,

time: 174 us -> 130 us (0.75)
  Pallas kernels: 40.8 us -> 23.2 us
  starting transfers between devices: 47.4 us -> 30.8 us
  waiting for transfers between devices: 75 us -> 63.1 us
  other arithmetic: 1.25 us -> 3.3 us
    ppermute x25 -> x18, starting transfers between devices: 39.5 us -> 19.2 us  [partner(): return lax.ppermute(array, axis, [(i, i ^ distance) for i in range(count)])]
    pallas_call x7, Pallas kernels: 26 us -> 12.5 us  [call(): pl.pallas_call(kernel, out_shape=shapes, in_specs=[pl.BlockSpec(memory_sp...]
    ppermute x25 -> x18, waiting for transfers between devices: 67.1 us -> 55.3 us  [partner(): return lax.ppermute(array, axis, [(i, i ^ distance) for i in range(count)])]
    pallas_call x2, Pallas kernels: 14.9 us -> 10.8 us  [backward(): pl.pallas_call(backward_kernel, out_shape=shapes, grid_spec=pltpu.Prefetc...]
    ppermute x0 -> x2, starting transfers between devices: none -> 3.84 us  [over_both(): return lax.ppermute(array, ('dp', 'seq'), pairs)]
    unnamed x72 -> x18, local copies, waits for them, and re-layouts: 2.39 us -> 5.54 us
    dynamic_slice x1, local copies, waits for them, and re-layouts: 2.38 us -> 0.08 us  [local_fast(): lax.dynamic_slice_in_dim(weight_near, core * half_rows, half_rows, axis=0)]
  transfers between devices with their start and end apart: 31 -> 26, of which waited for: 14 -> 9; matrix products, arithmetic and copies ran while one was open for 2% -> 5% of each run, Pallas kernels for 22% -> 17%
where the time goes in v2:
time: 130 us; the launch traced here: 128 us
  waiting for transfers between devices  63.1 us (49%)
  starting transfers between devices  30.8 us (24%)
  Pallas kernels  23.2 us (18%)
  local copies, waits for them, and re-layouts  6.66 us (5%)
  other arithmetic  3.3 us (3%)
    ppermute x18, waiting for transfers between devices, partner(): return lax.ppermute(array, axis, [(i, i ^ distance) for i in range(count)])  55.3 us
    ppermute x18, starting transfers between devices, partner(): return lax.ppermute(array, axis, [(i, i ^ distance) for i in range(count)])  19.2 us
    pallas_call x7, Pallas kernels, call(): pl.pallas_call(kernel, out_shape=shapes, in_specs=[pl.BlockSpec(memory_sp...  12.5 us
    pallas_call x2, Pallas kernels, backward(): pl.pallas_call(backward_kernel, out_shape=shapes, grid_spec=pltpu.Prefetc...  10.8 us
    ppermute x6, waiting for transfers between devices, send_back(): lax.ppermute(terms[k - 1], 'seq', [(i, i ^ k) for i in range(seq_n) if i...  7.78 us
    ppermute x6, starting transfers between devices, send_back(): lax.ppermute(terms[k - 1], 'seq', [(i, i ^ k) for i in range(seq_n) if i...  7.74 us
    unnamed x18, local copies, waits for them, and re-layouts  5.54 us
    ppermute x2, starting transfers between devices, over_both(): return lax.ppermute(array, ('dp', 'seq'), pairs)  3.84 us
  transfers between devices with their start and end apart: 26, of which 9 were waited for; matrix products, arithmetic and copies ran while one was open for 5% of the time, Pallas kernels for 17%

profile of v2, /device:TPU:8, one launch (start us, length us, event | category | flops | bytes accessed | tf_op | source)
XLA Modules:
  0.0 127.9 jit_solution(14548169492742141563)
XLA Ops:
  0.6 1.6 %collective-permute-start = (bf16[1024,1024]{1,0:T(8,128)(2,1)}, bf16[1024,1024]{1,0:T(8,128)(2,1)S(1)}, u32[]{:S(2)}, u32[]{:S(2)}) collective-permute-start(bf16[1024,1024]{1,0:T(8,128)(2,1)} %w0.3), channel_id=1, source_target_pairs={{0,4},{4,0},{8,12},{12,8},{16,24},{20,28},{24,16},{28,20},{1,5},{5... | collective-permute-start | bytes 6291464 | tf_op jit(solution)/shard_map/ppermute | solution.py:540
  3.1 1.6 %collective-permute-start.6 = (bf16[128,512]{1,0:T(8,128)(2,1)S(1)}, bf16[128,512]{1,0:T(8,128)(2,1)S(1)}, u32[]{:S(2)}, u32[]{:S(2)}) collective-permute-start(bf16[128,512]{1,0:T(8,128)(2,1)S(1)} %pad_maximum_fusion.v0.rest_0_.rest_4_), channel_id=1, source_target_pairs={{0,12},{4,8},{8,4},{12,0},{1,13},{5,9},{9,5},{13,1},{2,14},{6,10},... | collective-permute-start | bytes 393224 | tf_op jit(solution)/shard_map/ppermute | solution.py:266
  5.1 1.5 %collective-permute-start.4 = (bf16[128,512]{1,0:T(8,128)(2,1)S(1)}, bf16[128,512]{1,0:T(8,128)(2,1)S(1)}, u32[]{:S(2)}, u32[]{:S(2)}) collective-permute-start(bf16[128,512]{1,0:T(8,128)(2,1)S(1)} %pad_maximum_fusion.v0.rest_0_.rest_4_), channel_id=1, source_target_pairs={{0,4},{4,0},{8,12},{12,8},{1,5},{5,1},{9,13},{13,9},{2,6},{6,2},{1... | collective-permute-start | bytes 393224 | tf_op jit(solution)/shard_map/ppermute | solution.py:266
  6.6 1.7 %fusion.1.r0 = bf16[144,1024]{1,0:T(8,128)(2,1)} fusion(bf16[4,1024]{1,0:T(4,128)(2,1)} %bitcast.36, bf16[128,1024]{1,0:T(8,128)(2,1)} %bitcast.20), kind=kLoop, calls=%fused_computation.2 | loop fusion | flops 884736 | bytes 565248 | tf_op jit(solution)/shard_map/concatenate | solution.py:547
  8.8 23.3 %collective-permute-done.6.v3.rest_3_.rest_7_ = bf16[128,512]{1,0:T(8,128)(2,1)S(1)} collective-permute-done((bf16[128,512]{1,0:T(8,128)(2,1)S(1)}, bf16[128,512]{1,0:T(8,128)(2,1)S(1)}, u32[]{:S(2)}, u32[]{:S(2)}) %collective-permute-start.6) | collective-permute-done | bytes 131104 | tf_op jit(solution)/shard_map/ppermute | solution.py:266
  32.1 1.6 %collective-permute-start.3 = (bf16[128,1024]{1,0:T(8,128)(2,1)}, bf16[128,1024]{1,0:T(8,128)(2,1)S(1)}, u32[]{:S(2)}, u32[]{:S(2)}) collective-permute-start(bf16[128,1024]{1,0:T(8,128)(2,1)} %bitcast.23), channel_id=1, source_target_pairs={{0,3},{1,2},{2,1},{3,0},{4,7},{5,6},{6,5},{7,4},{8,11},{9,10},{10,... | collective-permute-start | bytes 786440 | tf_op jit(solution)/shard_map/ppermute | solution.py:266
  34.9 1.3 %collective-permute-start.1 = (bf16[128,1024]{1,0:T(8,128)(2,1)}, bf16[128,1024]{1,0:T(8,128)(2,1)}, u32[]{:S(2)}, u32[]{:S(2)}) collective-permute-start(bf16[128,1024]{1,0:T(8,128)(2,1)} %bitcast.25), channel_id=1, source_target_pairs={{0,1},{1,0},{2,3},{3,2},{4,5},{5,4},{6,7},{7,6},{8,9},{9,8},{10,11... | collective-permute-start | bytes 786440 | tf_op jit(solution)/shard_map/ppermute | solution.py:266
  36.2 1.6 %copy.15 = bf16[1024,4]{1,0:T(8,128)(2,1)} copy(bf16[1024,4]{0,1:T(4,128)(2,1)} %param.15) | data formatting | bytes 16384 | tf_op args[6]
  41.9 1.3 %shard_map.128 = (f32[8,128]{1,0:T(8,128)S(1)}, bf16[128,128]{1,0:T(8,128)(2,1)S(1)}, bf16[128,4096]{1,0:T(8,128)(2,1)S(1)}) custom-call(s32[3]{0:T(128)S(1)} %pad_add_fusion.meta, s32[128,2]{1,0:T(8,128)S(1)} %bitcast.30, bf16[1024,128]{1,0:T(8,128)(2,1)S(1)} %pad.9.router_pad, bf16[128,1024]{1,0:T(8,128)(2,1)S(1)} %bitcast.21, bf16[128,4096]{1,0:T(8,128)(2,1)S(1)} %bitcast.29), custom_call_target="tpu_custom_call" | custom-call | tf_op jit(solution)/shard_map/pallas_call | solution.py:505
  44.2 3.3 %collective-permute-done.3.g3 = bf16[128,1024]{1,0:T(8,128)(2,1)S(1)} collective-permute-done((bf16[128,1024]{1,0:T(8,128)(2,1)}, bf16[128,1024]{1,0:T(8,128)(2,1)S(1)}, u32[]{:S(2)}, u32[]{:S(2)}) %collective-permute-start.3) | collective-permute-done | bytes 262176 | tf_op jit(solution)/shard_map/ppermute | solution.py:266
  47.5 2.8 %collective-permute-done.2.g2 = bf16[128,1024]{1,0:T(8,128)(2,1)S(1)} collective-permute-done((bf16[128,1024]{1,0:T(8,128)(2,1)}, bf16[128,1024]{1,0:T(8,128)(2,1)S(1)}, u32[]{:S(2)}, u32[]{:S(2)}) %collective-permute-start.2) | collective-permute-done | bytes 262176 | tf_op jit(solution)/shard_map/ppermute | solution.py:266
  50.6 2.3 %collective-permute-start.8 = (bf16[512,1024]{1,0:T(8,128)(2,1)S(1)}, bf16[512,1024]{1,0:T(8,128)(2,1)S(1)}, u32[]{:S(2)}, u32[]{:S(2)}) collective-permute-start(bf16[512,1024]{1,0:T(8,128)(2,1)S(1)} %constant_dynamic-slice_fusion), channel_id=1, source_target_pairs={{0,8},{4,12},{8,0},{12,4},{16,20},{20,16},{24,28},{28,24},{1,9},{5... | collective-permute-start | bytes 3145736 | tf_op jit(solution)/shard_map/ppermute | solution.py:540
  52.8 3.9 %collective-permute-start.10 = (bf16[144,1024]{1,0:T(8,128)(2,1)}, bf16[144,1024]{1,0:T(8,128)(2,1)S(1)}, u32[]{:S(2)}, u32[]{:S(2)}) collective-permute-start(bf16[144,1024]{1,0:T(8,128)(2,1)} %fusion.1.r0), channel_id=1, source_target_pairs={{0,2},{1,3},{2,0},{3,1},{4,6},{5,7},{6,4},{7,5},{8,10},{9,11},{10,... | collective-permute-start | bytes 884744 | tf_op jit(solution)/shard_map/ppermute | solution.py:266
  56.7 1.4 %shard_map.129.refs_1_ = f32[8,128]{1,0:T(8,128)S(1)} custom-call(s32[3]{0:T(128)S(1)} %pad_add_fusion.meta, s32[128,2]{1,0:T(8,128)S(1)} %bitcast.31, f32[8,128]{1,0:T(8,128)S(1)} %get-tuple-element.48.rows, bf16[128,4096]{1,0:T(8,128)(2,1)S(1)} %copy-done.7, bf16[128,1024]{1,0:T(8,128)(2,1)S(1)} %bitcast.26, bf16[128,1024]{1,0:T(8,128)(2,1)} %collective-permute-done.1.g1, ...), custom_call_target="tpu_custom_call" | custom-call | tf_op jit(solution)/shard_map/pallas_call | solution.py:505
  58.1 2.4 %collective-permute-start.14 = (f32[8,128]{1,0:T(8,128)S(1)}, f32[8,128]{1,0:T(8,128)S(1)}, u32[]{:S(2)}, u32[]{:S(2)}) collective-permute-start(f32[8,128]{1,0:T(8,128)S(1)} %shard_map.129.refs_1_), channel_id=1, source_target_pairs={{0,3},{1,2},{2,1},{3,0},{4,7},{5,6},{6,5},{7,4},{8,11},{9,10},{10,... | collective-permute-start | bytes 12296 | tf_op jit(solution)/shard_map/ppermute | solution.py:266
  60.5 20.1 %collective-permute-done.14.refs_4_ = f32[8,128]{1,0:T(8,128)S(1)} collective-permute-done((f32[8,128]{1,0:T(8,128)S(1)}, f32[8,128]{1,0:T(8,128)S(1)}, u32[]{:S(2)}, u32[]{:S(2)}) %collective-permute-start.14) | collective-permute-done | bytes 4128 | tf_op jit(solution)/shard_map/ppermute | solution.py:266
  80.6 4.5 %collective-permute-done.13.refs_3_ = f32[8,128]{1,0:T(8,128)S(1)} collective-permute-done((f32[8,128]{1,0:T(8,128)S(1)}, f32[8,128]{1,0:T(8,128)S(1)}, u32[]{:S(2)}, u32[]{:S(2)}) %collective-permute-start.13) | collective-permute-done | bytes 4128 | tf_op jit(solution)/shard_map/ppermute | solution.py:266
  85.1 2.4 %shard_map.132 = (f32[2,512,512]{2,1,0:T(8,128)S(1)}, f32[128,1024]{1,0:T(8,128)S(1)}) custom-call(s32[3]{0:T(128)S(1)} %pad_add_fusion.meta, bf16[128,1024]{1,0:T(8,128)(2,1)S(1)} %bitcast.17, bf16[128,512]{1,0:T(8,128)(2,1)S(1)} %pad_maximum_fusion.v0.rest_0_.rest_4_, bf16[128,512]{1,0:T(8,128)(2,1)S(1)} %collective-permute-done.4.v1.rest_1_.rest_5_, ...), custom_call_target="tpu_custom_call" | custom-call | tf_op jit(solution)/shard_map/pallas_call | solution.py:505
  89.9 2.5 %shard_map.131 = bf16[128,4096]{1,0:T(8,128)(2,1)} custom-call(s32[3]{0:T(128)S(1)} %pad_add_fusion.meta, f32[128,128]{1,0:T(8,128)S(1)} %get-tuple-element.60.columns, bf16[128,128]{1,0:T(8,128)(2,1)S(1)} %get-tuple-element.54.place, bf16[128,1024]{1,0:T(8,128)(2,1)S(1)} %bitcast.27, bf16[128,1024]{1,0:T(8,128)(2,1)} %collective-permute-done.1.g1, ...), custom_call_target="tpu_custom_call" | custom-call | tf_op jit(solution)/shard_map/pallas_call | solution.py:505
  93.0 2.3 %shard_map.133.resid_grad = bf16[128,4096]{1,0:T(8,128)(2,1)S(1)} custom-call(s32[3]{0:T(128)S(1)} %pad_add_fusion.meta, f32[128,128]{1,0:T(8,128)S(1)} %get-tuple-element.60.columns, bf16[128,1024]{1,0:T(8,128)(2,1)S(1)} %bitcast.28, bf16[128,1024]{1,0:T(8,128)(2,1)} %collective-permute-done.1.g1, bf16[128,1024]{1,0:T(8,128)(2,1)S(1)} %collective-permute-done.2.g2, ...), custom_call_target="tpu_custom_call" | custom-call | tf_op jit(solution)/shard_map/pallas_call | solution.py:505
  95.3 5.4 %shard_map.134 = (bf16[128,512]{1,0:T(8,128)(2,1)S(1)}, f32[128,256]{1,0:T(8,128)S(1)}, bf16[128,256]{1,0:T(8,128)(2,1)S(1)}, bf16[128,256]{1,0:T(8,128)(2,1)S(1)}, bf16[128,256]{1,0:T(8,128)(2,1)S(1)}) custom-call(s32[3]{0:T(128)S(1)} %pad_add_fusion.meta, bf16[128,4096]{1,0:T(8,128)(2,1)S(1)} %shard_map.133.resid_grad, bf16[1024,1024]{1,0:T(8,128)(2,1)S(1)} %copy-done, ...), custom_call_target="tpu_custom_call" | custom-call | tf_op jit(solution)/shard_map/pallas_call | solution.py:634
  100.7 1.3 %collective-permute-start.15 = (bf16[128,256]{1,0:T(8,128)(2,1)S(1)}, bf16[128,256]{1,0:T(8,128)(2,1)S(1)}, u32[]{:S(2)}, u32[]{:S(2)}) collective-permute-start(bf16[128,256]{1,0:T(8,128)(2,1)S(1)} %get-tuple-element.69), channel_id=1, source_target_pairs={{4,0},{12,8},{5,1},{13,9},{6,2},{14,10},{7,3},{15,11},{20,16},{28,... | collective-permute-start | bytes 196616 | tf_op jit(solution)/shard_map/ppermute | solution.py:649
  102.0 3.2 %collective-permute-start.25 = (f32[8,1024]{1,0:T(8,128)S(1)}, f32[8,1024]{1,0:T(8,128)S(1)}, u32[]{:S(2)}, u32[]{:S(2)}) collective-permute-start(f32[8,1024]{1,0:T(8,128)S(1)} %add.20), channel_id=1, source_target_pairs={{0,12},{4,8},{8,4},{12,0},{1,13},{5,9},{9,5},{13,1},{2,14},{6,10},... | collective-permute-start | bytes 98312 | tf_op jit(solution)/shard_map/ppermute | solution.py:266
  107.5 5.4 %shard_map.135 = (bf16[128,512]{1,0:T(8,128)(2,1)S(1)}, f32[128,256]{1,0:T(8,128)S(1)}, bf16[128,256]{1,0:T(8,128)(2,1)S(1)}, bf16[128,256]{1,0:T(8,128)(2,1)S(1)}, bf16[128,256]{1,0:T(8,128)(2,1)S(1)}) custom-call(s32[3]{0:T(128)S(1)} %pad_add_fusion.meta, bf16[128,4096]{1,0:T(8,128)(2,1)S(1)} %shard_map.133.resid_grad, bf16[1024,1024]{1,0:T(8,128)(2,1)S(1)} %copy-done, ...), custom_call_target="tpu_custom_call" | custom-call | tf_op jit(solution)/shard_map/pallas_call | solution.py:634
  112.9 1.3 %collective-permute-start.17 = (bf16[128,256]{1,0:T(8,128)(2,1)S(1)}, bf16[128,256]{1,0:T(8,128)(2,1)S(1)}, u32[]{:S(2)}, u32[]{:S(2)}) collective-permute-start(bf16[128,256]{1,0:T(8,128)(2,1)S(1)} %get-tuple-element.71), channel_id=1, source_target_pairs={{8,4},{12,0},{9,5},{13,1},{10,6},{14,2},{11,7},{15,3},{24,20},{28,... | collective-permute-start | bytes 196616 | tf_op jit(solution)/shard_map/ppermute | solution.py:649
  114.2 1.3 %collective-permute-start.19 = (bf16[128,256]{1,0:T(8,128)(2,1)S(1)}, bf16[128,256]{1,0:T(8,128)(2,1)S(1)}, u32[]{:S(2)}, u32[]{:S(2)}) collective-permute-start(bf16[128,256]{1,0:T(8,128)(2,1)S(1)} %get-tuple-element.73), channel_id=1, source_target_pairs={{4,0},{12,8},{5,1},{13,9},{6,2},{14,10},{7,3},{15,11},{20,16},{28,... | collective-permute-start | bytes 196616 | tf_op jit(solution)/shard_map/ppermute | solution.py:649
  115.6 1.3 %collective-permute-start.20 = (bf16[128,256]{1,0:T(8,128)(2,1)S(1)}, bf16[128,256]{1,0:T(8,128)(2,1)S(1)}, u32[]{:S(2)}, u32[]{:S(2)}) collective-permute-start(bf16[128,256]{1,0:T(8,128)(2,1)S(1)} %get-tuple-element.74), channel_id=1, source_target_pairs={{8,0},{12,4},{9,1},{13,5},{10,2},{14,6},{11,3},{15,7},{24,16},{28,... | collective-permute-start | bytes 196616 | tf_op jit(solution)/shard_map/ppermute | solution.py:649
  116.9 1.3 %collective-permute-start.21 = (bf16[128,256]{1,0:T(8,128)(2,1)S(1)}, bf16[128,256]{1,0:T(8,128)(2,1)S(1)}, u32[]{:S(2)}, u32[]{:S(2)}) collective-permute-start(bf16[128,256]{1,0:T(8,128)(2,1)S(1)} %get-tuple-element.75), channel_id=1, source_target_pairs={{8,4},{12,0},{9,5},{13,1},{10,6},{14,2},{11,7},{15,3},{24,20},{28,... | collective-permute-start | bytes 196616 | tf_op jit(solution)/shard_map/ppermute | solution.py:649
  118.8 1.8 %collective-permute-done.17.a3 = bf16[128,256]{1,0:T(8,128)(2,1)S(1)} collective-permute-done((bf16[128,256]{1,0:T(8,128)(2,1)S(1)}, bf16[128,256]{1,0:T(8,128)(2,1)S(1)}, u32[]{:S(2)}, u32[]{:S(2)}) %collective-permute-start.17) | collective-permute-done | bytes 65568 | tf_op jit(solution)/shard_map/ppermute | solution.py:649
  120.6 2.6 %collective-permute-done.20.b2 = bf16[128,256]{1,0:T(8,128)(2,1)S(1)} collective-permute-done((bf16[128,256]{1,0:T(8,128)(2,1)S(1)}, bf16[128,256]{1,0:T(8,128)(2,1)S(1)}, u32[]{:S(2)}, u32[]{:S(2)}) %collective-permute-start.20) | collective-permute-done | bytes 65568 | tf_op jit(solution)/shard_map/ppermute | solution.py:649
  123.2 3.4 %collective-permute-done.21.b3 = bf16[128,256]{1,0:T(8,128)(2,1)S(1)} collective-permute-done((bf16[128,256]{1,0:T(8,128)(2,1)S(1)}, bf16[128,256]{1,0:T(8,128)(2,1)S(1)}, u32[]{:S(2)}, u32[]{:S(2)}) %collective-permute-start.21) | collective-permute-done | bytes 65568 | tf_op jit(solution)/shard_map/ppermute | solution.py:649
  126.6 1.3 %shard_map.136 = (bf16[128,256]{1,0:T(8,128)(2,1)}, bf16[128,256]{1,0:T(8,128)(2,1)}, bf16[128,1024]{1,0:T(8,128)(2,1)}) custom-call(s32[3]{0:T(128)S(1)} %pad_add_fusion.meta, f32[128,256]{1,0:T(8,128)S(1)} %get-tuple-element.68.a0, bf16[128,256]{1,0:T(8,128)(2,1)S(1)} %collective-permute-done.15.a1, bf16[128,256]{1,0:T(8,128)(2,1)S(1)} %collective-permute-done.16.a2, ...), custom_call_target="tpu_custom_call" | custom-call | tf_op jit(solution)/shard_map/pallas_call | solution.py:505
  (54 shorter events, 14.3 us)
Async XLA Ops:
  0.6 49.7 %collective-permute-start = (bf16[1024,1024]{1,0:T(8,128)(2,1)}, bf16[1024,1024]{1,0:T(8,128)(2,1)S(1)}, u32[]{:S(2)}, u32[]{:S(2)}) collective-permute-start(bf16[1024,1024]{1,0:T(8,128)(2,1)} %w0.3), channel_id=1, source_target_pairs={{0,4},{4,0},{8,12},{12,8},{16,24},{20,28},{24,16},{28,20},{1,5},{5... | collective-permute-start | bytes 6291464 | tf_op jit(solution)/shard_map/ppermute | solution.py:540
  3.1 29.0 %collective-permute-start.6 = (bf16[128,512]{1,0:T(8,128)(2,1)S(1)}, bf16[128,512]{1,0:T(8,128)(2,1)S(1)}, u32[]{:S(2)}, u32[]{:S(2)}) collective-permute-start(bf16[128,512]{1,0:T(8,128)(2,1)S(1)} %pad_maximum_fusion.v0.rest_0_.rest_4_), channel_id=1, source_target_pairs={{0,12},{4,8},{8,4},{12,0},{1,13},{5,9},{9,5},{13,1},{2,14},{6,10},... | collective-permute-start | bytes 393224 | tf_op jit(solution)/shard_map/ppermute | solution.py:266
  4.6 29.1 %collective-permute-start.5 = (bf16[128,512]{1,0:T(8,128)(2,1)S(1)}, bf16[128,512]{1,0:T(8,128)(2,1)S(1)}, u32[]{:S(2)}, u32[]{:S(2)}) collective-permute-start(bf16[128,512]{1,0:T(8,128)(2,1)S(1)} %pad_maximum_fusion.v0.rest_0_.rest_4_), channel_id=1, source_target_pairs={{0,8},{4,12},{8,0},{12,4},{1,9},{5,13},{9,1},{13,5},{2,10},{6,14},... | collective-permute-start | bytes 393224 | tf_op jit(solution)/shard_map/ppermute | solution.py:266
  5.1 29.8 %collective-permute-start.4 = (bf16[128,512]{1,0:T(8,128)(2,1)S(1)}, bf16[128,512]{1,0:T(8,128)(2,1)S(1)}, u32[]{:S(2)}, u32[]{:S(2)}) collective-permute-start(bf16[128,512]{1,0:T(8,128)(2,1)S(1)} %pad_maximum_fusion.v0.rest_0_.rest_4_), channel_id=1, source_target_pairs={{0,4},{4,0},{8,12},{12,8},{1,5},{5,1},{9,13},{13,9},{2,6},{6,2},{1... | collective-permute-start | bytes 393224 | tf_op jit(solution)/shard_map/ppermute | solution.py:266
  8.3 42.0 %collective-permute-start.7 = (bf16[144,1024]{1,0:T(8,128)(2,1)}, bf16[144,1024]{1,0:T(8,128)(2,1)}, u32[]{:S(2)}, u32[]{:S(2)}) collective-permute-start(bf16[144,1024]{1,0:T(8,128)(2,1)} %fusion.1.r0), channel_id=1, source_target_pairs={{0,1},{1,0},{2,3},{3,2},{4,5},{5,4},{6,7},{7,6},{8,9},{9,8},{10,11... | collective-permute-start | bytes 884744 | tf_op jit(solution)/shard_map/ppermute | solution.py:266
  32.1 15.4 %collective-permute-start.3 = (bf16[128,1024]{1,0:T(8,128)(2,1)}, bf16[128,1024]{1,0:T(8,128)(2,1)S(1)}, u32[]{:S(2)}, u32[]{:S(2)}) collective-permute-start(bf16[128,1024]{1,0:T(8,128)(2,1)} %bitcast.23), channel_id=1, source_target_pairs={{0,3},{1,2},{2,1},{3,0},{4,7},{5,6},{6,5},{7,4},{8,11},{9,10},{10,... | collective-permute-start | bytes 786440 | tf_op jit(solution)/shard_map/ppermute | solution.py:266
  33.7 16.6 %collective-permute-start.2 = (bf16[128,1024]{1,0:T(8,128)(2,1)}, bf16[128,1024]{1,0:T(8,128)(2,1)S(1)}, u32[]{:S(2)}, u32[]{:S(2)}) collective-permute-start(bf16[128,1024]{1,0:T(8,128)(2,1)} %bitcast.24), channel_id=1, source_target_pairs={{0,2},{1,3},{2,0},{3,1},{4,6},{5,7},{6,4},{7,5},{8,10},{9,11},{10,... | collective-permute-start | bytes 786440 | tf_op jit(solution)/shard_map/ppermute | solution.py:266
  34.9 15.4 %collective-permute-start.1 = (bf16[128,1024]{1,0:T(8,128)(2,1)}, bf16[128,1024]{1,0:T(8,128)(2,1)}, u32[]{:S(2)}, u32[]{:S(2)}) collective-permute-start(bf16[128,1024]{1,0:T(8,128)(2,1)} %bitcast.25), channel_id=1, source_target_pairs={{0,1},{1,0},{2,3},{3,2},{4,5},{5,4},{6,7},{7,6},{8,9},{9,8},{10,11... | collective-permute-start | bytes 786440 | tf_op jit(solution)/shard_map/ppermute | solution.py:266
  38.6 18.1 %copy-start.4 = (bf16[1,128,1024]{2,1,0:T(8,128)(2,1)S(1)}, bf16[1,128,1024]{2,1,0:T(8,128)(2,1)}, u32[]{:S(2)}) copy-start(bf16[1,128,1024]{2,1,0:T(8,128)(2,1)} %param.13) | copy-start | bytes 786436
  40.7 1.2 copy-start.5
  50.3 42.1 %collective-permute-start.9 = (bf16[1024,1024]{1,0:T(8,128)(2,1)S(1)}, bf16[1024,1024]{1,0:T(8,128)(2,1)}, u32[]{:S(2)}, u32[]{:S(2)}) collective-permute-start(bf16[1024,1024]{1,0:T(8,128)(2,1)S(1)} %collective-permute-done.w1), channel_id=1, source_target_pairs={{0,16},{16,0},{1,17},{17,1},{2,18},{18,2},{3,19},{19,3},{4,20},{20... | collective-permute-start | bytes 6291464 | tf_op jit(solution)/shard_map/ppermute | solution.py:266
  50.4 6.3 %copy-start.7 = (bf16[128,4096]{1,0:T(8,128)(2,1)S(1)}, bf16[128,4096]{1,0:T(8,128)(2,1)}, u32[]{:S(2)}) copy-start(bf16[128,4096]{1,0:T(8,128)(2,1)} %copy-done.6) | copy-start | bytes 3145732
  50.4 34.7 %copy-start.1 = (bf16[1,128,1024]{2,1,0:T(8,128)(2,1)S(1)}, bf16[1,128,1024]{2,1,0:T(8,128)(2,1)}, u32[]{:S(2)}) copy-start(bf16[1,128,1024]{2,1,0:T(8,128)(2,1)} %param.9) | copy-start | bytes 786436
  50.5 38.2 %copy-start.3 = (bf16[1,128,1024]{2,1,0:T(8,128)(2,1)S(1)}, bf16[1,128,1024]{2,1,0:T(8,128)(2,1)}, u32[]{:S(2)}) copy-start(bf16[1,128,1024]{2,1,0:T(8,128)(2,1)} %param.12) | copy-start | bytes 786436
  50.6 41.9 %collective-permute-start.8 = (bf16[512,1024]{1,0:T(8,128)(2,1)S(1)}, bf16[512,1024]{1,0:T(8,128)(2,1)S(1)}, u32[]{:S(2)}, u32[]{:S(2)}) collective-permute-start(bf16[512,1024]{1,0:T(8,128)(2,1)S(1)} %constant_dynamic-slice_fusion), channel_id=1, source_target_pairs={{0,8},{4,12},{8,0},{12,4},{16,20},{20,16},{24,28},{28,24},{1,9},{5... | collective-permute-start | bytes 3145736 | tf_op jit(solution)/shard_map/ppermute | solution.py:540
  52.8 39.6 %collective-permute-start.11 = (bf16[144,1024]{1,0:T(8,128)(2,1)}, bf16[144,1024]{1,0:T(8,128)(2,1)S(1)}, u32[]{:S(2)}, u32[]{:S(2)}) collective-permute-start(bf16[144,1024]{1,0:T(8,128)(2,1)} %fusion.1.r0), channel_id=1, source_target_pairs={{0,3},{1,2},{2,1},{3,0},{4,7},{5,6},{6,5},{7,4},{8,11},{9,10},{10,... | collective-permute-start | bytes 884744 | tf_op jit(solution)/shard_map/ppermute | solution.py:266
  52.8 39.6 %collective-permute-start.10 = (bf16[144,1024]{1,0:T(8,128)(2,1)}, bf16[144,1024]{1,0:T(8,128)(2,1)S(1)}, u32[]{:S(2)}, u32[]{:S(2)}) collective-permute-start(bf16[144,1024]{1,0:T(8,128)(2,1)} %fusion.1.r0), channel_id=1, source_target_pairs={{0,2},{1,3},{2,0},{3,1},{4,6},{5,7},{6,4},{7,5},{8,10},{9,11},{10,... | collective-permute-start | bytes 884744 | tf_op jit(solution)/shard_map/ppermute | solution.py:266
  58.1 22.5 %collective-permute-start.14 = (f32[8,128]{1,0:T(8,128)S(1)}, f32[8,128]{1,0:T(8,128)S(1)}, u32[]{:S(2)}, u32[]{:S(2)}) collective-permute-start(f32[8,128]{1,0:T(8,128)S(1)} %shard_map.129.refs_1_), channel_id=1, source_target_pairs={{0,3},{1,2},{2,1},{3,0},{4,7},{5,6},{6,5},{7,4},{8,11},{9,10},{10,... | collective-permute-start | bytes 12296 | tf_op jit(solution)/shard_map/ppermute | solution.py:266
  80.6 4.5 %collective-permute-start.13 = (f32[8,128]{1,0:T(8,128)S(1)}, f32[8,128]{1,0:T(8,128)S(1)}, u32[]{:S(2)}, u32[]{:S(2)}) collective-permute-start(f32[8,128]{1,0:T(8,128)S(1)} %shard_map.129.refs_1_), channel_id=1, source_target_pairs={{0,2},{1,3},{2,0},{3,1},{4,6},{5,7},{6,4},{7,5},{8,10},{9,11},{10,... | collective-permute-start | bytes 12296 | tf_op jit(solution)/shard_map/ppermute | solution.py:266
  85.1 3.6 %collective-permute-start.12 = (f32[8,128]{1,0:T(8,128)S(1)}, f32[8,128]{1,0:T(8,128)S(1)}, u32[]{:S(2)}, u32[]{:S(2)}) collective-permute-start(f32[8,128]{1,0:T(8,128)S(1)} %shard_map.129.refs_1_), channel_id=1, source_target_pairs={{0,1},{1,0},{2,3},{3,2},{4,5},{5,4},{6,7},{7,6},{8,9},{9,8},{10,11... | collective-permute-start | bytes 12296 | tf_op jit(solution)/shard_map/ppermute | solution.py:266
  92.4 2.9 %copy-start = (bf16[1024,1024]{1,0:T(8,128)(2,1)S(1)}, bf16[1024,1024]{1,0:T(8,128)(2,1)}, u32[]{:S(2)}) copy-start(bf16[1024,1024]{1,0:T(8,128)(2,1)} %w0.3) | copy-start | bytes 6291460
  92.4 13.8 %collective-permute-start.18 = (bf16[512,1024]{1,0:T(8,128)(2,1)S(1)}, bf16[512,1024]{1,0:T(8,128)(2,1)S(1)}, u32[]{:S(2)}, u32[]{:S(2)}) collective-permute-start(bf16[512,1024]{1,0:T(8,128)(2,1)S(1)} %collective-permute-done.8.w3), channel_id=1, source_target_pairs={{0,16},{16,0},{1,17},{17,1},{2,18},{18,2},{3,19},{19,3},{4,20},{20... | collective-permute-start | bytes 3145736 | tf_op jit(solution)/shard_map/ppermute | solution.py:266
  92.5 9.5 %collective-permute-start.22 = (f32[8,1024]{1,0:T(8,128)S(1)}, f32[8,1024]{1,0:T(8,128)S(1)}, u32[]{:S(2)}, u32[]{:S(2)}) collective-permute-start(f32[8,1024]{1,0:T(8,128)S(1)} %get-tuple-element.81), channel_id=1, source_target_pairs={{0,16},{16,0},{1,17},{17,1},{2,18},{18,2},{3,19},{19,3},{4,20},{20... | collective-permute-start | bytes 98312 | tf_op jit(solution)/shard_map/ppermute | solution.py:266
  100.7 16.1 %collective-permute-start.15 = (bf16[128,256]{1,0:T(8,128)(2,1)S(1)}, bf16[128,256]{1,0:T(8,128)(2,1)S(1)}, u32[]{:S(2)}, u32[]{:S(2)}) collective-permute-start(bf16[128,256]{1,0:T(8,128)(2,1)S(1)} %get-tuple-element.69), channel_id=1, source_target_pairs={{4,0},{12,8},{5,1},{13,9},{6,2},{14,10},{7,3},{15,11},{20,16},{28,... | collective-permute-start | bytes 196616 | tf_op jit(solution)/shard_map/ppermute | solution.py:649
  102.0 10.9 %collective-permute-start.25 = (f32[8,1024]{1,0:T(8,128)S(1)}, f32[8,1024]{1,0:T(8,128)S(1)}, u32[]{:S(2)}, u32[]{:S(2)}) collective-permute-start(f32[8,1024]{1,0:T(8,128)S(1)} %add.20), channel_id=1, source_target_pairs={{0,12},{4,8},{8,4},{12,0},{1,13},{5,9},{9,5},{13,1},{2,14},{6,10},... | collective-permute-start | bytes 98312 | tf_op jit(solution)/shard_map/ppermute | solution.py:266
  105.2 9.0 %collective-permute-start.24 = (f32[8,1024]{1,0:T(8,128)S(1)}, f32[8,1024]{1,0:T(8,128)S(1)}, u32[]{:S(2)}, u32[]{:S(2)}) collective-permute-start(f32[8,1024]{1,0:T(8,128)S(1)} %add.20), channel_id=1, source_target_pairs={{0,8},{4,12},{8,0},{12,4},{1,9},{5,13},{9,1},{13,5},{2,10},{6,14},... | collective-permute-start | bytes 98312 | tf_op jit(solution)/shard_map/ppermute | solution.py:266
  106.2 9.3 %collective-permute-start.23 = (f32[8,1024]{1,0:T(8,128)S(1)}, f32[8,1024]{1,0:T(8,128)S(1)}, u32[]{:S(2)}, u32[]{:S(2)}) collective-permute-start(f32[8,1024]{1,0:T(8,128)S(1)} %add.20), channel_id=1, source_target_pairs={{0,4},{4,0},{8,12},{12,8},{1,5},{5,1},{9,13},{13,9},{2,6},{6,2},{1... | collective-permute-start | bytes 98312 | tf_op jit(solution)/shard_map/ppermute | solution.py:266
  106.2 12.6 %collective-permute-start.16 = (bf16[128,256]{1,0:T(8,128)(2,1)S(1)}, bf16[128,256]{1,0:T(8,128)(2,1)S(1)}, u32[]{:S(2)}, u32[]{:S(2)}) collective-permute-start(bf16[128,256]{1,0:T(8,128)(2,1)S(1)} %get-tuple-element.70), channel_id=1, source_target_pairs={{8,0},{12,4},{9,1},{13,5},{10,2},{14,6},{11,3},{15,7},{24,16},{28,... | collective-permute-start | bytes 196616 | tf_op jit(solution)/shard_map/ppermute | solution.py:649
  112.9 7.6 %collective-permute-start.17 = (bf16[128,256]{1,0:T(8,128)(2,1)S(1)}, bf16[128,256]{1,0:T(8,128)(2,1)S(1)}, u32[]{:S(2)}, u32[]{:S(2)}) collective-permute-start(bf16[128,256]{1,0:T(8,128)(2,1)S(1)} %get-tuple-element.71), channel_id=1, source_target_pairs={{8,4},{12,0},{9,5},{13,1},{10,6},{14,2},{11,7},{15,3},{24,20},{28,... | collective-permute-start | bytes 196616 | tf_op jit(solution)/shard_map/ppermute | solution.py:649
  114.2 6.3 %collective-permute-start.19 = (bf16[128,256]{1,0:T(8,128)(2,1)S(1)}, bf16[128,256]{1,0:T(8,128)(2,1)S(1)}, u32[]{:S(2)}, u32[]{:S(2)}) collective-permute-start(bf16[128,256]{1,0:T(8,128)(2,1)S(1)} %get-tuple-element.73), channel_id=1, source_target_pairs={{4,0},{12,8},{5,1},{13,9},{6,2},{14,10},{7,3},{15,11},{20,16},{28,... | collective-permute-start | bytes 196616 | tf_op jit(solution)/shard_map/ppermute | solution.py:649
  115.6 7.6 %collective-permute-start.20 = (bf16[128,256]{1,0:T(8,128)(2,1)S(1)}, bf16[128,256]{1,0:T(8,128)(2,1)S(1)}, u32[]{:S(2)}, u32[]{:S(2)}) collective-permute-start(bf16[128,256]{1,0:T(8,128)(2,1)S(1)} %get-tuple-element.74), channel_id=1, source_target_pairs={{8,0},{12,4},{9,1},{13,5},{10,2},{14,6},{11,3},{15,7},{24,16},{28,... | collective-permute-start | bytes 196616 | tf_op jit(solution)/shard_map/ppermute | solution.py:649
  116.9 9.7 %collective-permute-start.21 = (bf16[128,256]{1,0:T(8,128)(2,1)S(1)}, bf16[128,256]{1,0:T(8,128)(2,1)S(1)}, u32[]{:S(2)}, u32[]{:S(2)}) collective-permute-start(bf16[128,256]{1,0:T(8,128)(2,1)S(1)} %get-tuple-element.75), channel_id=1, source_target_pairs={{8,4},{12,0},{9,5},{13,1},{10,6},{14,2},{11,7},{15,3},{24,20},{28,... | collective-permute-start | bytes 196616 | tf_op jit(solution)/shard_map/ppermute | solution.py:649
  (2 other events, 1.9 us)

commit v3 on v2

--- a/solution.py
+++ b/solution.py
@@ -313,14 +313,21 @@
     rows[...] = as_rows(jnp.where(lanes == EXPERTS_ROW, square, raw))
 
 
-def gate_grad_kernel(meta, route, rows, saved_tok, g0, g1, g2, g3, terms):
+def spread(my_expert, refs, rows):
+    for k, ref in enumerate(refs):
+        yield my_expert ^ k, lambda ref=ref: ref[rows].astype(jnp.float32)
+
+
+def gate_grad_kernel(meta, route, rows, saved_tok, *refs):
+    blocks, terms = refs[:-1], refs[-1]
     my_expert = meta[2]
-    tok_rows, feats = g0.shape
+    tok_rows = route.shape[0]
+    feats = blocks[0].shape[1]
     total = jnp.zeros((tok_rows, 1), jnp.float32)
-    for k, grad in enumerate((g0, g1, g2, g3)):
-        start = pl.multiple_of((my_expert ^ k) * feats, LANES)
+    for index, grad in spread(my_expert, blocks, slice(0, tok_rows)):
+        start = pl.multiple_of(index * feats, LANES)
         saved = saved_tok[:, pl.ds(start, feats)].astype(jnp.float32)
-        total = total + jnp.sum(grad[...].astype(jnp.float32) * saved, axis=1, keepdims=True)
+        total = total + jnp.sum(grad() * saved, axis=1, keepdims=True)
     first = (route[:, 0:1] == my_expert).astype(jnp.float32)
     second = (route[:, 1:2] == my_expert).astype(jnp.float32)
     signed = as_rows(jnp.broadcast_to((first - second) * total, (tok_rows, LANES)))
@@ -362,33 +369,44 @@
     )
 
 
-def expert_grad_kernel(meta, columns, place, g0, g1, g2, g3, expert_grad):
-    my_expert = meta[2]
-    feats = g0.shape[1]
+def expert_grad_kernel(meta, columns, place, *refs):
+    blocks, expert_grad = refs[:-1], refs[-1]
+    tok_rows = place.shape[0]
+    feats = blocks[0].shape[1]
     gate = column(columns[...], EXPERTS_ROW + 1)
-    for k, grad in enumerate((g0, g1, g2, g3)):
-        start = pl.multiple_of((my_expert ^ k) * feats, LANES)
-        value = (gate * grad[...].astype(jnp.float32)).astype(jnp.bfloat16)
+    for index, grad in spread(meta[2], blocks, slice(0, tok_rows)):
+        start = pl.multiple_of(index * feats, LANES)
+        value = (gate * grad()).astype(jnp.bfloat16)
         expert_grad[:, pl.ds(start, feats)] = lax.dot_general(
             place[...], value, TN, preferred_element_type=jnp.float32
         ).astype(jnp.bfloat16)
 
 
-def resid_grad_kernel(meta, columns, g0, g1, g2, g3, r0, r1, r2, r3, resid_grad):
-    my_expert = meta[2]
-    tok_rows, feats = g0.shape
-    cols = columns[...]
-    weights = [column(cols, e) for e in range(EXPERTS_ROW)]
-    along = column(cols, EXPERTS_ROW)
-    for k, (grad, resid) in enumerate(((g0, r0), (g1, r1), (g2, r2), (g3, r3))):
-        start = pl.multiple_of((my_expert ^ k) * feats, LANES)
-        router = resid[tok_rows : tok_rows + ROW_TILE].astype(jnp.float32)
-        back = weights[0] * router[0:1]
-        for e in range(1, EXPERTS_ROW):
-            back = back + weights[e] * router[e : e + 1]
-        resid_grad[:, pl.ds(start, feats)] = (
-            grad[...].astype(jnp.float32) + back - along * resid[0:tok_rows].astype(jnp.float32)
-        ).astype(jnp.bfloat16)
+def project_kernel(meta, *refs):
+    weights, grads, resids = refs[0:5], refs[5:9], refs[9:13]
+    total, rows = refs[13:]
+    my_core, my_seq, my_expert = meta[0], meta[1], meta[2]
+    step = pl.program_id(0)
+    tok_rows, feats = grads[0].shape
+    width = weights[0].shape[1]
+    half = weights[3].shape[0]
+
+    @pl.when(step == 0)
+    def _():
+        total[...] = jnp.zeros_like(total)
+        for k in range(4):
+            rows[my_expert ^ k, 0:tok_rows] = grads[k][...]
+            rows[my_expert ^ k, tok_rows:] = resids[k][...]
+
+    columns = pl.ds(pl.multiple_of(step * width, LANES), width)
+    for k, weight in ((0, weights[0]), (1 + my_core, weights[1]), (2 - my_core, weights[2])):
+        total[...] += lax.dot_general(
+            rows[my_seq ^ k, :, columns], weight[...], NT, preferred_element_type=jnp.float32
+        )
+    for part, weight in ((my_core, weights[3]), (1 - my_core, weights[4])):
+        total[:, pl.ds(pl.multiple_of(part * half, LANES), half)] += lax.dot_general(
+            rows[my_seq ^ 3, :, columns], weight[...], NT, preferred_element_type=jnp.float32
+        )
 
 
 def stacked(matrix, heads):
@@ -432,68 +450,82 @@
 
 
 def backward_kernel(
-    meta, resid_grad, w0, w1, w2, w3, query, probs, attn_out, *rest
+    meta, columns, projected, router, query, probs, attn_out, v0, v1, v2, v3,
+    dquery, d0, d1, d2, d3,
 ):
-    key_refs, value_refs, (dquery, d0, d1, d2, d3, total) = rest[0:4], rest[4:8], rest[8:]
-    step = pl.program_id(0)
-    my_core = meta[0]
-    my_seq = meta[1]
     tok_rows = query.shape[0]
-    group = query.shape[1] // HEAD_DIM
-    width = w0.shape[1]
-    feats = width * pl.num_programs(0)
-
-    @pl.when(step == 0)
-    def _():
-        total[...] = jnp.zeros_like(total)
-
-    for k, weight in ((0, w0), (1 + my_core, w1), (2 - my_core, w2), (3, w3)):
-        start = pl.multiple_of((my_seq ^ k) * feats + step * width, LANES)
-        total[...] += lax.dot_general(
-            resid_grad[:, pl.ds(start, width)], weight[...], NT, preferred_element_type=jnp.float32
-        )
-
-    @pl.when(step == pl.num_programs(0) - 1)
-    def _():
-        score_scale = HEAD_DIM ** (-0.5)
-        attn_grad = total[...].astype(jnp.bfloat16)
-        grads = stacked(attn_grad, group)
-        heads = stacked(query[...], group)
-        mixed = stacked(attn_out[...], group)
-        keys = jnp.concatenate([ref[...] for ref in key_refs], axis=0)
-        values = jnp.concatenate([ref[...] for ref in value_refs], axis=0)
+    kv_count = v0.shape[1] // (2 * HEAD_DIM)
+    group = query.shape[1] // (kv_count * HEAD_DIM)
+    wide = group * HEAD_DIM
+    score_scale = HEAD_DIM ** (-0.5)
+    cols = columns[...]
+    weights = [column(cols, e) for e in range(EXPERTS_ROW)]
+    along = column(cols, EXPERTS_ROW)
+    for kv in range(kv_count):
+        here = slice(kv * wide, (kv + 1) * wide)
+        attn_grad = projected[0:tok_rows, here] - along * projected[tok_rows : 2 * tok_rows, here]
+        for e in range(EXPERTS_ROW):
+            attn_grad = attn_grad + weights[e] * projected[2 * tok_rows + e : 2 * tok_rows + e + 1, here]
+        grads = stacked(attn_grad.astype(jnp.bfloat16), group)
+        heads = stacked(query[:, here], group)
+        mixed = stacked(attn_out[:, here], group)
+        key_cols = slice(kv * HEAD_DIM, (kv + 1) * HEAD_DIM)
+        value_cols = slice((kv_count + kv) * HEAD_DIM, (kv_count + kv + 1) * HEAD_DIM)
+        keys = jnp.concatenate([v[:, key_cols] for v in (v0, v1, v2, v3)], axis=0)
+        values = jnp.concatenate([v[:, value_cols] for v in (v0, v1, v2, v3)], axis=0)
         delta = jnp.sum(grads.astype(jnp.float32) * mixed, axis=1, keepdims=True)
         dprobs = lax.dot_general(grads, values, NT, preferred_element_type=jnp.float32)
-        chances = probs[0]
+        chances = probs[kv]
         dscores = (chances * (dprobs - delta)).astype(jnp.bfloat16)
         dheads = (
             jnp.dot(dscores, keys, preferred_element_type=jnp.float32) * score_scale
         ).astype(jnp.bfloat16)
         for h in range(group):
-            dquery[:, h * HEAD_DIM : (h + 1) * HEAD_DIM] = dheads[h * tok_rows : (h + 1) * tok_rows]
+            at = (kv * group + h) * HEAD_DIM
+            dquery[:, at : at + HEAD_DIM] = dheads[h * tok_rows : (h + 1) * tok_rows]
         dkeys = lax.dot_general(dscores, heads, TN, preferred_element_type=jnp.float32) * score_scale
         dvalues = lax.dot_general(
             chances.astype(jnp.bfloat16), grads, TN, preferred_element_type=jnp.float32
         )
         for k, out in enumerate((d0, d1, d2, d3)):
-            here = slice(k * tok_rows, (k + 1) * tok_rows)
-            out[:, 0:HEAD_DIM] = dkeys[here].astype(out.dtype)
-            out[:, HEAD_DIM : 2 * HEAD_DIM] = dvalues[here].astype(out.dtype)
-
-
-def finish_kernel(meta, a0, a1, a2, a3, b0, b1, b2, b3, qa, qb, key_grad, value_grad, query_grad):
-    my_core = meta[0]
-    wide = qa.shape[1]
-    for half, parts, dquery in ((0, (a0, a1, a2, a3), qa), (1, (b0, b1, b2, b3), qb)):
-        total = parts[0][...]
-        for part in parts[1:]:
-            total = total + part[...].astype(jnp.float32)
-        total = total.astype(jnp.bfloat16)
-        head = my_core ^ half
-        start = pl.multiple_of(head * HEAD_DIM, LANES)
-        key_grad[:, pl.ds(start, HEAD_DIM)] = total[:, 0:HEAD_DIM]
-        value_grad[:, pl.ds(start, HEAD_DIM)] = total[:, HEAD_DIM : 2 * HEAD_DIM]
-        query_grad[:, pl.ds(pl.multiple_of(head * wide, LANES), wide)] = dquery[...]
+            part = slice(k * tok_rows, (k + 1) * tok_rows)
+            out[0:tok_rows, key_cols] = dkeys[part].astype(out.dtype)
+            out[0:tok_rows, value_cols] = dvalues[part].astype(out.dtype)
+    for out in (d1, d2, d3):
+        out[tok_rows:] = router[...]
+
+
+def router_pair_kernel(meta, mine, other, rows):
+    part = mine[...] + other[...]
+    width = rows.shape[1]
+    high = part.astype(jnp.bfloat16).astype(jnp.float32)
+    pieces = [
+        half[0:EXPERTS_ROW, at : at + width]
+        for half in (high, part - high)
+        for at in range(0, part.shape[1], width)
+    ]
+    rows[...] = jnp.concatenate(pieces, axis=0).astype(jnp.bfloat16)
+
+
+def finish_kernel(meta, router, own, t1, t2, t3, key_grad, value_grad, router_grad):
+    tok_rows, kv_width = key_grad.shape
+    total = own[...]
+    for part in (t1, t2, t3):
+        total = total + part[0:tok_rows].astype(jnp.float32)
+    total = total.astype(jnp.bfloat16)
+    key_grad[...] = total[:, 0:kv_width]
+    value_grad[...] = total[:, kv_width:]
+    sums = []
+    for rows in (router[...], t1[tok_rows:], t2[tok_rows:], t3[tok_rows:]):
+        rows = rows.astype(jnp.float32)
+        count = rows.shape[0] // 2
+        sums.append(rows[0:count] + rows[count:])
+    total = (sums[0] + sums[1]) + (sums[2] + sums[3])
+    width = total.shape[1]
+    for piece in range(total.shape[0] // EXPERTS_ROW):
+        router_grad[:, piece * width : (piece + 1) * width] = total[
+            piece * EXPERTS_ROW : (piece + 1) * EXPERTS_ROW
+        ]
 
 
 EXPERTS_ROW = 4
@@ -540,14 +572,11 @@
         return lax.ppermute(array, ("dp", "seq"), pairs)
 
     half_rows = o_weight.shape[0] // dp_n
+    router_rows = jnp.pad(router_weight.T, ((0, ROW_TILE - EXPERTS_ROW), (0, 0)))
     grads = over_expert(grad)
+    resids = over_expert(jnp.concatenate([resid, router_rows], axis=0))
+    pair = jnp.concatenate([key_in[0], value_in[0]], axis=1)
     weight_near = over_both(o_weight, lambda c: 1 + c)
-    pair = jnp.concatenate([key_in[0], value_in[0]], axis=1)
-    pairs = [pair] + over_seq(pair)
-    resid_rows = jnp.concatenate(
-        [resid, jnp.pad(router_weight.T, ((0, ROW_TILE - EXPERTS_ROW), (0, 0)))], axis=0
-    )
-    resids = over_expert(resid_rows)
     router_pad = jnp.pad(router_weight, ((0, 0), (0, LANES - router_weight.shape[1])))
     rows, place, saved_tok = call(
         prepare_kernel,
@@ -559,29 +588,16 @@
             ((tok_rows, width), bf16),
         ),
     )
-    weight_near, grads[1:], pairs[1:], resids[1], rows, place, saved_tok = lax.optimization_barrier(
-        (weight_near, grads[1:], pairs[1:], resids[1], rows, place, saved_tok)
-    )
+    grads[1:], resids[1], weight_near, rows, place, saved_tok, pair = lax.optimization_barrier(
+        (grads[1:], resids[1], weight_near, rows, place, saved_tok, pair)
+    )
+    (terms,) = call(
+        gate_grad_kernel, meta, (route, rows, saved_tok, *grads), (((8, tok_rows), f32),)
+    )
+    pairs = [pair] + over_seq(pair)
     weight_far = partner(weight_near, "dp", dp_n, 1)
     across = lax.dynamic_slice_in_dim(weight_near, core * half_rows, half_rows, axis=0)
     across_mine = over_both(across, lambda c: 2 - c)
-
-    (terms,) = call(
-        gate_grad_kernel, meta, (route, rows, saved_tok, *grads), (((8, tok_rows), f32),)
-    )
-    total_tokens = dp_n * seq_n * tok_rows
-    columns, router_part = call(
-        lambda meta, *refs: router_kernel(meta, total_tokens, *refs),
-        meta,
-        (route, *over_expert(terms), resid),
-        (((tok_rows, LANES), f32), ((8, feats), f32)),
-    )
-    (expert_grad,) = call(
-        expert_grad_kernel, meta, (columns, place, *grads), (((capacity, width), bf16),)
-    )
-    router_pair = router_part + partner(router_part, "dp", dp_n, 1)
-    r1, r2, r3 = over_seq(router_pair)
-    router_sum = (router_pair + r1) + (r2 + r3)
 
     kv_width = key_in.shape[2]
     kv_count = kv_width // HEAD_DIM
@@ -595,77 +611,64 @@
             (query.shape, f32),
         ),
     )
-    across_mine, weight_far, resids[2:], columns, expert_grad, probs, attn_out = (
-        lax.optimization_barrier(
-            (across_mine, weight_far, resids[2:], columns, expert_grad, probs, attn_out)
-        )
+    terms, across_mine, weight_far, resids[2:], probs, attn_out = lax.optimization_barrier(
+        (terms, across_mine, weight_far, resids[2:], probs, attn_out)
     )
     across_other = partner(across_mine, "dp", dp_n, 1)
-    router_grad = router_sum[0 : router_weight.shape[1]].T
-    (resid_grad,) = call(
-        resid_grad_kernel,
+    total_tokens = dp_n * seq_n * tok_rows
+    columns, router_part = call(
+        lambda meta, *refs: router_kernel(meta, total_tokens, *refs),
         meta,
-        (columns, *grads, *resids),
-        (((tok_rows, width), bf16),),
-    )
-
-    def backward(half, weights):
-        steps = 4
-        wide = group * HEAD_DIM
-        head = lambda i, m: m[0] ^ half
-        in_specs = [
-            whole(resid_grad.shape),
-            pl.BlockSpec((half_rows, feats // steps), lambda i, m: (head(i, m), i)),
-        ]
-        in_specs += [pl.BlockSpec((half_rows, feats // steps), lambda i, m: (head(i, m), i))] * 2
-        in_specs += [pl.BlockSpec((half_rows, feats // steps), lambda i, m: (0, i))]
-        in_specs += [
-            pl.BlockSpec((tok_rows, wide), lambda i, m: (0, head(i, m))),
-            pl.BlockSpec((1, group * tok_rows, seq_n * tok_rows), lambda i, m: (head(i, m), 0, 0)),
-            pl.BlockSpec((tok_rows, wide), lambda i, m: (0, head(i, m))),
-        ]
-        in_specs += [pl.BlockSpec((tok_rows, HEAD_DIM), lambda i, m: (0, head(i, m)))] * 4
-        in_specs += [
-            pl.BlockSpec((tok_rows, HEAD_DIM), lambda i, m: (0, kv_count + head(i, m)))
-        ] * 4
-        term = (tok_rows, 2 * HEAD_DIM)
-        shapes = [jax.ShapeDtypeStruct((tok_rows, wide), bf16), jax.ShapeDtypeStruct(term, f32)]
-        shapes += [jax.ShapeDtypeStruct(term, bf16)] * 3
-        return pl.pallas_call(
-            backward_kernel,
-            out_shape=shapes,
-            grid_spec=pltpu.PrefetchScalarGridSpec(
-                num_scalar_prefetch=1,
-                grid=(steps,),
-                in_specs=in_specs,
-                out_specs=[whole(s.shape) for s in shapes],
-                scratch_shapes=[pltpu.VMEM((tok_rows, wide), f32)],
-            ),
-            compiler_params=params(),
-        )(meta, resid_grad, o_weight, *weights, query, probs, attn_out, *pairs, *pairs)
-
-    def send_back(terms):
-        return [
-            lax.ppermute(
-                terms[k - 1], "seq", [(i, i ^ k) for i in range(seq_n) if i > i ^ k]
-            )
-            for k in range(1, seq_n)
-        ]
-
-    dquery_a, own_a, *terms_a = backward(0, (weight_near, weight_far, across_mine))
-    back_a = send_back(terms_a)
-    dquery_b, own_b, *terms_b = backward(1, (weight_near, weight_far, across_other))
-    back_b = send_back(terms_b)
-    key_grad, value_grad, query_grad = call(
+        (route, *over_expert(terms), resid),
+        (((tok_rows, LANES), f32), ((8, feats), f32)),
+    )
+    term_width = 2 * kv_width
+    (router_term,) = call(
+        router_pair_kernel,
+        meta,
+        (router_part, partner(router_part, "dp", dp_n, 1)),
+        (((2 * EXPERTS_ROW * feats // term_width, term_width), bf16),),
+    )
+    steps = 4
+    model_rows = o_weight.shape[0]
+    blocks = [(model_rows, feats // steps)] * 3 + [(half_rows, feats // steps)] * 2
+    token_parts = (*grads, *resids)
+    (projected,) = pl.pallas_call(
+        project_kernel,
+        out_shape=[jax.ShapeDtypeStruct((2 * tok_rows + ROW_TILE, model_rows), f32)],
+        grid_spec=pltpu.PrefetchScalarGridSpec(
+            num_scalar_prefetch=1,
+            grid=(steps,),
+            in_specs=[pl.BlockSpec(b, lambda i, m: (0, i)) for b in blocks]
+            + [pl.BlockSpec(memory_space=pltpu.VMEM)] * len(token_parts),
+            out_specs=[whole((2 * tok_rows + ROW_TILE, model_rows))],
+            scratch_shapes=[pltpu.VMEM((expert_n, 2 * tok_rows + ROW_TILE, feats), bf16)],
+        ),
+        compiler_params=params(),
+    )(meta, o_weight, weight_near, weight_far, across_mine, across_other, *token_parts)
+    term = (tok_rows + router_term.shape[0], term_width)
+    query_grad, own, *key_terms = call(
+        backward_kernel,
+        meta,
+        (columns, projected, router_term, query, probs, attn_out, *pairs),
+        ((query.shape, bf16), ((tok_rows, term_width), f32), *(((term, bf16),) * 3)),
+    )
+    back = [partner(key_terms[k - 1], "seq", seq_n, k) for k in range(1, seq_n)]
+    columns, own = lax.optimization_barrier((columns, own))
+    (expert_grad,) = call(
+        expert_grad_kernel, meta, (columns, place, *grads), (((capacity, width), bf16),)
+    )
+    key_grad, value_grad, router_grad = call(
         finish_kernel,
         meta,
-        (own_a, *back_a, own_b, *back_b, dquery_a, dquery_b),
+        (router_term, own, *back),
         (
             ((tok_rows, kv_width), bf16),
             ((tok_rows, kv_width), bf16),
-            ((tok_rows, query.shape[1]), bf16),
+            ((EXPERTS_ROW, feats), f32),
         ),
     )
+    router_grad = router_grad.T
     return (query_grad[None], key_grad[None], value_grad[None], router_grad, expert_grad[None])
 
 

time: 130 us -> 91.8 us (0.71)
  the two profiles are of different devices: /device:TPU:8 before, /device:TPU:0 now
where the time goes in v3:
time: 91.8 us; the launch traced here: 91.5 us
  waiting for transfers between devices  40.1 us (44%)
  starting transfers between devices  25.4 us (28%)
  Pallas kernels  18.3 us (20%)
  local copies, waits for them, and re-layouts  5.2 us (6%)
  other arithmetic  1.73 us (2%)
    ppermute x18, waiting for transfers between devices, partner(): return lax.ppermute(array, axis, [(i, i ^ distance) for i in range(count)])  40.1 us
    ppermute x18, starting transfers between devices, partner(): return lax.ppermute(array, axis, [(i, i ^ distance) for i in range(count)])  21.8 us
    pallas_call x8, Pallas kernels, call(): pl.pallas_call(kernel, out_shape=shapes, in_specs=[pl.BlockSpec(memory_sp...  12.4 us
    pallas_call x1, Pallas kernels, local_fast(): pl.pallas_call(project_kernel, out_shape=[jax.ShapeDtypeStruct((2 * tok_r...  5.9 us
    unnamed x24, local copies, waits for them, and re-layouts  5.07 us
    ppermute x2, starting transfers between devices, over_both(): return lax.ppermute(array, ('dp', 'seq'), pairs)  3.58 us
  transfers between devices with their start and end apart: 20, of which 12 were waited for; matrix products, arithmetic and copies ran while one was open for 4% of the time, Pallas kernels for 9%

profile of v3, /device:TPU:0, one launch (start us, length us, event | category | flops | bytes accessed | tf_op | source)
XLA Modules:
  0.0 91.5 jit_solution(5132203554815376170)
XLA Ops:
  0.6 3.0 %collective-permute-start.4 = (bf16[1024,1024]{1,0:T(8,128)(2,1)}, bf16[1024,1024]{1,0:T(8,128)(2,1)S(1)}, u32[]{:S(2)}, u32[]{:S(2)}) collective-permute-start(bf16[1024,1024]{1,0:T(8,128)(2,1)} %refs_0_.1), channel_id=1, source_target_pairs={{0,4},{4,0},{8,12},{12,8},{16,24},{20,28},{24,16},{28,20},{1,5},{5... | collective-permute-start | bytes 6291464 | tf_op jit(solution)/shard_map/ppermute | solution.py:572
  4.6 1.6 %collective-permute-start.3 = (bf16[144,1024]{1,0:T(8,128)(2,1)S(1)}, bf16[144,1024]{1,0:T(8,128)(2,1)}, u32[]{:S(2)}, u32[]{:S(2)}) collective-permute-start(bf16[144,1024]{1,0:T(8,128)(2,1)S(1)} %fusion.1.refs_9_), channel_id=1, source_target_pairs={{0,1},{1,0},{2,3},{3,2},{4,5},{5,4},{6,7},{7,6},{8,9},{9,8},{10,11... | collective-permute-start | bytes 884744 | tf_op jit(solution)/shard_map/ppermute | solution.py:266
  6.3 2.5 %collective-permute-start.2 = (bf16[128,1024]{1,0:T(8,128)(2,1)}, bf16[128,1024]{1,0:T(8,128)(2,1)S(1)}, u32[]{:S(2)}, u32[]{:S(2)}) collective-permute-start(bf16[128,1024]{1,0:T(8,128)(2,1)} %bitcast.16), channel_id=1, source_target_pairs={{0,3},{1,2},{2,1},{3,0},{4,7},{5,6},{6,5},{7,4},{8,11},{9,10},{10,... | collective-permute-start | bytes 786440 | tf_op jit(solution)/shard_map/ppermute | solution.py:266
  8.9 1.8 %collective-permute-start = (bf16[128,1024]{1,0:T(8,128)(2,1)}, bf16[128,1024]{1,0:T(8,128)(2,1)S(1)}, u32[]{:S(2)}, u32[]{:S(2)}) collective-permute-start(bf16[128,1024]{1,0:T(8,128)(2,1)} %bitcast.18), channel_id=1, source_target_pairs={{0,1},{1,0},{2,3},{3,2},{4,5},{5,4},{6,7},{7,6},{8,9},{9,8},{10,11... | collective-permute-start | bytes 786440 | tf_op jit(solution)/shard_map/ppermute | solution.py:266
  13.5 1.2 %copy-done.5 = bf16[1,128,4096]{2,1,0:T(8,128)(2,1)S(1)} copy-done((bf16[1,128,4096]{2,1,0:T(8,128)(2,1)S(1)}, bf16[1,128,4096]{2,1,0:T(8,128)(2,1)}, u32[]{:S(2)}) %copy-start.5) | copy-done | bytes 1048600
  14.7 1.3 %shard_map.128 = (f32[8,128]{1,0:T(8,128)S(1)}, bf16[128,128]{1,0:T(8,128)(2,1)S(1)}, bf16[128,4096]{1,0:T(8,128)(2,1)S(1)}) custom-call(s32[3]{0:T(128)S(1)} %pad_add_fusion.meta, s32[128,2]{1,0:T(8,128)S(1)} %bitcast.26, bf16[1024,128]{1,0:T(8,128)(2,1)S(1)} %pad.9.router_pad, bf16[128,1024]{1,0:T(8,128)(2,1)S(1)} %bitcast.23, bf16[128,4096]{1,0:T(8,128)(2,1)S(1)} %bitcast.25), custom_call_target="tpu_custom_call" | custom-call | tf_op jit(solution)/shard_map/pallas_call | solution.py:537
  17.7 4.7 %collective-permute-done.2.refs_3_.refs_8_ = bf16[128,1024]{1,0:T(8,128)(2,1)S(1)} collective-permute-done((bf16[128,1024]{1,0:T(8,128)(2,1)}, bf16[128,1024]{1,0:T(8,128)(2,1)S(1)}, u32[]{:S(2)}, u32[]{:S(2)}) %collective-permute-start.2) | collective-permute-done | bytes 262176 | tf_op jit(solution)/shard_map/ppermute | solution.py:266
  22.4 9.3 %collective-permute-done.1.refs_2_.refs_7_ = bf16[128,1024]{1,0:T(8,128)(2,1)S(1)} collective-permute-done((bf16[128,1024]{1,0:T(8,128)(2,1)}, bf16[128,1024]{1,0:T(8,128)(2,1)S(1)}, u32[]{:S(2)}, u32[]{:S(2)}) %collective-permute-start.1) | collective-permute-done | bytes 262176 | tf_op jit(solution)/shard_map/ppermute | solution.py:266
  32.7 2.3 %collective-permute-start.11 = (bf16[128,512]{1,0:T(8,128)(2,1)S(1)}, bf16[128,512]{1,0:T(8,128)(2,1)S(1)}, u32[]{:S(2)}, u32[]{:S(2)}) collective-permute-start(bf16[128,512]{1,0:T(8,128)(2,1)S(1)} %copy-done.4), channel_id=1, source_target_pairs={{0,12},{4,8},{8,4},{12,0},{1,13},{5,9},{9,5},{13,1},{2,14},{6,10},... | collective-permute-start | bytes 393224 | tf_op jit(solution)/shard_map/ppermute | solution.py:266
  35.0 2.6 %collective-permute-start.8 = (bf16[144,1024]{1,0:T(8,128)(2,1)S(1)}, bf16[144,1024]{1,0:T(8,128)(2,1)S(1)}, u32[]{:S(2)}, u32[]{:S(2)}) collective-permute-start(bf16[144,1024]{1,0:T(8,128)(2,1)S(1)} %fusion.1.refs_9_), channel_id=1, source_target_pairs={{0,3},{1,2},{2,1},{3,0},{4,7},{5,6},{6,5},{7,4},{8,11},{9,10},{10,... | collective-permute-start | bytes 884744 | tf_op jit(solution)/shard_map/ppermute | solution.py:266
  37.6 2.4 %collective-permute-done.11.v3 = bf16[128,512]{1,0:T(8,128)(2,1)S(1)} collective-permute-done((bf16[128,512]{1,0:T(8,128)(2,1)S(1)}, bf16[128,512]{1,0:T(8,128)(2,1)S(1)}, u32[]{:S(2)}, u32[]{:S(2)}) %collective-permute-start.11) | collective-permute-done | bytes 131104 | tf_op jit(solution)/shard_map/ppermute | solution.py:266
  40.0 1.3 %collective-permute-start.10 = (bf16[128,512]{1,0:T(8,128)(2,1)S(1)}, bf16[128,512]{1,0:T(8,128)(2,1)S(1)}, u32[]{:S(2)}, u32[]{:S(2)}) collective-permute-start(bf16[128,512]{1,0:T(8,128)(2,1)S(1)} %copy-done.4), channel_id=1, source_target_pairs={{0,8},{4,12},{8,0},{12,4},{1,9},{5,13},{9,1},{13,5},{2,10},{6,14},... | collective-permute-start | bytes 393224 | tf_op jit(solution)/shard_map/ppermute | solution.py:266
  41.4 9.6 %collective-permute-done.10.v2 = bf16[128,512]{1,0:T(8,128)(2,1)S(1)} collective-permute-done((bf16[128,512]{1,0:T(8,128)(2,1)S(1)}, bf16[128,512]{1,0:T(8,128)(2,1)S(1)}, u32[]{:S(2)}, u32[]{:S(2)}) %collective-permute-start.10) | collective-permute-done | bytes 131104 | tf_op jit(solution)/shard_map/ppermute | solution.py:266
  51.0 1.5 %collective-permute-start.9 = (bf16[128,512]{1,0:T(8,128)(2,1)S(1)}, bf16[128,512]{1,0:T(8,128)(2,1)S(1)}, u32[]{:S(2)}, u32[]{:S(2)}) collective-permute-start(bf16[128,512]{1,0:T(8,128)(2,1)S(1)} %copy-done.4), channel_id=1, source_target_pairs={{0,4},{4,0},{8,12},{12,8},{1,5},{5,1},{9,13},{13,9},{2,6},{6,2},{1... | collective-permute-start | bytes 393224 | tf_op jit(solution)/shard_map/ppermute | solution.py:266
  53.5 3.1 %collective-permute-done.9.v1 = bf16[128,512]{1,0:T(8,128)(2,1)S(1)} collective-permute-done((bf16[128,512]{1,0:T(8,128)(2,1)S(1)}, bf16[128,512]{1,0:T(8,128)(2,1)S(1)}, u32[]{:S(2)}, u32[]{:S(2)}) %collective-permute-start.9) | collective-permute-done | bytes 131104 | tf_op jit(solution)/shard_map/ppermute | solution.py:266
  56.6 2.4 %shard_map.130 = (f32[2,512,512]{2,1,0:T(8,128)S(1)}, f32[128,1024]{1,0:T(8,128)S(1)}) custom-call(s32[3]{0:T(128)S(1)} %pad_add_fusion.meta, bf16[128,1024]{1,0:T(8,128)(2,1)S(1)} %bitcast.29, bf16[128,512]{1,0:T(8,128)(2,1)S(1)} %copy-done.4, bf16[128,512]{1,0:T(8,128)(2,1)S(1)} %collective-permute-done.9.v1, ...), custom_call_target="tpu_custom_call" | custom-call | tf_op jit(solution)/shard_map/pallas_call | solution.py:537
  59.0 2.6 %collective-permute-done.7.refs_11_ = bf16[144,1024]{1,0:T(8,128)(2,1)S(1)} collective-permute-done((bf16[144,1024]{1,0:T(8,128)(2,1)S(1)}, bf16[144,1024]{1,0:T(8,128)(2,1)S(1)}, u32[]{:S(2)}, u32[]{:S(2)}) %collective-permute-start.7) | collective-permute-done | bytes 294944 | tf_op jit(solution)/shard_map/ppermute | solution.py:266
  61.6 2.5 %collective-permute-start.14 = (f32[8,128]{1,0:T(8,128)S(1)}, f32[8,128]{1,0:T(8,128)S(1)}, u32[]{:S(2)}, u32[]{:S(2)}) collective-permute-start(f32[8,128]{1,0:T(8,128)S(1)} %shard_map.129.refs_1_), channel_id=1, source_target_pairs={{0,3},{1,2},{2,1},{3,0},{4,7},{5,6},{6,5},{7,4},{8,11},{9,10},{10,... | collective-permute-start | bytes 12296 | tf_op jit(solution)/shard_map/ppermute | solution.py:266
  64.1 2.0 %collective-permute-start.12 = (f32[8,128]{1,0:T(8,128)S(1)}, f32[8,128]{1,0:T(8,128)S(1)}, u32[]{:S(2)}, u32[]{:S(2)}) collective-permute-start(f32[8,128]{1,0:T(8,128)S(1)} %shard_map.129.refs_1_), channel_id=1, source_target_pairs={{0,1},{1,0},{2,3},{3,2},{4,5},{5,4},{6,7},{7,6},{8,9},{9,8},{10,11... | collective-permute-start | bytes 12296 | tf_op jit(solution)/shard_map/ppermute | solution.py:266
  66.1 1.0 %collective-permute-done.14.refs_4_ = f32[8,128]{1,0:T(8,128)S(1)} collective-permute-done((f32[8,128]{1,0:T(8,128)S(1)}, f32[8,128]{1,0:T(8,128)S(1)}, u32[]{:S(2)}, u32[]{:S(2)}) %collective-permute-start.14) | collective-permute-done | bytes 4128 | tf_op jit(solution)/shard_map/ppermute | solution.py:266
  67.1 1.5 %collective-permute-done.13.refs_3_ = f32[8,128]{1,0:T(8,128)S(1)} collective-permute-done((f32[8,128]{1,0:T(8,128)S(1)}, f32[8,128]{1,0:T(8,128)S(1)}, u32[]{:S(2)}, u32[]{:S(2)}) %collective-permute-start.13) | collective-permute-done | bytes 4128 | tf_op jit(solution)/shard_map/ppermute | solution.py:266
  68.6 1.2 %shard_map.131 = (f32[128,128]{1,0:T(8,128)S(1)}, f32[8,1024]{1,0:T(8,128)S(1)}) custom-call(s32[3]{0:T(128)S(1)} %pad_add_fusion.meta, s32[128,2]{1,0:T(8,128)S(1)} %bitcast.28, f32[8,128]{1,0:T(8,128)S(1)} %shard_map.129.refs_1_, f32[8,128]{1,0:T(8,128)S(1)} %collective-permute-done.12.refs_2_, f32[8,128]{1,0:T(8,128)S(1)} %collective-permute-done.13.refs_3_, ...), custom_call_target="tpu_custom_call" | custom-call | tf_op jit(solution)/shard_map/pallas_call | solution.py:537
  69.9 1.2 %collective-permute-done.16.other = f32[8,1024]{1,0:T(8,128)S(1)} collective-permute-done((f32[8,1024]{1,0:T(8,128)S(1)}, f32[8,1024]{1,0:T(8,128)S(1)}, u32[]{:S(2)}, u32[]{:S(2)}) %collective-permute-start.16) | collective-permute-done | bytes 32800 | tf_op jit(solution)/shard_map/ppermute | solution.py:266
  71.7 5.9 %shard_map.132.projected = f32[272,1024]{1,0:T(8,128)S(1)} custom-call(s32[3]{0:T(128)S(1)} %pad_add_fusion.meta, bf16[1024,1024]{1,0:T(8,128)(2,1)S(1)} %copy-done.3, bf16[1024,1024]{1,0:T(8,128)(2,1)S(1)} %collective-permute-done.4.refs_1_, bf16[1024,1024]{1,0:T(8,128)(2,1)} %collective-permute-done.6.refs_2_, ...), custom_call_target="tpu_custom_call" | custom-call | tf_op jit(solution)/shard_map/pallas_call | solution.py:636
  77.6 2.6 %shard_map.134 = (bf16[128,1024]{1,0:T(8,128)(2,1)}, f32[128,512]{1,0:T(8,128)S(1)}, bf16[144,512]{1,0:T(8,128)(2,1)S(1)}, bf16[144,512]{1,0:T(8,128)(2,1)S(1)}, bf16[144,512]{1,0:T(8,128)(2,1)S(1)}) custom-call(s32[3]{0:T(128)S(1)} %pad_add_fusion.meta, f32[128,128]{1,0:T(8,128)S(1)} %get-tuple-element.69.columns, f32[272,1024]{1,0:T(8,128)S(1)} %shard_map.132.projected, ...), custom_call_target="tpu_custom_call" | custom-call | tf_op jit(solution)/shard_map/pallas_call | solution.py:537
  80.2 1.0 %collective-permute-start.17 = (bf16[144,512]{1,0:T(8,128)(2,1)S(1)}, bf16[144,512]{1,0:T(8,128)(2,1)S(1)}, u32[]{:S(2)}, u32[]{:S(2)}) collective-permute-start(bf16[144,512]{1,0:T(8,128)(2,1)S(1)} %get-tuple-element.63), channel_id=1, source_target_pairs={{0,4},{4,0},{8,12},{12,8},{1,5},{5,1},{9,13},{13,9},{2,6},{6,2},{1... | collective-permute-start | bytes 442376 | tf_op jit(solution)/shard_map/ppermute | solution.py:266
  81.2 1.5 %collective-permute-start.18 = (bf16[144,512]{1,0:T(8,128)(2,1)S(1)}, bf16[144,512]{1,0:T(8,128)(2,1)S(1)}, u32[]{:S(2)}, u32[]{:S(2)}) collective-permute-start(bf16[144,512]{1,0:T(8,128)(2,1)S(1)} %get-tuple-element.64), channel_id=1, source_target_pairs={{0,8},{4,12},{8,0},{12,4},{1,9},{5,13},{9,1},{13,5},{2,10},{6,14},... | collective-permute-start | bytes 442376 | tf_op jit(solution)/shard_map/ppermute | solution.py:266
  83.7 2.0 %shard_map.136 = bf16[128,4096]{1,0:T(8,128)(2,1)} custom-call(s32[3]{0:T(128)S(1)} %pad_add_fusion.meta, f32[128,128]{1,0:T(8,128)S(1)} %get-tuple-element.69.columns, bf16[128,128]{1,0:T(8,128)(2,1)S(1)} %get-tuple-element.70.place, bf16[128,1024]{1,0:T(8,128)(2,1)S(1)} %bitcast.21, bf16[128,1024]{1,0:T(8,128)(2,1)S(1)} %collective-permute-done.refs_1_.refs_6_, ...), custom_call_target="tpu_custom_call" | custom-call | tf_op jit(solution)/shard_map/pallas_call | solution.py:537
  85.7 1.2 %collective-permute-done.17.t1 = bf16[144,512]{1,0:T(8,128)(2,1)S(1)} collective-permute-done((bf16[144,512]{1,0:T(8,128)(2,1)S(1)}, bf16[144,512]{1,0:T(8,128)(2,1)S(1)}, u32[]{:S(2)}, u32[]{:S(2)}) %collective-permute-start.17) | collective-permute-done | bytes 147488 | tf_op jit(solution)/shard_map/ppermute | solution.py:266
  86.9 2.2 %collective-permute-done.18.t2 = bf16[144,512]{1,0:T(8,128)(2,1)S(1)} collective-permute-done((bf16[144,512]{1,0:T(8,128)(2,1)S(1)}, bf16[144,512]{1,0:T(8,128)(2,1)S(1)}, u32[]{:S(2)}, u32[]{:S(2)}) %collective-permute-start.18) | collective-permute-done | bytes 147488 | tf_op jit(solution)/shard_map/ppermute | solution.py:266
  89.0 1.2 %collective-permute-done.19.t3 = bf16[144,512]{1,0:T(8,128)(2,1)S(1)} collective-permute-done((bf16[144,512]{1,0:T(8,128)(2,1)S(1)}, bf16[144,512]{1,0:T(8,128)(2,1)S(1)}, u32[]{:S(2)}, u32[]{:S(2)}) %collective-permute-start.19) | collective-permute-done | bytes 147488 | tf_op jit(solution)/shard_map/ppermute | solution.py:266
  90.2 1.2 %shard_map.135 = (bf16[128,256]{1,0:T(8,128)(2,1)}, bf16[128,256]{1,0:T(8,128)(2,1)}, f32[4,1024]{1,0:T(4,128)}) custom-call(s32[3]{0:T(128)S(1)} %pad_add_fusion.meta, bf16[16,512]{1,0:T(8,128)(2,1)S(1)} %shard_map.133.router, f32[128,512]{1,0:T(8,128)S(1)} %get-tuple-element.62.own, bf16[144,512]{1,0:T(8,128)(2,1)S(1)} %collective-permute-done.17.t1, ...), custom_call_target="tpu_custom_call" | custom-call | tf_op jit(solution)/shard_map/pallas_call | solution.py:537
  (46 shorter events, 9.0 us)
Async XLA Ops:
  0.6 31.1 %collective-permute-start.4 = (bf16[1024,1024]{1,0:T(8,128)(2,1)}, bf16[1024,1024]{1,0:T(8,128)(2,1)S(1)}, u32[]{:S(2)}, u32[]{:S(2)}) collective-permute-start(bf16[1024,1024]{1,0:T(8,128)(2,1)} %refs_0_.1), channel_id=1, source_target_pairs={{0,4},{4,0},{8,12},{12,8},{16,24},{20,28},{24,16},{28,20},{1,5},{5... | collective-permute-start | bytes 6291464 | tf_op jit(solution)/shard_map/ppermute | solution.py:572
  4.6 27.1 %collective-permute-start.3 = (bf16[144,1024]{1,0:T(8,128)(2,1)S(1)}, bf16[144,1024]{1,0:T(8,128)(2,1)}, u32[]{:S(2)}, u32[]{:S(2)}) collective-permute-start(bf16[144,1024]{1,0:T(8,128)(2,1)S(1)} %fusion.1.refs_9_), channel_id=1, source_target_pairs={{0,1},{1,0},{2,3},{3,2},{4,5},{5,4},{6,7},{7,6},{8,9},{9,8},{10,11... | collective-permute-start | bytes 884744 | tf_op jit(solution)/shard_map/ppermute | solution.py:266
  6.3 16.1 %collective-permute-start.2 = (bf16[128,1024]{1,0:T(8,128)(2,1)}, bf16[128,1024]{1,0:T(8,128)(2,1)S(1)}, u32[]{:S(2)}, u32[]{:S(2)}) collective-permute-start(bf16[128,1024]{1,0:T(8,128)(2,1)} %bitcast.16), channel_id=1, source_target_pairs={{0,3},{1,2},{2,1},{3,0},{4,7},{5,6},{6,5},{7,4},{8,11},{9,10},{10,... | collective-permute-start | bytes 786440 | tf_op jit(solution)/shard_map/ppermute | solution.py:266
  8.7 22.9 %collective-permute-start.1 = (bf16[128,1024]{1,0:T(8,128)(2,1)}, bf16[128,1024]{1,0:T(8,128)(2,1)S(1)}, u32[]{:S(2)}, u32[]{:S(2)}) collective-permute-start(bf16[128,1024]{1,0:T(8,128)(2,1)} %bitcast.17), channel_id=1, source_target_pairs={{0,2},{1,3},{2,0},{3,1},{4,6},{5,7},{6,4},{7,5},{8,10},{9,11},{10,... | collective-permute-start | bytes 786440 | tf_op jit(solution)/shard_map/ppermute | solution.py:266
  8.9 22.8 %collective-permute-start = (bf16[128,1024]{1,0:T(8,128)(2,1)}, bf16[128,1024]{1,0:T(8,128)(2,1)S(1)}, u32[]{:S(2)}, u32[]{:S(2)}) collective-permute-start(bf16[128,1024]{1,0:T(8,128)(2,1)} %bitcast.18), channel_id=1, source_target_pairs={{0,1},{1,0},{2,3},{3,2},{4,5},{5,4},{6,7},{7,6},{8,9},{9,8},{10,11... | collective-permute-start | bytes 786440 | tf_op jit(solution)/shard_map/ppermute | solution.py:266
  12.4 4.7 %copy-start.9 = (bf16[1,128,256]{2,1,0:T(8,128)(2,1)S(1)}, bf16[1,128,256]{2,1,0:T(8,128)(2,1)}, u32[]{:S(2)}) copy-start(bf16[1,128,256]{2,1,0:T(8,128)(2,1)} %param.11) | copy-start | bytes 196612
  12.4 4.7 %copy-start.10 = (bf16[1,128,256]{2,1,0:T(8,128)(2,1)S(1)}, bf16[1,128,256]{2,1,0:T(8,128)(2,1)}, u32[]{:S(2)}) copy-start(bf16[1,128,256]{2,1,0:T(8,128)(2,1)} %param.10) | copy-start | bytes 196612
  12.4 40.1 %copy-start = (bf16[1,128,1024]{2,1,0:T(8,128)(2,1)S(1)}, bf16[1,128,1024]{2,1,0:T(8,128)(2,1)}, u32[]{:S(2)}) copy-start(bf16[1,128,1024]{2,1,0:T(8,128)(2,1)} %param.13) | copy-start | bytes 786436
  12.5 1.0 %copy-start.1 = (bf16[1,128,1024]{2,1,0:T(8,128)(2,1)S(1)}, bf16[1,128,1024]{2,1,0:T(8,128)(2,1)}, u32[]{:S(2)}) copy-start(bf16[1,128,1024]{2,1,0:T(8,128)(2,1)} %param.12) | copy-start | bytes 786436
  13.5 1.2 %copy-start.5 = (bf16[1,128,4096]{2,1,0:T(8,128)(2,1)S(1)}, bf16[1,128,4096]{2,1,0:T(8,128)(2,1)}, u32[]{:S(2)}) copy-start(bf16[1,128,4096]{2,1,0:T(8,128)(2,1)} %param.17) | copy-start | bytes 3145732
  16.0 1.0 %copy-start.6 = (bf16[128,4096]{1,0:T(8,128)(2,1)}, bf16[128,4096]{1,0:T(8,128)(2,1)S(1)}, u32[]{:S(2)}) copy-start(bf16[128,4096]{1,0:T(8,128)(2,1)S(1)} %get-tuple-element.42.saved_tok) | copy-start | bytes 3145732
  31.7 29.9 %collective-permute-start.6 = (bf16[1024,1024]{1,0:T(8,128)(2,1)S(1)}, bf16[1024,1024]{1,0:T(8,128)(2,1)}, u32[]{:S(2)}, u32[]{:S(2)}) collective-permute-start(bf16[1024,1024]{1,0:T(8,128)(2,1)S(1)} %collective-permute-done.4.refs_1_), channel_id=1, source_target_pairs={{0,16},{16,0},{1,17},{17,1},{2,18},{18,2},{3,19},{19,3},{4,20},{20... | collective-permute-start | bytes 6291464 | tf_op jit(solution)/shard_map/ppermute | solution.py:266
  31.8 0.9 copy-start.4
  31.8 20.7 %copy-start.7 = (bf16[128,4096]{1,0:T(8,128)(2,1)S(1)}, bf16[128,4096]{1,0:T(8,128)(2,1)}, u32[]{:S(2)}) copy-start(bf16[128,4096]{1,0:T(8,128)(2,1)} %copy-done.6) | copy-start | bytes 3145732
  31.8 24.8 %copy-start.8 = (bf16[1,128,1024]{2,1,0:T(8,128)(2,1)S(1)}, bf16[1,128,1024]{2,1,0:T(8,128)(2,1)}, u32[]{:S(2)}) copy-start(bf16[1,128,1024]{2,1,0:T(8,128)(2,1)} %param.9) | copy-start | bytes 786436
  31.8 36.8 %copy-start.2 = (bf16[1,128,1024]{2,1,0:T(8,128)(2,1)S(1)}, bf16[1,128,1024]{2,1,0:T(8,128)(2,1)}, u32[]{:S(2)}) copy-start(bf16[1,128,1024]{2,1,0:T(8,128)(2,1)} %param.12) | copy-start | bytes 786436
  31.9 39.7 %copy-start.3 = (bf16[1024,1024]{1,0:T(8,128)(2,1)S(1)}, bf16[1024,1024]{1,0:T(8,128)(2,1)}, u32[]{:S(2)}) copy-start(bf16[1024,1024]{1,0:T(8,128)(2,1)} %refs_0_.1) | copy-start | bytes 6291460
  31.9 29.7 %collective-permute-start.5 = (bf16[512,1024]{1,0:T(8,128)(2,1)S(1)}, bf16[512,1024]{1,0:T(8,128)(2,1)S(1)}, u32[]{:S(2)}, u32[]{:S(2)}) collective-permute-start(bf16[512,1024]{1,0:T(8,128)(2,1)S(1)} %constant_dynamic-slice_fusion), channel_id=1, source_target_pairs={{0,8},{4,12},{8,0},{12,4},{16,20},{20,16},{24,28},{28,24},{1,9},{5... | collective-permute-start | bytes 3145736 | tf_op jit(solution)/shard_map/ppermute | solution.py:572
  32.7 7.3 %collective-permute-start.11 = (bf16[128,512]{1,0:T(8,128)(2,1)S(1)}, bf16[128,512]{1,0:T(8,128)(2,1)S(1)}, u32[]{:S(2)}, u32[]{:S(2)}) collective-permute-start(bf16[128,512]{1,0:T(8,128)(2,1)S(1)} %copy-done.4), channel_id=1, source_target_pairs={{0,12},{4,8},{8,4},{12,0},{1,13},{5,9},{9,5},{13,1},{2,14},{6,10},... | collective-permute-start | bytes 393224 | tf_op jit(solution)/shard_map/ppermute | solution.py:266
  35.0 24.0 %collective-permute-start.8 = (bf16[144,1024]{1,0:T(8,128)(2,1)S(1)}, bf16[144,1024]{1,0:T(8,128)(2,1)S(1)}, u32[]{:S(2)}, u32[]{:S(2)}) collective-permute-start(bf16[144,1024]{1,0:T(8,128)(2,1)S(1)} %fusion.1.refs_9_), channel_id=1, source_target_pairs={{0,3},{1,2},{2,1},{3,0},{4,7},{5,6},{6,5},{7,4},{8,11},{9,10},{10,... | collective-permute-start | bytes 884744 | tf_op jit(solution)/shard_map/ppermute | solution.py:266
  37.6 24.0 %collective-permute-start.7 = (bf16[144,1024]{1,0:T(8,128)(2,1)S(1)}, bf16[144,1024]{1,0:T(8,128)(2,1)S(1)}, u32[]{:S(2)}, u32[]{:S(2)}) collective-permute-start(bf16[144,1024]{1,0:T(8,128)(2,1)S(1)} %fusion.1.refs_9_), channel_id=1, source_target_pairs={{0,2},{1,3},{2,0},{3,1},{4,6},{5,7},{6,4},{7,5},{8,10},{9,11},{10,... | collective-permute-start | bytes 884744 | tf_op jit(solution)/shard_map/ppermute | solution.py:266
  40.0 11.0 %collective-permute-start.10 = (bf16[128,512]{1,0:T(8,128)(2,1)S(1)}, bf16[128,512]{1,0:T(8,128)(2,1)S(1)}, u32[]{:S(2)}, u32[]{:S(2)}) collective-permute-start(bf16[128,512]{1,0:T(8,128)(2,1)S(1)} %copy-done.4), channel_id=1, source_target_pairs={{0,8},{4,12},{8,0},{12,4},{1,9},{5,13},{9,1},{13,5},{2,10},{6,14},... | collective-permute-start | bytes 393224 | tf_op jit(solution)/shard_map/ppermute | solution.py:266
  51.0 5.6 %collective-permute-start.9 = (bf16[128,512]{1,0:T(8,128)(2,1)S(1)}, bf16[128,512]{1,0:T(8,128)(2,1)S(1)}, u32[]{:S(2)}, u32[]{:S(2)}) collective-permute-start(bf16[128,512]{1,0:T(8,128)(2,1)S(1)} %copy-done.4), channel_id=1, source_target_pairs={{0,4},{4,0},{8,12},{12,8},{1,5},{5,1},{9,13},{13,9},{2,6},{6,2},{1... | collective-permute-start | bytes 393224 | tf_op jit(solution)/shard_map/ppermute | solution.py:266
  61.6 10.1 %collective-permute-start.15 = (bf16[512,1024]{1,0:T(8,128)(2,1)S(1)}, bf16[512,1024]{1,0:T(8,128)(2,1)S(1)}, u32[]{:S(2)}, u32[]{:S(2)}) collective-permute-start(bf16[512,1024]{1,0:T(8,128)(2,1)S(1)} %collective-permute-done.5.refs_3_), channel_id=1, source_target_pairs={{0,16},{16,0},{1,17},{17,1},{2,18},{18,2},{3,19},{19,3},{4,20},{20... | collective-permute-start | bytes 3145736 | tf_op jit(solution)/shard_map/ppermute | solution.py:266
  61.6 5.5 %collective-permute-start.14 = (f32[8,128]{1,0:T(8,128)S(1)}, f32[8,128]{1,0:T(8,128)S(1)}, u32[]{:S(2)}, u32[]{:S(2)}) collective-permute-start(f32[8,128]{1,0:T(8,128)S(1)} %shard_map.129.refs_1_), channel_id=1, source_target_pairs={{0,3},{1,2},{2,1},{3,0},{4,7},{5,6},{6,5},{7,4},{8,11},{9,10},{10,... | collective-permute-start | bytes 12296 | tf_op jit(solution)/shard_map/ppermute | solution.py:266
  64.1 4.5 %collective-permute-start.13 = (f32[8,128]{1,0:T(8,128)S(1)}, f32[8,128]{1,0:T(8,128)S(1)}, u32[]{:S(2)}, u32[]{:S(2)}) collective-permute-start(f32[8,128]{1,0:T(8,128)S(1)} %shard_map.129.refs_1_), channel_id=1, source_target_pairs={{0,2},{1,3},{2,0},{3,1},{4,6},{5,7},{6,4},{7,5},{8,10},{9,11},{10,... | collective-permute-start | bytes 12296 | tf_op jit(solution)/shard_map/ppermute | solution.py:266
  64.1 4.5 %collective-permute-start.12 = (f32[8,128]{1,0:T(8,128)S(1)}, f32[8,128]{1,0:T(8,128)S(1)}, u32[]{:S(2)}, u32[]{:S(2)}) collective-permute-start(f32[8,128]{1,0:T(8,128)S(1)} %shard_map.129.refs_1_), channel_id=1, source_target_pairs={{0,1},{1,0},{2,3},{3,2},{4,5},{5,4},{6,7},{7,6},{8,9},{9,8},{10,11... | collective-permute-start | bytes 12296 | tf_op jit(solution)/shard_map/ppermute | solution.py:266
  69.9 1.2 %collective-permute-start.16 = (f32[8,1024]{1,0:T(8,128)S(1)}, f32[8,1024]{1,0:T(8,128)S(1)}, u32[]{:S(2)}, u32[]{:S(2)}) collective-permute-start(f32[8,1024]{1,0:T(8,128)S(1)} %get-tuple-element.57.mine), channel_id=1, source_target_pairs={{0,16},{16,0},{1,17},{17,1},{2,18},{18,2},{3,19},{19,3},{4,20},{20... | collective-permute-start | bytes 98312 | tf_op jit(solution)/shard_map/ppermute | solution.py:266
  80.2 6.7 %collective-permute-start.17 = (bf16[144,512]{1,0:T(8,128)(2,1)S(1)}, bf16[144,512]{1,0:T(8,128)(2,1)S(1)}, u32[]{:S(2)}, u32[]{:S(2)}) collective-permute-start(bf16[144,512]{1,0:T(8,128)(2,1)S(1)} %get-tuple-element.63), channel_id=1, source_target_pairs={{0,4},{4,0},{8,12},{12,8},{1,5},{5,1},{9,13},{13,9},{2,6},{6,2},{1... | collective-permute-start | bytes 442376 | tf_op jit(solution)/shard_map/ppermute | solution.py:266
  81.2 7.8 %collective-permute-start.18 = (bf16[144,512]{1,0:T(8,128)(2,1)S(1)}, bf16[144,512]{1,0:T(8,128)(2,1)S(1)}, u32[]{:S(2)}, u32[]{:S(2)}) collective-permute-start(bf16[144,512]{1,0:T(8,128)(2,1)S(1)} %get-tuple-element.64), channel_id=1, source_target_pairs={{0,8},{4,12},{8,0},{12,4},{1,9},{5,13},{9,1},{13,5},{2,10},{6,14},... | collective-permute-start | bytes 442376 | tf_op jit(solution)/shard_map/ppermute | solution.py:266
  82.7 7.5 %collective-permute-start.19 = (bf16[144,512]{1,0:T(8,128)(2,1)S(1)}, bf16[144,512]{1,0:T(8,128)(2,1)S(1)}, u32[]{:S(2)}, u32[]{:S(2)}) collective-permute-start(bf16[144,512]{1,0:T(8,128)(2,1)S(1)} %get-tuple-element.65), channel_id=1, source_target_pairs={{0,12},{4,8},{8,4},{12,0},{1,13},{5,9},{9,5},{13,1},{2,14},{6,10},... | collective-permute-start | bytes 442376 | tf_op jit(solution)/shard_map/ppermute | solution.py:266

commit v4 on v3

--- a/solution.py
+++ b/solution.py
@@ -415,9 +415,15 @@
     )
 
 
-def forward_kernel(meta, query, v0, v1, v2, v3, probs, attn_out):
+def four(pair, pair_x, pair_y):
+    count = pair.shape[0]
+    return pair[...], pair_x[...], pair_y[0:count], pair_y[count:]
+
+
+def forward_kernel(meta, query, pair, pair_x, pair_y, probs, attn_out):
     my_seq = meta[1]
     tok_rows = query.shape[0]
+    v0, v1, v2, v3 = four(pair, pair_x, pair_y)
     kv_count = v0.shape[1] // (2 * HEAD_DIM)
     group = query.shape[1] // (kv_count * HEAD_DIM)
     rows = group * tok_rows
@@ -450,10 +456,11 @@
 
 
 def backward_kernel(
-    meta, columns, projected, router, query, probs, attn_out, v0, v1, v2, v3,
-    dquery, d0, d1, d2, d3,
+    meta, columns, projected, router_a, router_b, query, probs, attn_out, pair, pair_x,
+    pair_y, dquery, router, d0, d1, d2, d3,
 ):
     tok_rows = query.shape[0]
+    v0, v1, v2, v3 = four(pair, pair_x, pair_y)
     kv_count = v0.shape[1] // (2 * HEAD_DIM)
     group = query.shape[1] // (kv_count * HEAD_DIM)
     wide = group * HEAD_DIM
@@ -491,20 +498,20 @@
             part = slice(k * tok_rows, (k + 1) * tok_rows)
             out[0:tok_rows, key_cols] = dkeys[part].astype(out.dtype)
             out[0:tok_rows, value_cols] = dvalues[part].astype(out.dtype)
+    halves = paired(router_a[...] + router_b[...], router.shape[1])
+    router[...] = halves
     for out in (d1, d2, d3):
-        out[tok_rows:] = router[...]
-
-
-def router_pair_kernel(meta, mine, other, rows):
-    part = mine[...] + other[...]
-    width = rows.shape[1]
+        out[tok_rows:] = halves
+
+
+def paired(part, width):
     high = part.astype(jnp.bfloat16).astype(jnp.float32)
     pieces = [
         half[0:EXPERTS_ROW, at : at + width]
         for half in (high, part - high)
         for at in range(0, part.shape[1], width)
     ]
-    rows[...] = jnp.concatenate(pieces, axis=0).astype(jnp.bfloat16)
+    return jnp.concatenate(pieces, axis=0).astype(jnp.bfloat16)
 
 
 def finish_kernel(meta, router, own, t1, t2, t3, key_grad, value_grad, router_grad):
@@ -574,8 +581,8 @@
     half_rows = o_weight.shape[0] // dp_n
     router_rows = jnp.pad(router_weight.T, ((0, ROW_TILE - EXPERTS_ROW), (0, 0)))
     grads = over_expert(grad)
-    resids = over_expert(jnp.concatenate([resid, router_rows], axis=0))
     pair = jnp.concatenate([key_in[0], value_in[0]], axis=1)
+    pair_x = partner(pair, "seq", seq_n, 1)
     weight_near = over_both(o_weight, lambda c: 1 + c)
     router_pad = jnp.pad(router_weight, ((0, 0), (0, LANES - router_weight.shape[1])))
     rows, place, saved_tok = call(
@@ -588,14 +595,16 @@
             ((tok_rows, width), bf16),
         ),
     )
-    grads[1:], resids[1], weight_near, rows, place, saved_tok, pair = lax.optimization_barrier(
-        (grads[1:], resids[1], weight_near, rows, place, saved_tok, pair)
-    )
+    own_rows = jnp.concatenate([resid, router_rows], axis=0)
+    grads[1:], weight_near, rows, place, saved_tok, pair_x, own_rows = lax.optimization_barrier(
+        (grads[1:], weight_near, rows, place, saved_tok, pair_x, own_rows)
+    )
+    resids = over_expert(own_rows)
     (terms,) = call(
         gate_grad_kernel, meta, (route, rows, saved_tok, *grads), (((8, tok_rows), f32),)
     )
-    pairs = [pair] + over_seq(pair)
-    weight_far = partner(weight_near, "dp", dp_n, 1)
+    pair_y = partner(jnp.concatenate([pair, pair_x], axis=0), "seq", seq_n, 2)
+    pairs = (pair, pair_x, pair_y)
     across = lax.dynamic_slice_in_dim(weight_near, core * half_rows, half_rows, axis=0)
     across_mine = over_both(across, lambda c: 2 - c)
 
@@ -611,47 +620,54 @@
             (query.shape, f32),
         ),
     )
-    terms, across_mine, weight_far, resids[2:], probs, attn_out = lax.optimization_barrier(
-        (terms, across_mine, weight_far, resids[2:], probs, attn_out)
-    )
+    steps = 4
+    model_rows = o_weight.shape[0]
+    all_rows = 2 * tok_rows + ROW_TILE
+    terms, across_mine, resids[1:], probs, attn_out, weight_near = lax.optimization_barrier(
+        (terms, across_mine, resids[1:], probs, attn_out, weight_near)
+    )
+    weight_far = partner(weight_near, "dp", dp_n, 1)
     across_other = partner(across_mine, "dp", dp_n, 1)
+    weights = (o_weight, weight_near, weight_far, across_mine, across_other)
+    token_parts = (*grads, *resids)
+    projected = pl.pallas_call(
+        project_kernel,
+        out_shape=jax.ShapeDtypeStruct((all_rows, model_rows), f32),
+        grid_spec=pltpu.PrefetchScalarGridSpec(
+            num_scalar_prefetch=1,
+            grid=(steps,),
+            in_specs=[
+                pl.BlockSpec((w.shape[0], feats // steps), lambda i, m: (0, i)) for w in weights
+            ]
+            + [pl.BlockSpec(memory_space=pltpu.VMEM)] * len(token_parts),
+            out_specs=whole((all_rows, model_rows)),
+            scratch_shapes=[pltpu.VMEM((expert_n, all_rows, feats), bf16)],
+        ),
+        compiler_params=params(),
+    )(meta, *weights, *token_parts)
+    all_terms = over_expert(terms)
+    projected, all_terms[1:] = lax.optimization_barrier((projected, all_terms[1:]))
     total_tokens = dp_n * seq_n * tok_rows
     columns, router_part = call(
         lambda meta, *refs: router_kernel(meta, total_tokens, *refs),
         meta,
-        (route, *over_expert(terms), resid),
+        (route, *all_terms, resid),
         (((tok_rows, LANES), f32), ((8, feats), f32)),
     )
     term_width = 2 * kv_width
-    (router_term,) = call(
-        router_pair_kernel,
-        meta,
-        (router_part, partner(router_part, "dp", dp_n, 1)),
-        (((2 * EXPERTS_ROW * feats // term_width, term_width), bf16),),
-    )
-    steps = 4
-    model_rows = o_weight.shape[0]
-    blocks = [(model_rows, feats // steps)] * 3 + [(half_rows, feats // steps)] * 2
-    token_parts = (*grads, *resids)
-    (projected,) = pl.pallas_call(
-        project_kernel,
-        out_shape=[jax.ShapeDtypeStruct((2 * tok_rows + ROW_TILE, model_rows), f32)],
-        grid_spec=pltpu.PrefetchScalarGridSpec(
-            num_scalar_prefetch=1,
-            grid=(steps,),
-            in_specs=[pl.BlockSpec(b, lambda i, m: (0, i)) for b in blocks]
-            + [pl.BlockSpec(memory_space=pltpu.VMEM)] * len(token_parts),
-            out_specs=[whole((2 * tok_rows + ROW_TILE, model_rows))],
-            scratch_shapes=[pltpu.VMEM((expert_n, 2 * tok_rows + ROW_TILE, feats), bf16)],
-        ),
-        compiler_params=params(),
-    )(meta, o_weight, weight_near, weight_far, across_mine, across_other, *token_parts)
-    term = (tok_rows + router_term.shape[0], term_width)
-    query_grad, own, *key_terms = call(
+    router_rows = 2 * EXPERTS_ROW * feats // term_width
+    term = (tok_rows + router_rows, term_width)
+    router_other = partner(router_part, "dp", dp_n, 1)
+    query_grad, router_term, own, *key_terms = call(
         backward_kernel,
         meta,
-        (columns, projected, router_term, query, probs, attn_out, *pairs),
-        ((query.shape, bf16), ((tok_rows, term_width), f32), *(((term, bf16),) * 3)),
+        (columns, projected, router_part, router_other, query, probs, attn_out, *pairs),
+        (
+            (query.shape, bf16),
+            ((router_rows, term_width), bf16),
+            ((tok_rows, term_width), f32),
+            *(((term, bf16),) * 3),
+        ),
     )
     back = [partner(key_terms[k - 1], "seq", seq_n, k) for k in range(1, seq_n)]
     columns, own = lax.optimization_barrier((columns, own))

time: 91.8 us -> 85.5 us (0.931)
  the two profiles are of different devices: /device:TPU:0 before, /device:TPU:8 now
where the time goes in v4:
time: 85.5 us; the launch traced here: 84.8 us
  waiting for transfers between devices  40.6 us (47%)
  starting transfers between devices  19.6 us (23%)
  Pallas kernels  17.1 us (20%)
  local copies, waits for them, and re-layouts  5.65 us (7%)
  other arithmetic  1 us (1%)
    ppermute x17, waiting for transfers between devices, partner(): return lax.ppermute(array, axis, [(i, i ^ distance) for i in range(count)])  40.6 us
    ppermute x17, starting transfers between devices, partner(): return lax.ppermute(array, axis, [(i, i ^ distance) for i in range(count)])  15.5 us
    pallas_call x7, Pallas kernels, call(): pl.pallas_call(kernel, out_shape=shapes, in_specs=[pl.BlockSpec(memory_sp...  11.9 us
    pallas_call x1, Pallas kernels, local_fast(): pl.pallas_call(project_kernel, out_shape=jax.ShapeDtypeStruct((all_rows,...  5.19 us
    unnamed x20, local copies, waits for them, and re-layouts  4.57 us
    ppermute x2, starting transfers between devices, over_both(): return lax.ppermute(array, ('dp', 'seq'), pairs)  4.16 us
  transfers between devices with their start and end apart: 19, of which 8 were waited for; matrix products, arithmetic and copies ran while one was open for 5% of the time, Pallas kernels for 14%

profile of v4, /device:TPU:8, one launch (start us, length us, event | category | flops | bytes accessed | tf_op | source)
XLA Modules:
  0.0 84.8 jit_solution(16620345430525189563)
XLA Ops:
  0.6 1.6 %collective-permute-start.3 = (bf16[1024,1024]{1,0:T(8,128)(2,1)}, bf16[1024,1024]{1,0:T(8,128)(2,1)S(1)}, u32[]{:S(2)}, u32[]{:S(2)}) collective-permute-start(bf16[1024,1024]{1,0:T(8,128)(2,1)} %refs_0_.1), channel_id=1, source_target_pairs={{0,4},{4,0},{8,12},{12,8},{16,24},{20,28},{24,16},{28,20},{1,5},{5... | collective-permute-start | bytes 6291464 | tf_op jit(solution)/shard_map/ppermute | solution.py:579
  2.6 2.6 %collective-permute-start.1 = (bf16[128,1024]{1,0:T(8,128)(2,1)}, bf16[128,1024]{1,0:T(8,128)(2,1)S(1)}, u32[]{:S(2)}, u32[]{:S(2)}) collective-permute-start(bf16[128,1024]{1,0:T(8,128)(2,1)} %bitcast.17), channel_id=1, source_target_pairs={{0,2},{1,3},{2,0},{3,1},{4,6},{5,7},{6,4},{7,5},{8,10},{9,11},{10,... | collective-permute-start | bytes 786440 | tf_op jit(solution)/shard_map/ppermute | solution.py:266
  5.2 0.5 collective-permute-start.2
  5.7 0.9 %pad_maximum_fusion.1.pair = bf16[128,512]{1,0:T(8,128)(2,1)S(1)} fusion(bf16[128,256]{1,0:T(8,128)(2,1)} %bitcast.32, bf16[128,256]{1,0:T(8,128)(2,1)} %bitcast.34), kind=kLoop, calls=%fused_computation.4 | loop fusion | flops 262144 | bytes 262144 | tf_op jit(solution)/shard_map/concatenate | solution.py:584
  6.6 0.6 collective-permute-start.4
  7.2 0.8 copy.14
  8.0 1.6 %copy.15 = bf16[1024,4]{1,0:T(8,128)(2,1)} copy(bf16[1024,4]{0,1:T(4,128)(2,1)} %param.15) | data formatting | bytes 16384 | tf_op args[6]
  9.6 1.0 %pad.8.router_pad = bf16[1024,128]{1,0:T(8,128)(2,1)S(1)} pad(bf16[1024,4]{1,0:T(8,128)(2,1)} %copy.15, bf16[]{:T(256)} %constant.17.clone.1), padding=0_0x0_124 | pad | bytes 270338 | tf_op jit(solution)/shard_map/jit(_pad)/pad | solution.py:587
  10.6 0.9 %copy-done.1 = bf16[1,128,1024]{2,1,0:T(8,128)(2,1)S(1)} copy-done((bf16[1,128,1024]{2,1,0:T(8,128)(2,1)S(1)}, bf16[1,128,1024]{2,1,0:T(8,128)(2,1)}, u32[]{:S(2)}) %copy-start.1) | copy-done | bytes 262168
  11.6 1.2 %copy-done.4 = bf16[1,128,4096]{2,1,0:T(8,128)(2,1)S(1)} copy-done((bf16[1,128,4096]{2,1,0:T(8,128)(2,1)S(1)}, bf16[1,128,4096]{2,1,0:T(8,128)(2,1)}, u32[]{:S(2)}) %copy-start.4) | copy-done | bytes 1048600
  12.8 1.3 %shard_map.128 = (f32[8,128]{1,0:T(8,128)S(1)}, bf16[128,128]{1,0:T(8,128)(2,1)S(1)}, bf16[128,4096]{1,0:T(8,128)(2,1)S(1)}) custom-call(s32[3]{0:T(128)S(1)} %pad_add_fusion.meta, s32[128,2]{1,0:T(8,128)S(1)} %bitcast.26, bf16[1024,128]{1,0:T(8,128)(2,1)S(1)} %pad.8.router_pad, bf16[128,1024]{1,0:T(8,128)(2,1)S(1)} %bitcast.22, bf16[128,4096]{1,0:T(8,128)(2,1)S(1)} %bitcast.25), custom_call_target="tpu_custom_call" | custom-call | tf_op jit(solution)/shard_map/pallas_call | solution.py:544
  14.2 15.6 %collective-permute-done.4.pair_x = bf16[128,512]{1,0:T(8,128)(2,1)S(1)} collective-permute-done((bf16[128,512]{1,0:T(8,128)(2,1)S(1)}, bf16[128,512]{1,0:T(8,128)(2,1)S(1)}, u32[]{:S(2)}, u32[]{:S(2)}) %collective-permute-start.4) | collective-permute-done | bytes 131104 | tf_op jit(solution)/shard_map/ppermute | solution.py:266
  29.9 2.6 %collective-permute-start.5 = (bf16[512,1024]{1,0:T(8,128)(2,1)S(1)}, bf16[512,1024]{1,0:T(8,128)(2,1)S(1)}, u32[]{:S(2)}, u32[]{:S(2)}) collective-permute-start(bf16[512,1024]{1,0:T(8,128)(2,1)S(1)} %constant_dynamic-slice_fusion), channel_id=1, source_target_pairs={{0,8},{4,12},{8,0},{12,4},{16,20},{20,16},{24,28},{28,24},{1,9},{5... | collective-permute-start | bytes 3145736 | tf_op jit(solution)/shard_map/ppermute | solution.py:579
  32.9 2.6 %collective-permute-start.7 = (bf16[144,1024]{1,0:T(8,128)(2,1)S(1)}, bf16[144,1024]{1,0:T(8,128)(2,1)S(1)}, u32[]{:S(2)}, u32[]{:S(2)}) collective-permute-start(bf16[144,1024]{1,0:T(8,128)(2,1)S(1)} %fusion.1.refs_9_), channel_id=1, source_target_pairs={{0,2},{1,3},{2,0},{3,1},{4,6},{5,7},{6,4},{7,5},{8,10},{9,11},{10,... | collective-permute-start | bytes 884744 | tf_op jit(solution)/shard_map/ppermute | solution.py:266
  35.5 0.5 collective-permute-start.8
  36.3 1.0 %shard_map.129.refs_1_ = f32[8,128]{1,0:T(8,128)S(1)} custom-call(s32[3]{0:T(128)S(1)} %pad_add_fusion.meta, s32[128,2]{1,0:T(8,128)S(1)} %bitcast.27, f32[8,128]{1,0:T(8,128)S(1)} %get-tuple-element.47.rows, bf16[128,4096]{1,0:T(8,128)(2,1)S(1)} %get-tuple-element.48.saved_tok, bf16[128,1024]{1,0:T(8,128)(2,1)S(1)} %bitcast.19, ...), custom_call_target="tpu_custom_call" | custom-call | tf_op jit(solution)/shard_map/pallas_call | solution.py:544
  37.2 13.7 %collective-permute-done.9.pair_y = bf16[256,512]{1,0:T(8,128)(2,1)S(1)} collective-permute-done((bf16[256,512]{1,0:T(8,128)(2,1)S(1)}, bf16[256,512]{1,0:T(8,128)(2,1)S(1)}, u32[]{:S(2)}, u32[]{:S(2)}) %collective-permute-start.9) | collective-permute-done | bytes 262176 | tf_op jit(solution)/shard_map/ppermute | solution.py:266
  50.9 2.4 %shard_map.130 = (f32[2,512,512]{2,1,0:T(8,128)S(1)}, f32[128,1024]{1,0:T(8,128)S(1)}) custom-call(s32[3]{0:T(128)S(1)} %pad_add_fusion.meta, bf16[128,1024]{1,0:T(8,128)(2,1)S(1)} %bitcast.29, bf16[128,512]{1,0:T(8,128)(2,1)S(1)} %pad_maximum_fusion.1.pair, bf16[128,512]{1,0:T(8,128)(2,1)S(1)} %collective-permute-done.4.pair_x, ...), custom_call_target="tpu_custom_call" | custom-call | tf_op jit(solution)/shard_map/pallas_call | solution.py:544
  53.7 4.5 %collective-permute-done.8.refs_12_ = bf16[144,1024]{1,0:T(8,128)(2,1)S(1)} collective-permute-done((bf16[144,1024]{1,0:T(8,128)(2,1)S(1)}, bf16[144,1024]{1,0:T(8,128)(2,1)S(1)}, u32[]{:S(2)}, u32[]{:S(2)}) %collective-permute-start.8) | collective-permute-done | bytes 294944 | tf_op jit(solution)/shard_map/ppermute | solution.py:266
  58.2 0.5 collective-permute-start.11
  58.8 3.0 %collective-permute-start.13 = (f32[8,128]{1,0:T(8,128)S(1)}, f32[8,128]{1,0:T(8,128)S(1)}, u32[]{:S(2)}, u32[]{:S(2)}) collective-permute-start(f32[8,128]{1,0:T(8,128)S(1)} %shard_map.129.refs_1_), channel_id=1, source_target_pairs={{0,2},{1,3},{2,0},{3,1},{4,6},{5,7},{6,4},{7,5},{8,10},{9,11},{10,... | collective-permute-start | bytes 12296 | tf_op jit(solution)/shard_map/ppermute | solution.py:266
  61.8 0.5 collective-permute-start.14
  62.2 1.7 %collective-permute-done.11.refs_4_ = bf16[512,1024]{1,0:T(8,128)(2,1)S(1)} collective-permute-done((bf16[512,1024]{1,0:T(8,128)(2,1)S(1)}, bf16[512,1024]{1,0:T(8,128)(2,1)S(1)}, u32[]{:S(2)}, u32[]{:S(2)}) %collective-permute-start.11) | collective-permute-done | bytes 1048608 | tf_op jit(solution)/shard_map/ppermute | solution.py:266
  63.9 5.2 %shard_map.131.projected = f32[272,1024]{1,0:T(8,128)S(1)} custom-call(s32[3]{0:T(128)S(1)} %pad_add_fusion.meta, bf16[1024,1024]{1,0:T(8,128)(2,1)S(1)} %copy-done.3, bf16[1024,1024]{1,0:T(8,128)(2,1)S(1)} %collective-permute-done.3.refs_1_, bf16[1024,1024]{1,0:T(8,128)(2,1)S(1)} %collective-permute-done.10.refs_2_, ...), custom_call_target="tpu_custom_call" | custom-call | tf_op jit(solution)/shard_map/pallas_call | solution.py:633
  69.2 1.3 %shard_map.132 = (f32[128,128]{1,0:T(8,128)S(1)}, f32[8,1024]{1,0:T(8,128)S(1)}) custom-call(s32[3]{0:T(128)S(1)} %pad_add_fusion.meta, s32[128,2]{1,0:T(8,128)S(1)} %bitcast.28, f32[8,128]{1,0:T(8,128)S(1)} %shard_map.129.refs_1_, f32[8,128]{1,0:T(8,128)S(1)} %collective-permute-done.12.refs_2_, f32[8,128]{1,0:T(8,128)S(1)} %collective-permute-done.13.refs_3_, ...), custom_call_target="tpu_custom_call" | custom-call | tf_op jit(solution)/shard_map/pallas_call | solution.py:544
  70.6 1.1 %collective-permute-done.15.router_b = f32[8,1024]{1,0:T(8,128)S(1)} collective-permute-done((f32[8,1024]{1,0:T(8,128)S(1)}, f32[8,1024]{1,0:T(8,128)S(1)}, u32[]{:S(2)}, u32[]{:S(2)}) %collective-permute-start.15) | collective-permute-done | bytes 32800 | tf_op jit(solution)/shard_map/ppermute | solution.py:266
  71.6 2.7 %shard_map.133 = (bf16[128,1024]{1,0:T(8,128)(2,1)}, bf16[16,512]{1,0:T(8,128)(2,1)S(1)}, f32[128,512]{1,0:T(8,128)S(1)}, bf16[144,512]{1,0:T(8,128)(2,1)S(1)}, ...) custom-call(s32[3]{0:T(128)S(1)} %pad_add_fusion.meta, f32[128,128]{1,0:T(8,128)S(1)} %get-tuple-element.81.columns, ...), custom_call_target="tpu_custom_call" | custom-call | tf_op jit(solution)/shard_map/pallas_call | solution.py:544
  74.7 3.1 %collective-permute-start.18 = (bf16[144,512]{1,0:T(8,128)(2,1)S(1)}, bf16[144,512]{1,0:T(8,128)(2,1)S(1)}, u32[]{:S(2)}, u32[]{:S(2)}) collective-permute-start(bf16[144,512]{1,0:T(8,128)(2,1)S(1)} %get-tuple-element.77), channel_id=1, source_target_pairs={{0,12},{4,8},{8,4},{12,0},{1,13},{5,9},{9,5},{13,1},{2,14},{6,10},... | collective-permute-start | bytes 442376 | tf_op jit(solution)/shard_map/ppermute | solution.py:266
  77.9 2.0 %shard_map.135 = bf16[128,4096]{1,0:T(8,128)(2,1)} custom-call(s32[3]{0:T(128)S(1)} %pad_add_fusion.meta, f32[128,128]{1,0:T(8,128)S(1)} %get-tuple-element.81.columns, bf16[128,128]{1,0:T(8,128)(2,1)S(1)} %get-tuple-element.82.place, bf16[128,1024]{1,0:T(8,128)(2,1)S(1)} %bitcast.21, bf16[128,1024]{1,0:T(8,128)(2,1)S(1)} %collective-permute-done.refs_1_.refs_6_, ...), custom_call_target="tpu_custom_call" | custom-call | tf_op jit(solution)/shard_map/pallas_call | solution.py:544
  79.9 1.2 %collective-permute-done.16.t1 = bf16[144,512]{1,0:T(8,128)(2,1)S(1)} collective-permute-done((bf16[144,512]{1,0:T(8,128)(2,1)S(1)}, bf16[144,512]{1,0:T(8,128)(2,1)S(1)}, u32[]{:S(2)}, u32[]{:S(2)}) %collective-permute-start.16) | collective-permute-done | bytes 147488 | tf_op jit(solution)/shard_map/ppermute | solution.py:266
  81.1 2.5 %collective-permute-done.17.t2 = bf16[144,512]{1,0:T(8,128)(2,1)S(1)} collective-permute-done((bf16[144,512]{1,0:T(8,128)(2,1)S(1)}, bf16[144,512]{1,0:T(8,128)(2,1)S(1)}, u32[]{:S(2)}, u32[]{:S(2)}) %collective-permute-start.17) | collective-permute-done | bytes 147488 | tf_op jit(solution)/shard_map/ppermute | solution.py:266
  83.5 1.2 %shard_map.134 = (bf16[128,256]{1,0:T(8,128)(2,1)}, bf16[128,256]{1,0:T(8,128)(2,1)}, f32[4,1024]{1,0:T(4,128)}) custom-call(s32[3]{0:T(128)S(1)} %pad_add_fusion.meta, bf16[16,512]{1,0:T(8,128)(2,1)S(1)} %get-tuple-element.72.router, f32[128,512]{1,0:T(8,128)S(1)} %get-tuple-element.74.own, bf16[144,512]{1,0:T(8,128)(2,1)S(1)} %collective-permute-done.16.t1, ...), custom_call_target="tpu_custom_call" | custom-call | tf_op jit(solution)/shard_map/pallas_call | solution.py:544
  (40 shorter events, 2.4 us)
Async XLA Ops:
  0.6 13.5 %copy-start.8 = (bf16[1024,4]{0,1:T(4,128)(2,1)S(1)}, bf16[1024,4]{0,1:T(4,128)(2,1)}, u32[]{:S(2)}) copy-start(bf16[1024,4]{0,1:T(4,128)(2,1)} %param.15) | copy-start | bytes 24580
  0.6 29.1 %collective-permute-start.3 = (bf16[1024,1024]{1,0:T(8,128)(2,1)}, bf16[1024,1024]{1,0:T(8,128)(2,1)S(1)}, u32[]{:S(2)}, u32[]{:S(2)}) collective-permute-start(bf16[1024,1024]{1,0:T(8,128)(2,1)} %refs_0_.1), channel_id=1, source_target_pairs={{0,4},{4,0},{8,12},{12,8},{16,24},{20,28},{24,16},{28,20},{1,5},{5... | collective-permute-start | bytes 6291464 | tf_op jit(solution)/shard_map/ppermute | solution.py:579
  2.2 27.6 %collective-permute-start = (bf16[128,1024]{1,0:T(8,128)(2,1)}, bf16[128,1024]{1,0:T(8,128)(2,1)S(1)}, u32[]{:S(2)}, u32[]{:S(2)}) collective-permute-start(bf16[128,1024]{1,0:T(8,128)(2,1)} %bitcast.16), channel_id=1, source_target_pairs={{0,1},{1,0},{2,3},{3,2},{4,5},{5,4},{6,7},{7,6},{8,9},{9,8},{10,11... | collective-permute-start | bytes 786440 | tf_op jit(solution)/shard_map/ppermute | solution.py:266
  2.6 27.1 %collective-permute-start.1 = (bf16[128,1024]{1,0:T(8,128)(2,1)}, bf16[128,1024]{1,0:T(8,128)(2,1)S(1)}, u32[]{:S(2)}, u32[]{:S(2)}) collective-permute-start(bf16[128,1024]{1,0:T(8,128)(2,1)} %bitcast.17), channel_id=1, source_target_pairs={{0,2},{1,3},{2,0},{3,1},{4,6},{5,7},{6,4},{7,5},{8,10},{9,11},{10,... | collective-permute-start | bytes 786440 | tf_op jit(solution)/shard_map/ppermute | solution.py:266
  5.2 24.5 %collective-permute-start.2 = (bf16[128,1024]{1,0:T(8,128)(2,1)}, bf16[128,1024]{1,0:T(8,128)(2,1)S(1)}, u32[]{:S(2)}, u32[]{:S(2)}) collective-permute-start(bf16[128,1024]{1,0:T(8,128)(2,1)} %bitcast.18), channel_id=1, source_target_pairs={{0,3},{1,2},{2,1},{3,0},{4,7},{5,6},{6,5},{7,4},{8,11},{9,10},{10,... | collective-permute-start | bytes 786440 | tf_op jit(solution)/shard_map/ppermute | solution.py:266
  6.6 23.2 %collective-permute-start.4 = (bf16[128,512]{1,0:T(8,128)(2,1)S(1)}, bf16[128,512]{1,0:T(8,128)(2,1)S(1)}, u32[]{:S(2)}, u32[]{:S(2)}) collective-permute-start(bf16[128,512]{1,0:T(8,128)(2,1)S(1)} %pad_maximum_fusion.1.pair), channel_id=1, source_target_pairs={{0,4},{4,0},{8,12},{12,8},{1,5},{5,1},{9,13},{13,9},{2,6},{6,2},{1... | collective-permute-start | bytes 393224 | tf_op jit(solution)/shard_map/ppermute | solution.py:266
  10.6 1.0 %copy-start.1 = (bf16[1,128,1024]{2,1,0:T(8,128)(2,1)S(1)}, bf16[1,128,1024]{2,1,0:T(8,128)(2,1)}, u32[]{:S(2)}) copy-start(bf16[1,128,1024]{2,1,0:T(8,128)(2,1)} %param.12) | copy-start | bytes 786436
  11.6 1.2 %copy-start.4 = (bf16[1,128,4096]{2,1,0:T(8,128)(2,1)S(1)}, bf16[1,128,4096]{2,1,0:T(8,128)(2,1)}, u32[]{:S(2)}) copy-start(bf16[1,128,4096]{2,1,0:T(8,128)(2,1)} %param.17) | copy-start | bytes 3145732
  12.8 23.2 %copy-start.6 = (bf16[1,128,256]{2,1,0:T(8,128)(2,1)S(1)}, bf16[1,128,256]{2,1,0:T(8,128)(2,1)}, u32[]{:S(2)}) copy-start(bf16[1,128,256]{2,1,0:T(8,128)(2,1)} %param.11) | copy-start | bytes 196612
  12.8 23.2 %copy-start.7 = (bf16[1,128,256]{2,1,0:T(8,128)(2,1)S(1)}, bf16[1,128,256]{2,1,0:T(8,128)(2,1)}, u32[]{:S(2)}) copy-start(bf16[1,128,256]{2,1,0:T(8,128)(2,1)} %param.10) | copy-start | bytes 196612
  12.8 23.5 %copy-start = (bf16[1,128,1024]{2,1,0:T(8,128)(2,1)S(1)}, bf16[1,128,1024]{2,1,0:T(8,128)(2,1)}, u32[]{:S(2)}) copy-start(bf16[1,128,1024]{2,1,0:T(8,128)(2,1)} %param.13) | copy-start | bytes 786436
  29.8 21.1 %copy-start.5 = (bf16[1,128,1024]{2,1,0:T(8,128)(2,1)S(1)}, bf16[1,128,1024]{2,1,0:T(8,128)(2,1)}, u32[]{:S(2)}) copy-start(bf16[1,128,1024]{2,1,0:T(8,128)(2,1)} %param.9) | copy-start | bytes 786436
  29.9 34.0 %copy-start.3 = (bf16[1024,1024]{1,0:T(8,128)(2,1)S(1)}, bf16[1024,1024]{1,0:T(8,128)(2,1)}, u32[]{:S(2)}) copy-start(bf16[1024,1024]{1,0:T(8,128)(2,1)} %refs_0_.1) | copy-start | bytes 6291460
  29.9 28.3 %collective-permute-start.5 = (bf16[512,1024]{1,0:T(8,128)(2,1)S(1)}, bf16[512,1024]{1,0:T(8,128)(2,1)S(1)}, u32[]{:S(2)}, u32[]{:S(2)}) collective-permute-start(bf16[512,1024]{1,0:T(8,128)(2,1)S(1)} %constant_dynamic-slice_fusion), channel_id=1, source_target_pairs={{0,8},{4,12},{8,0},{12,4},{16,20},{20,16},{24,28},{28,24},{1,9},{5... | collective-permute-start | bytes 3145736 | tf_op jit(solution)/shard_map/ppermute | solution.py:579
  32.5 20.8 %collective-permute-start.6 = (bf16[144,1024]{1,0:T(8,128)(2,1)S(1)}, bf16[144,1024]{1,0:T(8,128)(2,1)S(1)}, u32[]{:S(2)}, u32[]{:S(2)}) collective-permute-start(bf16[144,1024]{1,0:T(8,128)(2,1)S(1)} %fusion.1.refs_9_), channel_id=1, source_target_pairs={{0,1},{1,0},{2,3},{3,2},{4,5},{5,4},{6,7},{7,6},{8,9},{9,8},{10,11... | collective-permute-start | bytes 884744 | tf_op jit(solution)/shard_map/ppermute | solution.py:266
  32.9 20.8 %collective-permute-start.7 = (bf16[144,1024]{1,0:T(8,128)(2,1)S(1)}, bf16[144,1024]{1,0:T(8,128)(2,1)S(1)}, u32[]{:S(2)}, u32[]{:S(2)}) collective-permute-start(bf16[144,1024]{1,0:T(8,128)(2,1)S(1)} %fusion.1.refs_9_), channel_id=1, source_target_pairs={{0,2},{1,3},{2,0},{3,1},{4,6},{5,7},{6,4},{7,5},{8,10},{9,11},{10,... | collective-permute-start | bytes 884744 | tf_op jit(solution)/shard_map/ppermute | solution.py:266
  35.5 22.7 %collective-permute-start.8 = (bf16[144,1024]{1,0:T(8,128)(2,1)S(1)}, bf16[144,1024]{1,0:T(8,128)(2,1)S(1)}, u32[]{:S(2)}, u32[]{:S(2)}) collective-permute-start(bf16[144,1024]{1,0:T(8,128)(2,1)S(1)} %fusion.1.refs_9_), channel_id=1, source_target_pairs={{0,3},{1,2},{2,1},{3,0},{4,7},{5,6},{6,5},{7,4},{8,11},{9,10},{10,... | collective-permute-start | bytes 884744 | tf_op jit(solution)/shard_map/ppermute | solution.py:266
  36.0 14.9 %collective-permute-start.9 = (bf16[256,512]{1,0:T(8,128)(2,1)S(1)}, bf16[256,512]{1,0:T(8,128)(2,1)S(1)}, u32[]{:S(2)}, u32[]{:S(2)}) collective-permute-start(bf16[256,512]{1,0:T(8,128)(2,1)S(1)} %pad_maximum_fusion), channel_id=1, source_target_pairs={{0,8},{4,12},{8,0},{12,4},{1,9},{5,13},{9,1},{13,5},{2,10},{6,14},... | collective-permute-start | bytes 786440 | tf_op jit(solution)/shard_map/ppermute | solution.py:266
  58.2 10.9 %copy-start.2 = (bf16[1,128,1024]{2,1,0:T(8,128)(2,1)S(1)}, bf16[1,128,1024]{2,1,0:T(8,128)(2,1)}, u32[]{:S(2)}) copy-start(bf16[1,128,1024]{2,1,0:T(8,128)(2,1)} %param.12) | copy-start | bytes 786436
  58.2 5.7 %collective-permute-start.10 = (bf16[1024,1024]{1,0:T(8,128)(2,1)S(1)}, bf16[1024,1024]{1,0:T(8,128)(2,1)S(1)}, u32[]{:S(2)}, u32[]{:S(2)}) collective-permute-start(bf16[1024,1024]{1,0:T(8,128)(2,1)S(1)} %collective-permute-done.3.refs_1_), channel_id=1, source_target_pairs={{0,16},{16,0},{1,17},{17,1},{2,18},{18,2},{3,19},{19,3},{4,20},{20... | collective-permute-start | bytes 6291464 | tf_op jit(solution)/shard_map/ppermute | solution.py:266
  58.2 5.7 %collective-permute-start.11 = (bf16[512,1024]{1,0:T(8,128)(2,1)S(1)}, bf16[512,1024]{1,0:T(8,128)(2,1)S(1)}, u32[]{:S(2)}, u32[]{:S(2)}) collective-permute-start(bf16[512,1024]{1,0:T(8,128)(2,1)S(1)} %collective-permute-done.5.refs_3_), channel_id=1, source_target_pairs={{0,16},{16,0},{1,17},{17,1},{2,18},{18,2},{3,19},{19,3},{4,20},{20... | collective-permute-start | bytes 3145736 | tf_op jit(solution)/shard_map/ppermute | solution.py:266
  58.8 10.4 %collective-permute-start.12 = (f32[8,128]{1,0:T(8,128)S(1)}, f32[8,128]{1,0:T(8,128)S(1)}, u32[]{:S(2)}, u32[]{:S(2)}) collective-permute-start(f32[8,128]{1,0:T(8,128)S(1)} %shard_map.129.refs_1_), channel_id=1, source_target_pairs={{0,1},{1,0},{2,3},{3,2},{4,5},{5,4},{6,7},{7,6},{8,9},{9,8},{10,11... | collective-permute-start | bytes 12296 | tf_op jit(solution)/shard_map/ppermute | solution.py:266
  58.8 10.4 %collective-permute-start.13 = (f32[8,128]{1,0:T(8,128)S(1)}, f32[8,128]{1,0:T(8,128)S(1)}, u32[]{:S(2)}, u32[]{:S(2)}) collective-permute-start(f32[8,128]{1,0:T(8,128)S(1)} %shard_map.129.refs_1_), channel_id=1, source_target_pairs={{0,2},{1,3},{2,0},{3,1},{4,6},{5,7},{6,4},{7,5},{8,10},{9,11},{10,... | collective-permute-start | bytes 12296 | tf_op jit(solution)/shard_map/ppermute | solution.py:266
  61.8 7.4 %collective-permute-start.14 = (f32[8,128]{1,0:T(8,128)S(1)}, f32[8,128]{1,0:T(8,128)S(1)}, u32[]{:S(2)}, u32[]{:S(2)}) collective-permute-start(f32[8,128]{1,0:T(8,128)S(1)} %shard_map.129.refs_1_), channel_id=1, source_target_pairs={{0,3},{1,2},{2,1},{3,0},{4,7},{5,6},{6,5},{7,4},{8,11},{9,10},{10,... | collective-permute-start | bytes 12296 | tf_op jit(solution)/shard_map/ppermute | solution.py:266
  70.4 1.2 %collective-permute-start.15 = (f32[8,1024]{1,0:T(8,128)S(1)}, f32[8,1024]{1,0:T(8,128)S(1)}, u32[]{:S(2)}, u32[]{:S(2)}) collective-permute-start(f32[8,1024]{1,0:T(8,128)S(1)} %get-tuple-element.68.router_a), channel_id=1, source_target_pairs={{0,16},{16,0},{1,17},{17,1},{2,18},{18,2},{3,19},{19,3},{4,20},{20... | collective-permute-start | bytes 98312 | tf_op jit(solution)/shard_map/ppermute | solution.py:266
  74.4 6.7 %collective-permute-start.16 = (bf16[144,512]{1,0:T(8,128)(2,1)S(1)}, bf16[144,512]{1,0:T(8,128)(2,1)S(1)}, u32[]{:S(2)}, u32[]{:S(2)}) collective-permute-start(bf16[144,512]{1,0:T(8,128)(2,1)S(1)} %get-tuple-element.75), channel_id=1, source_target_pairs={{0,4},{4,0},{8,12},{12,8},{1,5},{5,1},{9,13},{13,9},{2,6},{6,2},{1... | collective-permute-start | bytes 442376 | tf_op jit(solution)/shard_map/ppermute | solution.py:266
  74.7 8.8 %collective-permute-start.17 = (bf16[144,512]{1,0:T(8,128)(2,1)S(1)}, bf16[144,512]{1,0:T(8,128)(2,1)S(1)}, u32[]{:S(2)}, u32[]{:S(2)}) collective-permute-start(bf16[144,512]{1,0:T(8,128)(2,1)S(1)} %get-tuple-element.76), channel_id=1, source_target_pairs={{0,8},{4,12},{8,0},{12,4},{1,9},{5,13},{9,1},{13,5},{2,10},{6,14},... | collective-permute-start | bytes 442376 | tf_op jit(solution)/shard_map/ppermute | solution.py:266
  74.7 8.8 %collective-permute-start.18 = (bf16[144,512]{1,0:T(8,128)(2,1)S(1)}, bf16[144,512]{1,0:T(8,128)(2,1)S(1)}, u32[]{:S(2)}, u32[]{:S(2)}) collective-permute-start(bf16[144,512]{1,0:T(8,128)(2,1)S(1)} %get-tuple-element.77), channel_id=1, source_target_pairs={{0,12},{4,8},{8,4},{12,0},{1,13},{5,9},{9,5},{13,1},{2,14},{6,10},... | collective-permute-start | bytes 442376 | tf_op jit(solution)/shard_map/ppermute | solution.py:266

commit v5 on v4

--- a/solution.py
+++ b/solution.py
@@ -318,8 +318,12 @@
         yield my_expert ^ k, lambda ref=ref: ref[rows].astype(jnp.float32)
 
 
-def gate_grad_kernel(meta, route, rows, saved_tok, *refs):
-    blocks, terms = refs[:-1], refs[-1]
+def flat(rows):
+    return jnp.concatenate([rows[q : q + 1] for q in range(rows.shape[0])], axis=1)
+
+
+def gate_grad_kernel(meta, route, rows, saved_tok, resid, router_rows, *refs):
+    blocks, message = refs[:-1], refs[-1]
     my_expert = meta[2]
     tok_rows = route.shape[0]
     feats = blocks[0].shape[1]
@@ -331,13 +335,32 @@
     first = (route[:, 0:1] == my_expert).astype(jnp.float32)
     second = (route[:, 1:2] == my_expert).astype(jnp.float32)
     signed = as_rows(jnp.broadcast_to((first - second) * total, (tok_rows, LANES)))
-    terms[...] = jnp.where(iota(signed.shape, 0) == EXPERTS_ROW + 1, signed, rows[...])
-
-
-def router_kernel(meta, total_tokens, route, t0, t1, t2, t3, resid, columns, router_part):
+    rest = flat(jnp.where(iota(signed.shape, 0) == EXPERTS_ROW + 1, signed, rows[...]))
+    tile = router_rows[...].astype(jnp.float32)
+    at = iota(tile.shape, 0)
+    for piece in range(3):
+        part = rest.astype(jnp.bfloat16).astype(jnp.float32)
+        tile = jnp.where(at == EXPERTS_ROW + piece, part, tile)
+        rest = rest - part
+    message[0:tok_rows] = resid[...]
+    message[tok_rows:] = tile.astype(jnp.bfloat16)
+
+
+def told(message):
+    tok_rows = message.shape[0] - ROW_TILE
+    tile = message[tok_rows:].astype(jnp.float32)
+    one, two, three = (tile[EXPERTS_ROW + p : EXPERTS_ROW + p + 1] for p in range(3))
+    line = (one + two) + three
+    return jnp.concatenate(
+        [line[:, at : at + tok_rows] for at in range(0, 8 * tok_rows, tok_rows)], axis=0
+    )
+
+
+def router_kernel(meta, total_tokens, route, m0, m1, m2, m3, columns, router_part):
     my_expert = meta[2]
     experts = EXPERTS_ROW
-    sums = as_columns((t0[...] + t1[...]) + (t2[...] + t3[...]))
+    sums = as_columns((told(m0) + told(m1)) + (told(m2) + told(m3)))
+    resid = m0[0 : route.shape[0]]
     lanes = iota(sums.shape, 1)
     inv_rms = lax.rsqrt(column(sums, experts) / D + NORM_EPS)
     delta = column(sums, experts + 1)
@@ -361,7 +384,7 @@
     router_part[...] = (
         jnp.dot(
             as_rows(scaled),
-            resid[...].astype(jnp.float32),
+            resid.astype(jnp.float32),
             precision=lax.Precision.HIGHEST,
             preferred_element_type=jnp.float32,
         )
@@ -382,14 +405,20 @@
         ).astype(jnp.bfloat16)
 
 
-def project_kernel(meta, *refs):
-    weights, grads, resids = refs[0:5], refs[5:9], refs[9:13]
-    total, rows = refs[13:]
+def times(rows, weight):
+    return lax.dot_general(rows, weight, NT, preferred_element_type=jnp.float32)
+
+
+def half_of(part, half):
+    return pl.ds(pl.multiple_of(part * half, LANES), half)
+
+
+def project_kernel(meta, own, near, across, *refs):
+    grads, resids, total, rows = refs[0:4], refs[4:8], refs[8], refs[9]
     my_core, my_seq, my_expert = meta[0], meta[1], meta[2]
     step = pl.program_id(0)
-    tok_rows, feats = grads[0].shape
-    width = weights[0].shape[1]
-    half = weights[3].shape[0]
+    tok_rows = grads[0].shape[0]
+    width = own.shape[1]
 
     @pl.when(step == 0)
     def _():
@@ -399,20 +428,36 @@
             rows[my_expert ^ k, tok_rows:] = resids[k][...]
 
     columns = pl.ds(pl.multiple_of(step * width, LANES), width)
-    for k, weight in ((0, weights[0]), (1 + my_core, weights[1]), (2 - my_core, weights[2])):
-        total[...] += lax.dot_general(
-            rows[my_seq ^ k, :, columns], weight[...], NT, preferred_element_type=jnp.float32
-        )
-    for part, weight in ((my_core, weights[3]), (1 - my_core, weights[4])):
-        total[:, pl.ds(pl.multiple_of(part * half, LANES), half)] += lax.dot_general(
-            rows[my_seq ^ 3, :, columns], weight[...], NT, preferred_element_type=jnp.float32
-        )
+    total[...] += times(rows[my_seq, :, columns], own[...]) + times(
+        rows[my_seq ^ (1 + my_core), :, columns], near[...]
+    )
+    here = half_of(my_core, across.shape[0])
+    total[:, here] += times(rows[my_seq ^ 3, :, columns], across[...])
+
+
+def project_rest_kernel(meta, far, across, rows, most, total):
+    my_core, my_seq = meta[0], meta[1]
+    step = pl.program_id(0)
+    width = far.shape[1]
+
+    @pl.when(step == 0)
+    def _():
+        total[...] = most[...]
+
+    columns = pl.ds(pl.multiple_of(step * width, LANES), width)
+    total[...] += times(rows[my_seq ^ (2 - my_core), :, columns], far[...])
+    here = half_of(1 - my_core, across.shape[0])
+    total[:, here] += times(rows[my_seq ^ 3, :, columns], across[...])
 
 
 def stacked(matrix, heads):
     return jnp.concatenate(
         [matrix[:, h * HEAD_DIM : (h + 1) * HEAD_DIM] for h in range(heads)], axis=0
     )
+
+
+def distances(core):
+    return 0, 2 - core, 1 + core, 3
 
 
 def four(pair, pair_x, pair_y):
@@ -430,7 +475,11 @@
     position = lax.rem(iota((rows, tok_rows), 0), tok_rows)
     key_at = iota((rows, tok_rows), 1)
     allowed = jnp.concatenate(
-        [key_at + ((my_seq ^ k) - my_seq) * tok_rows <= position for k in range(4)], axis=1
+        [
+            key_at + ((my_seq ^ k) - my_seq) * tok_rows <= position
+            for k in distances(meta[0])
+        ],
+        axis=1,
     )
     for kv in range(kv_count):
         heads = stacked(query[:, kv * group * HEAD_DIM : (kv + 1) * group * HEAD_DIM], group)
@@ -527,7 +576,9 @@
         rows = rows.astype(jnp.float32)
         count = rows.shape[0] // 2
         sums.append(rows[0:count] + rows[count:])
-    total = (sums[0] + sums[1]) + (sums[2] + sums[3])
+    first = meta[0] == 0
+    one, two = jnp.where(first, sums[2], sums[1]), jnp.where(first, sums[1], sums[2])
+    total = (sums[0] + one) + (two + sums[3])
     width = total.shape[1]
     for piece in range(total.shape[0] // EXPERTS_ROW):
         router_grad[:, piece * width : (piece + 1) * width] = total[
@@ -582,7 +633,7 @@
     router_rows = jnp.pad(router_weight.T, ((0, ROW_TILE - EXPERTS_ROW), (0, 0)))
     grads = over_expert(grad)
     pair = jnp.concatenate([key_in[0], value_in[0]], axis=1)
-    pair_x = partner(pair, "seq", seq_n, 1)
+    pair_x = over_both(pair, lambda c: distances(c)[1])
     weight_near = over_both(o_weight, lambda c: 1 + c)
     router_pad = jnp.pad(router_weight, ((0, 0), (0, LANES - router_weight.shape[1])))
     rows, place, saved_tok = call(
@@ -595,15 +646,17 @@
             ((tok_rows, width), bf16),
         ),
     )
-    own_rows = jnp.concatenate([resid, router_rows], axis=0)
-    grads[1:], weight_near, rows, place, saved_tok, pair_x, own_rows = lax.optimization_barrier(
-        (grads[1:], weight_near, rows, place, saved_tok, pair_x, own_rows)
+    grads[1:], weight_near, rows, place, saved_tok, pair_x = lax.optimization_barrier(
+        (grads[1:], weight_near, rows, place, saved_tok, pair_x)
+    )
+    (own_rows,) = call(
+        gate_grad_kernel,
+        meta,
+        (route, rows, saved_tok, resid, router_rows, *grads),
+        (((tok_rows + ROW_TILE, feats), bf16),),
     )
     resids = over_expert(own_rows)
-    (terms,) = call(
-        gate_grad_kernel, meta, (route, rows, saved_tok, *grads), (((8, tok_rows), f32),)
-    )
-    pair_y = partner(jnp.concatenate([pair, pair_x], axis=0), "seq", seq_n, 2)
+    pair_y = over_both(jnp.concatenate([pair, pair_x], axis=0), lambda c: distances(c)[2])
     pairs = (pair, pair_x, pair_y)
     across = lax.dynamic_slice_in_dim(weight_near, core * half_rows, half_rows, axis=0)
     across_mine = over_both(across, lambda c: 2 - c)
@@ -623,35 +676,47 @@
     steps = 4
     model_rows = o_weight.shape[0]
     all_rows = 2 * tok_rows + ROW_TILE
-    terms, across_mine, resids[1:], probs, attn_out, weight_near = lax.optimization_barrier(
-        (terms, across_mine, resids[1:], probs, attn_out, weight_near)
+    across_mine, resids[1:], probs, attn_out, weight_near = lax.optimization_barrier(
+        (across_mine, resids[1:], probs, attn_out, weight_near)
     )
     weight_far = partner(weight_near, "dp", dp_n, 1)
     across_other = partner(across_mine, "dp", dp_n, 1)
-    weights = (o_weight, weight_near, weight_far, across_mine, across_other)
-    token_parts = (*grads, *resids)
-    projected = pl.pallas_call(
+    all_shape = (all_rows, model_rows)
+    rows_shape = (expert_n, all_rows, feats)
+
+    def project(kernel, weights, in_place, shapes):
+        return pl.pallas_call(
+            kernel,
+            out_shape=shapes,
+            grid_spec=pltpu.PrefetchScalarGridSpec(
+                num_scalar_prefetch=1,
+                grid=(steps,),
+                in_specs=[
+                    pl.BlockSpec((w.shape[0], feats // steps), lambda i, m: (0, i)) for w in weights
+                ]
+                + [pl.BlockSpec(memory_space=pltpu.VMEM)] * len(in_place),
+                out_specs=[whole(s.shape) for s in shapes],
+            ),
+            compiler_params=params(),
+        )(meta, *weights, *in_place)
+
+    most, staged = project(
         project_kernel,
-        out_shape=jax.ShapeDtypeStruct((all_rows, model_rows), f32),
-        grid_spec=pltpu.PrefetchScalarGridSpec(
-            num_scalar_prefetch=1,
-            grid=(steps,),
-            in_specs=[
-                pl.BlockSpec((w.shape[0], feats // steps), lambda i, m: (0, i)) for w in weights
-            ]
-            + [pl.BlockSpec(memory_space=pltpu.VMEM)] * len(token_parts),
-            out_specs=whole((all_rows, model_rows)),
-            scratch_shapes=[pltpu.VMEM((expert_n, all_rows, feats), bf16)],
-        ),
-        compiler_params=params(),
-    )(meta, *weights, *token_parts)
-    all_terms = over_expert(terms)
-    projected, all_terms[1:] = lax.optimization_barrier((projected, all_terms[1:]))
+        (o_weight, weight_near, across_mine),
+        (*grads, *resids),
+        [jax.ShapeDtypeStruct(all_shape, f32), jax.ShapeDtypeStruct(rows_shape, bf16)],
+    )
+    (projected,) = project(
+        project_rest_kernel,
+        (weight_far, across_other),
+        (staged, most),
+        [jax.ShapeDtypeStruct(all_shape, f32)],
+    )
     total_tokens = dp_n * seq_n * tok_rows
     columns, router_part = call(
         lambda meta, *refs: router_kernel(meta, total_tokens, *refs),
         meta,
-        (route, *all_terms, resid),
+        (route, *resids),
         (((tok_rows, LANES), f32), ((8, feats), f32)),
     )
     term_width = 2 * kv_width
@@ -669,7 +734,9 @@
             *(((term, bf16),) * 3),
         ),
     )
-    back = [partner(key_terms[k - 1], "seq", seq_n, k) for k in range(1, seq_n)]
+    back = [
+        over_both(term, lambda c: distances(c)[at]) for at, term in enumerate(key_terms, start=1)
+    ]
     columns, own = lax.optimization_barrier((columns, own))
     (expert_grad,) = call(
         expert_grad_kernel, meta, (columns, place, *grads), (((capacity, width), bf16),)

time: 85.5 us -> 82.2 us (0.961)
  waiting for transfers between devices: 40.6 us -> 36.7 us
  starting transfers between devices: 19.6 us -> 17.3 us
  local copies, waits for them, and re-layouts: 5.65 us -> 7.34 us
  Pallas kernels: 17.1 us -> 18.7 us
    ppermute x17 -> x9, waiting for transfers between devices: 40.6 us -> 24.5 us  [partner(): return lax.ppermute(array, axis, [(i, i ^ distance) for i in range(count)])]
    ppermute x2 -> x7, waiting for transfers between devices: 0.01 us -> 12.2 us  [over_both(): return lax.ppermute(array, ('dp', 'seq'), pairs)]
    ppermute x17 -> x9, starting transfers between devices: 15.5 us -> 7.57 us  [partner(): return lax.ppermute(array, axis, [(i, i ^ distance) for i in range(count)])]
    ppermute x2 -> x7, starting transfers between devices: 4.16 us -> 9.77 us  [over_both(): return lax.ppermute(array, ('dp', 'seq'), pairs)]
    pallas_call x1 -> x2, Pallas kernels: 5.19 us -> 6.63 us  [project(): pl.pallas_call(kernel, out_shape=shapes, grid_spec=pltpu.PrefetchScalarGr...]
    unnamed x20 -> x22, local copies, waits for them, and re-layouts: 4.57 us -> 5.52 us
  transfers between devices with their start and end apart: 19 -> 16, of which waited for: 8 -> 9; matrix products, arithmetic and copies ran while one was open for 5% -> 6% of each run, Pallas kernels for 14% -> 18%
where the time goes in v5:
time: 82.2 us; the launch traced here: 81.9 us
  waiting for transfers between devices  36.7 us (45%)
  Pallas kernels  18.7 us (23%)
  starting transfers between devices  17.3 us (21%)
  local copies, waits for them, and re-layouts  7.34 us (9%)
  other arithmetic  0.97 us (1%)
    ppermute x9, waiting for transfers between devices, partner(): return lax.ppermute(array, axis, [(i, i ^ distance) for i in range(count)])  24.5 us
    ppermute x7, waiting for transfers between devices, over_both(): return lax.ppermute(array, ('dp', 'seq'), pairs)  12.2 us
    pallas_call x7, Pallas kernels, call(): pl.pallas_call(kernel, out_shape=shapes, in_specs=[pl.BlockSpec(memory_sp...  12.1 us
    ppermute x7, starting transfers between devices, over_both(): return lax.ppermute(array, ('dp', 'seq'), pairs)  9.77 us
    ppermute x9, starting transfers between devices, partner(): return lax.ppermute(array, axis, [(i, i ^ distance) for i in range(count)])  7.57 us
    pallas_call x2, Pallas kernels, project(): pl.pallas_call(kernel, out_shape=shapes, grid_spec=pltpu.PrefetchScalarGr...  6.63 us
    unnamed x22, local copies, waits for them, and re-layouts  5.52 us
    pad x1, local copies, waits for them, and re-layouts, local_fast(): jnp.pad(router_weight, ((0, 0), (0, LANES - router_weight.shape[1])))  1.75 us
  transfers between devices with their start and end apart: 16, of which 9 were waited for; matrix products, arithmetic and copies ran while one was open for 6% of the time, Pallas kernels for 18%

profile of v5, /device:TPU:8, one launch (start us, length us, event | category | flops | bytes accessed | tf_op | source)
XLA Modules:
  0.0 81.9 jit_solution(6193041257917839540)
XLA Ops:
  0.6 1.6 %collective-permute-start.3 = (bf16[1024,1024]{1,0:T(8,128)(2,1)}, bf16[1024,1024]{1,0:T(8,128)(2,1)S(1)}, u32[]{:S(2)}, u32[]{:S(2)}) collective-permute-start(bf16[1024,1024]{1,0:T(8,128)(2,1)} %own.1), channel_id=1, source_target_pairs={{0,4},{4,0},{8,12},{12,8},{16,24},{20,28},{24,16},{28,20},{1,5},{5... | collective-permute-start | bytes 6291464 | tf_op jit(solution)/shard_map/ppermute | solution.py:630
  2.6 2.6 %collective-permute-start.1 = (bf16[128,1024]{1,0:T(8,128)(2,1)}, bf16[128,1024]{1,0:T(8,128)(2,1)S(1)}, u32[]{:S(2)}, u32[]{:S(2)}) collective-permute-start(bf16[128,1024]{1,0:T(8,128)(2,1)} %bitcast.17), channel_id=1, source_target_pairs={{0,2},{1,3},{2,0},{3,1},{4,6},{5,7},{6,4},{7,5},{8,10},{9,11},{10,... | collective-permute-start | bytes 786440 | tf_op jit(solution)/shard_map/ppermute | solution.py:266
  5.7 0.9 %pad_maximum_fusion.1.pair = bf16[128,512]{1,0:T(8,128)(2,1)S(1)} fusion(bf16[128,256]{1,0:T(8,128)(2,1)} %bitcast.31, bf16[128,256]{1,0:T(8,128)(2,1)} %bitcast.33), kind=kLoop, calls=%fused_computation.1 | loop fusion | flops 262144 | bytes 262144 | tf_op jit(solution)/shard_map/concatenate | solution.py:635
  6.6 1.6 %collective-permute-start.4 = (bf16[128,512]{1,0:T(8,128)(2,1)S(1)}, bf16[128,512]{1,0:T(8,128)(2,1)S(1)}, u32[]{:S(2)}, u32[]{:S(2)}) collective-permute-start(bf16[128,512]{1,0:T(8,128)(2,1)S(1)} %pad_maximum_fusion.1.pair), channel_id=1, source_target_pairs={{0,8},{4,12},{8,0},{12,4},{16,20},{20,16},{24,28},{28,24},{1,9},{5... | collective-permute-start | bytes 393224 | tf_op jit(solution)/shard_map/ppermute | solution.py:630
  8.1 0.8 copy.14
  8.9 1.6 %copy.15 = bf16[1024,4]{1,0:T(8,128)(2,1)} copy(bf16[1024,4]{0,1:T(4,128)(2,1)} %param.15) | data formatting | bytes 16384 | tf_op args[6]
  10.5 1.7 %pad.8.router_pad = bf16[1024,128]{1,0:T(8,128)(2,1)} pad(bf16[1024,4]{1,0:T(8,128)(2,1)} %copy.15, bf16[]{:T(256)} %constant.17.clone.1), padding=0_0x0_124 | pad | bytes 270338 | tf_op jit(solution)/shard_map/jit(_pad)/pad | solution.py:638
  12.3 1.2 %copy-done.2 = bf16[1,128,4096]{2,1,0:T(8,128)(2,1)S(1)} copy-done((bf16[1,128,4096]{2,1,0:T(8,128)(2,1)S(1)}, bf16[1,128,4096]{2,1,0:T(8,128)(2,1)}, u32[]{:S(2)}) %copy-start.2) | copy-done | bytes 1048600
  13.6 0.9 %copy-done.3 = bf16[1,128,1024]{2,1,0:T(8,128)(2,1)S(1)} copy-done((bf16[1,128,1024]{2,1,0:T(8,128)(2,1)S(1)}, bf16[1,128,1024]{2,1,0:T(8,128)(2,1)}, u32[]{:S(2)}) %copy-start.3) | copy-done | bytes 262168
  14.5 0.9 %copy-done.6 = bf16[1024,128]{1,0:T(8,128)(2,1)S(1)} copy-done((bf16[1024,128]{1,0:T(8,128)(2,1)S(1)}, bf16[1024,128]{1,0:T(8,128)(2,1)}, u32[]{:S(2)}) %copy-start.6) | copy-done | bytes 262168
  15.5 1.3 %shard_map.128 = (f32[8,128]{1,0:T(8,128)S(1)}, bf16[128,128]{1,0:T(8,128)(2,1)S(1)}, bf16[128,4096]{1,0:T(8,128)(2,1)S(1)}) custom-call(s32[3]{0:T(128)S(1)} %pad_add_fusion.meta, s32[128,2]{1,0:T(8,128)S(1)} %bitcast.22, bf16[1024,128]{1,0:T(8,128)(2,1)S(1)} %copy-done.6, bf16[128,1024]{1,0:T(8,128)(2,1)S(1)} %bitcast.26, bf16[128,4096]{1,0:T(8,128)(2,1)S(1)} %bitcast.25), custom_call_target="tpu_custom_call" | custom-call | tf_op jit(solution)/shard_map/pallas_call | solution.py:595
  16.8 6.7 %collective-permute-done.1.refs_2_ = bf16[128,1024]{1,0:T(8,128)(2,1)S(1)} collective-permute-done((bf16[128,1024]{1,0:T(8,128)(2,1)}, bf16[128,1024]{1,0:T(8,128)(2,1)S(1)}, u32[]{:S(2)}, u32[]{:S(2)}) %collective-permute-start.1) | collective-permute-done | bytes 262176 | tf_op jit(solution)/shard_map/ppermute | solution.py:266
  23.5 4.8 %collective-permute-done.2.refs_3_ = bf16[128,1024]{1,0:T(8,128)(2,1)S(1)} collective-permute-done((bf16[128,1024]{1,0:T(8,128)(2,1)}, bf16[128,1024]{1,0:T(8,128)(2,1)S(1)}, u32[]{:S(2)}, u32[]{:S(2)}) %collective-permute-start.2) | collective-permute-done | bytes 262176 | tf_op jit(solution)/shard_map/ppermute | solution.py:266
  28.4 1.6 %collective-permute-start.5 = (bf16[512,1024]{1,0:T(8,128)(2,1)S(1)}, bf16[512,1024]{1,0:T(8,128)(2,1)S(1)}, u32[]{:S(2)}, u32[]{:S(2)}) collective-permute-start(bf16[512,1024]{1,0:T(8,128)(2,1)S(1)} %constant_dynamic-slice_fusion), channel_id=1, source_target_pairs={{0,8},{4,12},{8,0},{12,4},{16,20},{20,16},{24,28},{28,24},{1,9},{5... | collective-permute-start | bytes 3145736 | tf_op jit(solution)/shard_map/ppermute | solution.py:630
  30.1 1.1 %shard_map.129.refs_1_.refs_4_ = bf16[144,1024]{1,0:T(8,128)(2,1)S(1)} custom-call(s32[3]{0:T(128)S(1)} %pad_add_fusion.meta, s32[128,2]{1,0:T(8,128)S(1)} %bitcast.23, f32[8,128]{1,0:T(8,128)S(1)} %get-tuple-element.43.rows, bf16[128,4096]{1,0:T(8,128)(2,1)S(1)} %get-tuple-element.44.saved_tok, bf16[128,1024]{1,0:T(8,128)(2,1)S(1)} %bitcast.27, ...), custom_call_target="tpu_custom_call" | custom-call | tf_op jit(solution)/shard_map/pallas_call | solution.py:595
  31.6 2.6 %collective-permute-start.7 = (bf16[144,1024]{1,0:T(8,128)(2,1)S(1)}, bf16[144,1024]{1,0:T(8,128)(2,1)S(1)}, u32[]{:S(2)}, u32[]{:S(2)}) collective-permute-start(bf16[144,1024]{1,0:T(8,128)(2,1)S(1)} %shard_map.129.refs_1_.refs_4_), channel_id=1, source_target_pairs={{0,2},{1,3},{2,0},{3,1},{4,6},{5,7},{6,4},{7,5},{8,10},{9,11},{10,... | collective-permute-start | bytes 884744 | tf_op jit(solution)/shard_map/ppermute | solution.py:266
  34.7 1.6 %collective-permute-start.9 = (bf16[256,512]{1,0:T(8,128)(2,1)S(1)}, bf16[256,512]{1,0:T(8,128)(2,1)S(1)}, u32[]{:S(2)}, u32[]{:S(2)}) collective-permute-start(bf16[256,512]{1,0:T(8,128)(2,1)S(1)} %pad_maximum_fusion), channel_id=1, source_target_pairs={{0,4},{4,0},{8,12},{12,8},{16,24},{20,28},{24,16},{28,20},{1,5},{5... | collective-permute-start | bytes 786440 | tf_op jit(solution)/shard_map/ppermute | solution.py:630
  36.3 7.8 %collective-permute-done.9.pair_y = bf16[256,512]{1,0:T(8,128)(2,1)S(1)} collective-permute-done((bf16[256,512]{1,0:T(8,128)(2,1)S(1)}, bf16[256,512]{1,0:T(8,128)(2,1)S(1)}, u32[]{:S(2)}, u32[]{:S(2)}) %collective-permute-start.9) | collective-permute-done | bytes 262176 | tf_op jit(solution)/shard_map/ppermute | solution.py:630
  44.0 2.4 %shard_map.130 = (f32[2,512,512]{2,1,0:T(8,128)S(1)}, f32[128,1024]{1,0:T(8,128)S(1)}) custom-call(s32[3]{0:T(128)S(1)} %pad_add_fusion.meta, bf16[128,1024]{1,0:T(8,128)(2,1)S(1)} %bitcast.28, bf16[128,512]{1,0:T(8,128)(2,1)S(1)} %pad_maximum_fusion.1.pair, bf16[128,512]{1,0:T(8,128)(2,1)S(1)} %collective-permute-done.4.pair_x, ...), custom_call_target="tpu_custom_call" | custom-call | tf_op jit(solution)/shard_map/pallas_call | solution.py:595
  46.4 7.9 %collective-permute-done.7.refs_3_.refs_6_ = bf16[144,1024]{1,0:T(8,128)(2,1)S(1)} collective-permute-done((bf16[144,1024]{1,0:T(8,128)(2,1)S(1)}, bf16[144,1024]{1,0:T(8,128)(2,1)S(1)}, u32[]{:S(2)}, u32[]{:S(2)}) %collective-permute-start.7) | collective-permute-done | bytes 294944 | tf_op jit(solution)/shard_map/ppermute | solution.py:266
  54.3 5.1 %collective-permute-done.8.refs_4_.refs_7_ = bf16[144,1024]{1,0:T(8,128)(2,1)S(1)} collective-permute-done((bf16[144,1024]{1,0:T(8,128)(2,1)S(1)}, bf16[144,1024]{1,0:T(8,128)(2,1)S(1)}, u32[]{:S(2)}, u32[]{:S(2)}) %collective-permute-start.8) | collective-permute-done | bytes 294944 | tf_op jit(solution)/shard_map/ppermute | solution.py:266
  59.9 1.3 %shard_map.131 = (f32[128,128]{1,0:T(8,128)S(1)}, f32[8,1024]{1,0:T(8,128)S(1)}) custom-call(s32[3]{0:T(128)S(1)} %pad_add_fusion.meta, s32[128,2]{1,0:T(8,128)S(1)} %bitcast.24, bf16[144,1024]{1,0:T(8,128)(2,1)S(1)} %shard_map.129.refs_1_.refs_4_, bf16[144,1024]{1,0:T(8,128)(2,1)S(1)} %collective-permute-done.6.refs_2_.refs_5_, ...), custom_call_target="tpu_custom_call" | custom-call | tf_op jit(solution)/shard_map/pallas_call | solution.py:595
  61.2 3.8 %shard_map.132 = (f32[272,1024]{1,0:T(8,128)S(1)}, bf16[4,272,1024]{2,1,0:T(8,128)(2,1)S(1)}) custom-call(s32[3]{0:T(128)S(1)} %pad_add_fusion.meta, bf16[1024,1024]{1,0:T(8,128)(2,1)S(1)} %copy-done.1, bf16[1024,1024]{1,0:T(8,128)(2,1)S(1)} %collective-permute-done.3.near, bf16[512,1024]{1,0:T(8,128)(2,1)S(1)} %collective-permute-done.5.across, ...), custom_call_target="tpu_custom_call" | custom-call | tf_op jit(solution)/shard_map/pallas_call | solution.py:688
  65.1 2.8 %shard_map.133.projected = f32[272,1024]{1,0:T(8,128)S(1)} custom-call(s32[3]{0:T(128)S(1)} %pad_add_fusion.meta, bf16[1024,1024]{1,0:T(8,128)(2,1)S(1)} %collective-permute-done.10.far, bf16[512,1024]{1,0:T(8,128)(2,1)S(1)} %collective-permute-done.11.across, bf16[4,272,1024]{2,1,0:T(8,128)(2,1)S(1)} %get-tuple-element.58.rows, ...), custom_call_target="tpu_custom_call" | custom-call | tf_op jit(solution)/shard_map/pallas_call | solution.py:688
  67.9 2.8 %shard_map.134 = (bf16[128,1024]{1,0:T(8,128)(2,1)}, bf16[16,512]{1,0:T(8,128)(2,1)S(1)}, f32[128,512]{1,0:T(8,128)S(1)}, bf16[144,512]{1,0:T(8,128)(2,1)S(1)}, ...) custom-call(s32[3]{0:T(128)S(1)} %pad_add_fusion.meta, f32[128,128]{1,0:T(8,128)S(1)} %get-tuple-element.73.columns, ...), custom_call_target="tpu_custom_call" | custom-call | tf_op jit(solution)/shard_map/pallas_call | solution.py:595
  70.7 1.1 %collective-permute-start.13 = (bf16[144,512]{1,0:T(8,128)(2,1)S(1)}, bf16[144,512]{1,0:T(8,128)(2,1)S(1)}, u32[]{:S(2)}, u32[]{:S(2)}) collective-permute-start(bf16[144,512]{1,0:T(8,128)(2,1)S(1)} %get-tuple-element.67), channel_id=1, source_target_pairs={{0,8},{4,12},{8,0},{12,4},{16,20},{20,16},{24,28},{28,24},{1,9},{5... | collective-permute-start | bytes 442376 | tf_op jit(solution)/shard_map/ppermute | solution.py:630
  72.3 1.9 %collective-permute-start.15 = (bf16[144,512]{1,0:T(8,128)(2,1)S(1)}, bf16[144,512]{1,0:T(8,128)(2,1)S(1)}, u32[]{:S(2)}, u32[]{:S(2)}) collective-permute-start(bf16[144,512]{1,0:T(8,128)(2,1)S(1)} %get-tuple-element.69), channel_id=1, source_target_pairs={{0,12},{4,8},{8,4},{12,0},{16,28},{20,24},{24,20},{28,16},{1,13},{... | collective-permute-start | bytes 442376 | tf_op jit(solution)/shard_map/ppermute | solution.py:630
  74.2 2.0 %shard_map.136 = bf16[128,4096]{1,0:T(8,128)(2,1)} custom-call(s32[3]{0:T(128)S(1)} %pad_add_fusion.meta, f32[128,128]{1,0:T(8,128)S(1)} %get-tuple-element.73.columns, bf16[128,128]{1,0:T(8,128)(2,1)S(1)} %get-tuple-element.74.place, bf16[128,1024]{1,0:T(8,128)(2,1)S(1)} %bitcast.21, bf16[128,1024]{1,0:T(8,128)(2,1)S(1)} %collective-permute-done.refs_1_, ...), custom_call_target="tpu_custom_call" | custom-call | tf_op jit(solution)/shard_map/pallas_call | solution.py:595
  76.2 1.7 %collective-permute-done.13.t1 = bf16[144,512]{1,0:T(8,128)(2,1)S(1)} collective-permute-done((bf16[144,512]{1,0:T(8,128)(2,1)S(1)}, bf16[144,512]{1,0:T(8,128)(2,1)S(1)}, u32[]{:S(2)}, u32[]{:S(2)}) %collective-permute-start.13) | collective-permute-done | bytes 147488 | tf_op jit(solution)/shard_map/ppermute | solution.py:630
  77.9 0.6 collective-permute-done.14.t2
  78.5 2.1 %collective-permute-done.15.t3 = bf16[144,512]{1,0:T(8,128)(2,1)S(1)} collective-permute-done((bf16[144,512]{1,0:T(8,128)(2,1)S(1)}, bf16[144,512]{1,0:T(8,128)(2,1)S(1)}, u32[]{:S(2)}, u32[]{:S(2)}) %collective-permute-start.15) | collective-permute-done | bytes 147488 | tf_op jit(solution)/shard_map/ppermute | solution.py:630
  80.6 1.2 %shard_map.135 = (bf16[128,256]{1,0:T(8,128)(2,1)}, bf16[128,256]{1,0:T(8,128)(2,1)}, f32[4,1024]{1,0:T(4,128)}) custom-call(s32[3]{0:T(128)S(1)} %pad_add_fusion.meta, bf16[16,512]{1,0:T(8,128)(2,1)S(1)} %get-tuple-element.64.router, f32[128,512]{1,0:T(8,128)S(1)} %get-tuple-element.66.own, bf16[144,512]{1,0:T(8,128)(2,1)S(1)} %collective-permute-done.13.t1, ...), custom_call_target="tpu_custom_call" | custom-call | tf_op jit(solution)/shard_map/pallas_call | solution.py:595
  (37 shorter events, 3.2 us)
Async XLA Ops:
  0.6 27.7 %collective-permute-start.3 = (bf16[1024,1024]{1,0:T(8,128)(2,1)}, bf16[1024,1024]{1,0:T(8,128)(2,1)S(1)}, u32[]{:S(2)}, u32[]{:S(2)}) collective-permute-start(bf16[1024,1024]{1,0:T(8,128)(2,1)} %own.1), channel_id=1, source_target_pairs={{0,4},{4,0},{8,12},{12,8},{16,24},{20,28},{24,16},{28,20},{1,5},{5... | collective-permute-start | bytes 6291464 | tf_op jit(solution)/shard_map/ppermute | solution.py:630
  2.2 14.6 %collective-permute-start = (bf16[128,1024]{1,0:T(8,128)(2,1)}, bf16[128,1024]{1,0:T(8,128)(2,1)S(1)}, u32[]{:S(2)}, u32[]{:S(2)}) collective-permute-start(bf16[128,1024]{1,0:T(8,128)(2,1)} %bitcast.16), channel_id=1, source_target_pairs={{0,1},{1,0},{2,3},{3,2},{4,5},{5,4},{6,7},{7,6},{8,9},{9,8},{10,11... | collective-permute-start | bytes 786440 | tf_op jit(solution)/shard_map/ppermute | solution.py:266
  2.6 20.9 %collective-permute-start.1 = (bf16[128,1024]{1,0:T(8,128)(2,1)}, bf16[128,1024]{1,0:T(8,128)(2,1)S(1)}, u32[]{:S(2)}, u32[]{:S(2)}) collective-permute-start(bf16[128,1024]{1,0:T(8,128)(2,1)} %bitcast.17), channel_id=1, source_target_pairs={{0,2},{1,3},{2,0},{3,1},{4,6},{5,7},{6,4},{7,5},{8,10},{9,11},{10,... | collective-permute-start | bytes 786440 | tf_op jit(solution)/shard_map/ppermute | solution.py:266
  5.2 23.1 %collective-permute-start.2 = (bf16[128,1024]{1,0:T(8,128)(2,1)}, bf16[128,1024]{1,0:T(8,128)(2,1)S(1)}, u32[]{:S(2)}, u32[]{:S(2)}) collective-permute-start(bf16[128,1024]{1,0:T(8,128)(2,1)} %bitcast.18), channel_id=1, source_target_pairs={{0,3},{1,2},{2,1},{3,0},{4,7},{5,6},{6,5},{7,4},{8,11},{9,10},{10,... | collective-permute-start | bytes 786440 | tf_op jit(solution)/shard_map/ppermute | solution.py:266
  6.6 10.2 %collective-permute-start.4 = (bf16[128,512]{1,0:T(8,128)(2,1)S(1)}, bf16[128,512]{1,0:T(8,128)(2,1)S(1)}, u32[]{:S(2)}, u32[]{:S(2)}) collective-permute-start(bf16[128,512]{1,0:T(8,128)(2,1)S(1)} %pad_maximum_fusion.1.pair), channel_id=1, source_target_pairs={{0,8},{4,12},{8,0},{12,4},{16,20},{20,16},{24,28},{28,24},{1,9},{5... | collective-permute-start | bytes 393224 | tf_op jit(solution)/shard_map/ppermute | solution.py:630
  10.5 19.5 %copy-start.9 = (bf16[1024,4]{0,1:T(4,128)(2,1)S(1)}, bf16[1024,4]{0,1:T(4,128)(2,1)}, u32[]{:S(2)}) copy-start(bf16[1024,4]{0,1:T(4,128)(2,1)} %param.15) | copy-start | bytes 24580
  10.5 19.5 %copy-start = (bf16[1,128,1024]{2,1,0:T(8,128)(2,1)S(1)}, bf16[1,128,1024]{2,1,0:T(8,128)(2,1)}, u32[]{:S(2)}) copy-start(bf16[1,128,1024]{2,1,0:T(8,128)(2,1)} %param.13) | copy-start | bytes 786436
  12.3 1.2 %copy-start.2 = (bf16[1,128,4096]{2,1,0:T(8,128)(2,1)S(1)}, bf16[1,128,4096]{2,1,0:T(8,128)(2,1)}, u32[]{:S(2)}) copy-start(bf16[1,128,4096]{2,1,0:T(8,128)(2,1)} %param.17) | copy-start | bytes 3145732
  13.6 0.9 %copy-start.3 = (bf16[1,128,1024]{2,1,0:T(8,128)(2,1)S(1)}, bf16[1,128,1024]{2,1,0:T(8,128)(2,1)}, u32[]{:S(2)}) copy-start(bf16[1,128,1024]{2,1,0:T(8,128)(2,1)} %param.12) | copy-start | bytes 786436
  14.5 0.9 %copy-start.6 = (bf16[1024,128]{1,0:T(8,128)(2,1)S(1)}, bf16[1024,128]{1,0:T(8,128)(2,1)}, u32[]{:S(2)}) copy-start(bf16[1024,128]{1,0:T(8,128)(2,1)} %pad.8.router_pad) | copy-start | bytes 786436
  15.5 14.6 %copy-start.4 = (bf16[1,128,1024]{2,1,0:T(8,128)(2,1)S(1)}, bf16[1,128,1024]{2,1,0:T(8,128)(2,1)}, u32[]{:S(2)}) copy-start(bf16[1,128,1024]{2,1,0:T(8,128)(2,1)} %param.12) | copy-start | bytes 786436
  28.3 6.3 %copy-start.7 = (bf16[1,128,256]{2,1,0:T(8,128)(2,1)S(1)}, bf16[1,128,256]{2,1,0:T(8,128)(2,1)}, u32[]{:S(2)}) copy-start(bf16[1,128,256]{2,1,0:T(8,128)(2,1)} %param.11) | copy-start | bytes 196612
  28.3 6.3 %copy-start.8 = (bf16[1,128,256]{2,1,0:T(8,128)(2,1)S(1)}, bf16[1,128,256]{2,1,0:T(8,128)(2,1)}, u32[]{:S(2)}) copy-start(bf16[1,128,256]{2,1,0:T(8,128)(2,1)} %param.10) | copy-start | bytes 196612
  28.4 15.6 %copy-start.5 = (bf16[1,128,1024]{2,1,0:T(8,128)(2,1)S(1)}, bf16[1,128,1024]{2,1,0:T(8,128)(2,1)}, u32[]{:S(2)}) copy-start(bf16[1,128,1024]{2,1,0:T(8,128)(2,1)} %param.9) | copy-start | bytes 786436
  28.4 31.0 %collective-permute-start.5 = (bf16[512,1024]{1,0:T(8,128)(2,1)S(1)}, bf16[512,1024]{1,0:T(8,128)(2,1)S(1)}, u32[]{:S(2)}, u32[]{:S(2)}) collective-permute-start(bf16[512,1024]{1,0:T(8,128)(2,1)S(1)} %constant_dynamic-slice_fusion), channel_id=1, source_target_pairs={{0,8},{4,12},{8,0},{12,4},{16,20},{20,16},{24,28},{28,24},{1,9},{5... | collective-permute-start | bytes 3145736 | tf_op jit(solution)/shard_map/ppermute | solution.py:630
  30.1 31.2 %copy-start.1 = (bf16[1024,1024]{1,0:T(8,128)(2,1)S(1)}, bf16[1024,1024]{1,0:T(8,128)(2,1)}, u32[]{:S(2)}) copy-start(bf16[1024,1024]{1,0:T(8,128)(2,1)} %own.1) | copy-start | bytes 6291460
  31.1 15.3 %collective-permute-start.6 = (bf16[144,1024]{1,0:T(8,128)(2,1)S(1)}, bf16[144,1024]{1,0:T(8,128)(2,1)S(1)}, u32[]{:S(2)}, u32[]{:S(2)}) collective-permute-start(bf16[144,1024]{1,0:T(8,128)(2,1)S(1)} %shard_map.129.refs_1_.refs_4_), channel_id=1, source_target_pairs={{0,1},{1,0},{2,3},{3,2},{4,5},{5,4},{6,7},{7,6},{8,9},{9,8},{10,11... | collective-permute-start | bytes 884744 | tf_op jit(solution)/shard_map/ppermute | solution.py:266
  31.6 22.7 %collective-permute-start.7 = (bf16[144,1024]{1,0:T(8,128)(2,1)S(1)}, bf16[144,1024]{1,0:T(8,128)(2,1)S(1)}, u32[]{:S(2)}, u32[]{:S(2)}) collective-permute-start(bf16[144,1024]{1,0:T(8,128)(2,1)S(1)} %shard_map.129.refs_1_.refs_4_), channel_id=1, source_target_pairs={{0,2},{1,3},{2,0},{3,1},{4,6},{5,7},{6,4},{7,5},{8,10},{9,11},{10,... | collective-permute-start | bytes 884744 | tf_op jit(solution)/shard_map/ppermute | solution.py:266
  34.2 25.2 %collective-permute-start.8 = (bf16[144,1024]{1,0:T(8,128)(2,1)S(1)}, bf16[144,1024]{1,0:T(8,128)(2,1)S(1)}, u32[]{:S(2)}, u32[]{:S(2)}) collective-permute-start(bf16[144,1024]{1,0:T(8,128)(2,1)S(1)} %shard_map.129.refs_1_.refs_4_), channel_id=1, source_target_pairs={{0,3},{1,2},{2,1},{3,0},{4,7},{5,6},{6,5},{7,4},{8,11},{9,10},{10,... | collective-permute-start | bytes 884744 | tf_op jit(solution)/shard_map/ppermute | solution.py:266
  34.7 9.3 %collective-permute-start.9 = (bf16[256,512]{1,0:T(8,128)(2,1)S(1)}, bf16[256,512]{1,0:T(8,128)(2,1)S(1)}, u32[]{:S(2)}, u32[]{:S(2)}) collective-permute-start(bf16[256,512]{1,0:T(8,128)(2,1)S(1)} %pad_maximum_fusion), channel_id=1, source_target_pairs={{0,4},{4,0},{8,12},{12,8},{16,24},{20,28},{24,16},{28,20},{1,5},{5... | collective-permute-start | bytes 786440 | tf_op jit(solution)/shard_map/ppermute | solution.py:630
  59.4 5.7 %collective-permute-start.10 = (bf16[1024,1024]{1,0:T(8,128)(2,1)S(1)}, bf16[1024,1024]{1,0:T(8,128)(2,1)S(1)}, u32[]{:S(2)}, u32[]{:S(2)}) collective-permute-start(bf16[1024,1024]{1,0:T(8,128)(2,1)S(1)} %collective-permute-done.3.near), channel_id=1, source_target_pairs={{0,16},{16,0},{1,17},{17,1},{2,18},{18,2},{3,19},{19,3},{4,20},{20... | collective-permute-start | bytes 6291464 | tf_op jit(solution)/shard_map/ppermute | solution.py:266
  59.4 5.7 %collective-permute-start.11 = (bf16[512,1024]{1,0:T(8,128)(2,1)S(1)}, bf16[512,1024]{1,0:T(8,128)(2,1)S(1)}, u32[]{:S(2)}, u32[]{:S(2)}) collective-permute-start(bf16[512,1024]{1,0:T(8,128)(2,1)S(1)} %collective-permute-done.5.across), channel_id=1, source_target_pairs={{0,16},{16,0},{1,17},{17,1},{2,18},{18,2},{3,19},{19,3},{4,20},{20... | collective-permute-start | bytes 3145736 | tf_op jit(solution)/shard_map/ppermute | solution.py:266
  61.2 6.7 %collective-permute-start.12 = (f32[8,1024]{1,0:T(8,128)S(1)}, f32[8,1024]{1,0:T(8,128)S(1)}, u32[]{:S(2)}, u32[]{:S(2)}) collective-permute-start(f32[8,1024]{1,0:T(8,128)S(1)} %get-tuple-element.60.router_a), channel_id=1, source_target_pairs={{0,16},{16,0},{1,17},{17,1},{2,18},{18,2},{3,19},{19,3},{4,20},{20... | collective-permute-start | bytes 98312 | tf_op jit(solution)/shard_map/ppermute | solution.py:266
  70.7 7.3 %collective-permute-start.13 = (bf16[144,512]{1,0:T(8,128)(2,1)S(1)}, bf16[144,512]{1,0:T(8,128)(2,1)S(1)}, u32[]{:S(2)}, u32[]{:S(2)}) collective-permute-start(bf16[144,512]{1,0:T(8,128)(2,1)S(1)} %get-tuple-element.67), channel_id=1, source_target_pairs={{0,8},{4,12},{8,0},{12,4},{16,20},{20,16},{24,28},{28,24},{1,9},{5... | collective-permute-start | bytes 442376 | tf_op jit(solution)/shard_map/ppermute | solution.py:630
  71.8 6.8 %collective-permute-start.14 = (bf16[144,512]{1,0:T(8,128)(2,1)S(1)}, bf16[144,512]{1,0:T(8,128)(2,1)S(1)}, u32[]{:S(2)}, u32[]{:S(2)}) collective-permute-start(bf16[144,512]{1,0:T(8,128)(2,1)S(1)} %get-tuple-element.68), channel_id=1, source_target_pairs={{0,4},{4,0},{8,12},{12,8},{16,24},{20,28},{24,16},{28,20},{1,5},{5... | collective-permute-start | bytes 442376 | tf_op jit(solution)/shard_map/ppermute | solution.py:630
  72.3 8.3 %collective-permute-start.15 = (bf16[144,512]{1,0:T(8,128)(2,1)S(1)}, bf16[144,512]{1,0:T(8,128)(2,1)S(1)}, u32[]{:S(2)}, u32[]{:S(2)}) collective-permute-start(bf16[144,512]{1,0:T(8,128)(2,1)S(1)} %get-tuple-element.69), channel_id=1, source_target_pairs={{0,12},{4,8},{8,4},{12,0},{16,28},{20,24},{24,20},{28,16},{1,13},{... | collective-permute-start | bytes 442376 | tf_op jit(solution)/shard_map/ppermute | solution.py:630

commit v6 on v5

--- a/solution.py
+++ b/solution.py
@@ -252,7 +252,7 @@
     return (query_grad[None], key_grad[None], value_grad[None], router_grad, expert_grad[None])
 
 
-VMEM_LIMIT = 16 * 1024 * 1024
+VMEM_LIMIT = 24 * 1024 * 1024
 NT = (((1,), (1,)), ((), ()))
 TN = (((0,), (0,)), ((), ()))
 LANES = 128
@@ -416,38 +416,18 @@
 def project_kernel(meta, own, near, across, *refs):
     grads, resids, total, rows = refs[0:4], refs[4:8], refs[8], refs[9]
     my_core, my_seq, my_expert = meta[0], meta[1], meta[2]
-    step = pl.program_id(0)
     tok_rows = grads[0].shape[0]
-    width = own.shape[1]
-
-    @pl.when(step == 0)
-    def _():
-        total[...] = jnp.zeros_like(total)
-        for k in range(4):
-            rows[my_expert ^ k, 0:tok_rows] = grads[k][...]
-            rows[my_expert ^ k, tok_rows:] = resids[k][...]
-
-    columns = pl.ds(pl.multiple_of(step * width, LANES), width)
-    total[...] += times(rows[my_seq, :, columns], own[...]) + times(
-        rows[my_seq ^ (1 + my_core), :, columns], near[...]
-    )
-    here = half_of(my_core, across.shape[0])
-    total[:, here] += times(rows[my_seq ^ 3, :, columns], across[...])
+    for k in range(4):
+        rows[my_expert ^ k, 0:tok_rows] = grads[k][...]
+        rows[my_expert ^ k, tok_rows:] = resids[k][...]
+    total[...] = times(rows[my_seq], own[...]) + times(rows[my_seq ^ (1 + my_core)], near[...])
+    total[:, half_of(my_core, across.shape[0])] += times(rows[my_seq ^ 3], across[...])
 
 
 def project_rest_kernel(meta, far, across, rows, most, total):
     my_core, my_seq = meta[0], meta[1]
-    step = pl.program_id(0)
-    width = far.shape[1]
-
-    @pl.when(step == 0)
-    def _():
-        total[...] = most[...]
-
-    columns = pl.ds(pl.multiple_of(step * width, LANES), width)
-    total[...] += times(rows[my_seq ^ (2 - my_core), :, columns], far[...])
-    here = half_of(1 - my_core, across.shape[0])
-    total[:, here] += times(rows[my_seq ^ 3, :, columns], across[...])
+    total[...] = most[...] + times(rows[my_seq ^ (2 - my_core)], far[...])
+    total[:, half_of(1 - my_core, across.shape[0])] += times(rows[my_seq ^ 3], across[...])
 
 
 def stacked(matrix, heads):
@@ -673,7 +653,6 @@
             (query.shape, f32),
         ),
     )
-    steps = 4
     model_rows = o_weight.shape[0]
     all_rows = 2 * tok_rows + ROW_TILE
     across_mine, resids[1:], probs, attn_out, weight_near = lax.optimization_barrier(
@@ -682,35 +661,17 @@
     weight_far = partner(weight_near, "dp", dp_n, 1)
     across_other = partner(across_mine, "dp", dp_n, 1)
     all_shape = (all_rows, model_rows)
-    rows_shape = (expert_n, all_rows, feats)
-
-    def project(kernel, weights, in_place, shapes):
-        return pl.pallas_call(
-            kernel,
-            out_shape=shapes,
-            grid_spec=pltpu.PrefetchScalarGridSpec(
-                num_scalar_prefetch=1,
-                grid=(steps,),
-                in_specs=[
-                    pl.BlockSpec((w.shape[0], feats // steps), lambda i, m: (0, i)) for w in weights
-                ]
-                + [pl.BlockSpec(memory_space=pltpu.VMEM)] * len(in_place),
-                out_specs=[whole(s.shape) for s in shapes],
-            ),
-            compiler_params=params(),
-        )(meta, *weights, *in_place)
-
-    most, staged = project(
+    most, staged = call(
         project_kernel,
-        (o_weight, weight_near, across_mine),
-        (*grads, *resids),
-        [jax.ShapeDtypeStruct(all_shape, f32), jax.ShapeDtypeStruct(rows_shape, bf16)],
-    )
-    (projected,) = project(
+        meta,
+        (o_weight, weight_near, across_mine, *grads, *resids),
+        ((all_shape, f32), ((expert_n, all_rows, feats), bf16)),
+    )
+    (projected,) = call(
         project_rest_kernel,
-        (weight_far, across_other),
-        (staged, most),
-        [jax.ShapeDtypeStruct(all_shape, f32)],
+        meta,
+        (weight_far, across_other, staged, most),
+        ((all_shape, f32),),
     )
     total_tokens = dp_n * seq_n * tok_rows
     columns, router_part = call(

time: 82.2 us -> 80.6 us (0.981)
  Pallas kernels: 18.7 us -> 16 us
  waiting for transfers between devices: 36.7 us -> 37.9 us
    pallas_call x2 -> x0, Pallas kernels: 6.63 us -> none  [project(): pl.pallas_call(kernel, out_shape=shapes, grid_spec=pltpu.PrefetchScalarGr...]
    pallas_call x7 -> x9, Pallas kernels: 12.1 us -> 16 us  [call(): pl.pallas_call(kernel, out_shape=shapes, in_specs=[pl.BlockSpec(memory_sp...]
    ppermute x9, waiting for transfers between devices: 24.5 us -> 26.1 us  [partner(): return lax.ppermute(array, axis, [(i, i ^ distance) for i in range(count)])]
  transfers between devices with their start and end apart: 16 -> 16, of which waited for: 9 -> 10; matrix products, arithmetic and copies ran while one was open for 6% -> 6% of each run, Pallas kernels for 18% -> 15%
where the time goes in v6:
time: 80.6 us; the launch traced here: 80.3 us
  waiting for transfers between devices  37.9 us (47%)
  starting transfers between devices  17.3 us (21%)
  Pallas kernels  16 us (20%)
  local copies, waits for them, and re-layouts  7.34 us (9%)
  other arithmetic  0.97 us (1%)
    ppermute x9, waiting for transfers between devices, partner(): return lax.ppermute(array, axis, [(i, i ^ distance) for i in range(count)])  26.1 us
    pallas_call x9, Pallas kernels, call(): pl.pallas_call(kernel, out_shape=shapes, in_specs=[pl.BlockSpec(memory_sp...  16 us
    ppermute x7, waiting for transfers between devices, over_both(): return lax.ppermute(array, ('dp', 'seq'), pairs)  11.9 us
    ppermute x7, starting transfers between devices, over_both(): return lax.ppermute(array, ('dp', 'seq'), pairs)  9.77 us
    ppermute x9, starting transfers between devices, partner(): return lax.ppermute(array, axis, [(i, i ^ distance) for i in range(count)])  7.57 us
    unnamed x22, local copies, waits for them, and re-layouts  5.52 us
    pad x1, local copies, waits for them, and re-layouts, local_fast(): jnp.pad(router_weight, ((0, 0), (0, LANES - router_weight.shape[1])))  1.75 us
  transfers between devices with their start and end apart: 16, of which 10 were waited for; matrix products, arithmetic and copies ran while one was open for 6% of the time, Pallas kernels for 15%

profile of v6, /device:TPU:8, one launch (start us, length us, event | category | flops | bytes accessed | tf_op | source)
XLA Modules:
  0.0 80.3 jit_solution(16356002769205798258)
XLA Ops:
  0.6 1.6 %collective-permute-start.3 = (bf16[1024,1024]{1,0:T(8,128)(2,1)}, bf16[1024,1024]{1,0:T(8,128)(2,1)S(1)}, u32[]{:S(2)}, u32[]{:S(2)}) collective-permute-start(bf16[1024,1024]{1,0:T(8,128)(2,1)} %own.1), channel_id=1, source_target_pairs={{0,4},{4,0},{8,12},{12,8},{16,24},{20,28},{24,16},{28,20},{1,5},{5... | collective-permute-start | bytes 6291464 | tf_op jit(solution)/shard_map/ppermute | solution.py:610
  2.6 2.6 %collective-permute-start.1 = (bf16[128,1024]{1,0:T(8,128)(2,1)}, bf16[128,1024]{1,0:T(8,128)(2,1)S(1)}, u32[]{:S(2)}, u32[]{:S(2)}) collective-permute-start(bf16[128,1024]{1,0:T(8,128)(2,1)} %bitcast.17), channel_id=1, source_target_pairs={{0,2},{1,3},{2,0},{3,1},{4,6},{5,7},{6,4},{7,5},{8,10},{9,11},{10,... | collective-permute-start | bytes 786440 | tf_op jit(solution)/shard_map/ppermute | solution.py:266
  5.7 0.9 %pad_maximum_fusion.1.pair = bf16[128,512]{1,0:T(8,128)(2,1)S(1)} fusion(bf16[128,256]{1,0:T(8,128)(2,1)} %bitcast.31, bf16[128,256]{1,0:T(8,128)(2,1)} %bitcast.33), kind=kLoop, calls=%fused_computation.1 | loop fusion | flops 262144 | bytes 262144 | tf_op jit(solution)/shard_map/concatenate | solution.py:615
  6.6 1.6 %collective-permute-start.4 = (bf16[128,512]{1,0:T(8,128)(2,1)S(1)}, bf16[128,512]{1,0:T(8,128)(2,1)S(1)}, u32[]{:S(2)}, u32[]{:S(2)}) collective-permute-start(bf16[128,512]{1,0:T(8,128)(2,1)S(1)} %pad_maximum_fusion.1.pair), channel_id=1, source_target_pairs={{0,8},{4,12},{8,0},{12,4},{16,20},{20,16},{24,28},{28,24},{1,9},{5... | collective-permute-start | bytes 393224 | tf_op jit(solution)/shard_map/ppermute | solution.py:610
  8.1 0.8 copy.14
  8.9 1.6 %copy.15 = bf16[1024,4]{1,0:T(8,128)(2,1)} copy(bf16[1024,4]{0,1:T(4,128)(2,1)} %param.15) | data formatting | bytes 16384 | tf_op args[6]
  10.5 1.7 %pad.8.router_pad = bf16[1024,128]{1,0:T(8,128)(2,1)} pad(bf16[1024,4]{1,0:T(8,128)(2,1)} %copy.15, bf16[]{:T(256)} %constant.17.clone.1), padding=0_0x0_124 | pad | bytes 270338 | tf_op jit(solution)/shard_map/jit(_pad)/pad | solution.py:618
  12.3 1.2 %copy-done.2 = bf16[1,128,4096]{2,1,0:T(8,128)(2,1)S(1)} copy-done((bf16[1,128,4096]{2,1,0:T(8,128)(2,1)S(1)}, bf16[1,128,4096]{2,1,0:T(8,128)(2,1)}, u32[]{:S(2)}) %copy-start.2) | copy-done | bytes 1048600
  13.6 0.9 %copy-done.3 = bf16[1,128,1024]{2,1,0:T(8,128)(2,1)S(1)} copy-done((bf16[1,128,1024]{2,1,0:T(8,128)(2,1)S(1)}, bf16[1,128,1024]{2,1,0:T(8,128)(2,1)}, u32[]{:S(2)}) %copy-start.3) | copy-done | bytes 262168
  14.5 0.9 %copy-done.6 = bf16[1024,128]{1,0:T(8,128)(2,1)S(1)} copy-done((bf16[1024,128]{1,0:T(8,128)(2,1)S(1)}, bf16[1024,128]{1,0:T(8,128)(2,1)}, u32[]{:S(2)}) %copy-start.6) | copy-done | bytes 262168
  15.5 1.3 %shard_map.128 = (f32[8,128]{1,0:T(8,128)S(1)}, bf16[128,128]{1,0:T(8,128)(2,1)S(1)}, bf16[128,4096]{1,0:T(8,128)(2,1)S(1)}) custom-call(s32[3]{0:T(128)S(1)} %pad_add_fusion.meta, s32[128,2]{1,0:T(8,128)S(1)} %bitcast.22, bf16[1024,128]{1,0:T(8,128)(2,1)S(1)} %copy-done.6, bf16[128,1024]{1,0:T(8,128)(2,1)S(1)} %bitcast.26, bf16[128,4096]{1,0:T(8,128)(2,1)S(1)} %bitcast.25), custom_call_target="tpu_custom_call" | custom-call | tf_op jit(solution)/shard_map/pallas_call | solution.py:575
  16.8 6.7 %collective-permute-done.1.refs_2_ = bf16[128,1024]{1,0:T(8,128)(2,1)S(1)} collective-permute-done((bf16[128,1024]{1,0:T(8,128)(2,1)}, bf16[128,1024]{1,0:T(8,128)(2,1)S(1)}, u32[]{:S(2)}, u32[]{:S(2)}) %collective-permute-start.1) | collective-permute-done | bytes 262176 | tf_op jit(solution)/shard_map/ppermute | solution.py:266
  23.5 4.8 %collective-permute-done.2.refs_3_ = bf16[128,1024]{1,0:T(8,128)(2,1)S(1)} collective-permute-done((bf16[128,1024]{1,0:T(8,128)(2,1)}, bf16[128,1024]{1,0:T(8,128)(2,1)S(1)}, u32[]{:S(2)}, u32[]{:S(2)}) %collective-permute-start.2) | collective-permute-done | bytes 262176 | tf_op jit(solution)/shard_map/ppermute | solution.py:266
  28.4 1.6 %collective-permute-start.5 = (bf16[512,1024]{1,0:T(8,128)(2,1)S(1)}, bf16[512,1024]{1,0:T(8,128)(2,1)S(1)}, u32[]{:S(2)}, u32[]{:S(2)}) collective-permute-start(bf16[512,1024]{1,0:T(8,128)(2,1)S(1)} %constant_dynamic-slice_fusion), channel_id=1, source_target_pairs={{0,8},{4,12},{8,0},{12,4},{16,20},{20,16},{24,28},{28,24},{1,9},{5... | collective-permute-start | bytes 3145736 | tf_op jit(solution)/shard_map/ppermute | solution.py:610
  30.1 1.1 %shard_map.129.refs_1_.refs_4_ = bf16[144,1024]{1,0:T(8,128)(2,1)S(1)} custom-call(s32[3]{0:T(128)S(1)} %pad_add_fusion.meta, s32[128,2]{1,0:T(8,128)S(1)} %bitcast.23, f32[8,128]{1,0:T(8,128)S(1)} %get-tuple-element.43.rows, bf16[128,4096]{1,0:T(8,128)(2,1)S(1)} %get-tuple-element.44.saved_tok, bf16[128,1024]{1,0:T(8,128)(2,1)S(1)} %bitcast.27, ...), custom_call_target="tpu_custom_call" | custom-call | tf_op jit(solution)/shard_map/pallas_call | solution.py:575
  31.6 2.6 %collective-permute-start.7 = (bf16[144,1024]{1,0:T(8,128)(2,1)S(1)}, bf16[144,1024]{1,0:T(8,128)(2,1)S(1)}, u32[]{:S(2)}, u32[]{:S(2)}) collective-permute-start(bf16[144,1024]{1,0:T(8,128)(2,1)S(1)} %shard_map.129.refs_1_.refs_4_), channel_id=1, source_target_pairs={{0,2},{1,3},{2,0},{3,1},{4,6},{5,7},{6,4},{7,5},{8,10},{9,11},{10,... | collective-permute-start | bytes 884744 | tf_op jit(solution)/shard_map/ppermute | solution.py:266
  34.7 1.6 %collective-permute-start.9 = (bf16[256,512]{1,0:T(8,128)(2,1)S(1)}, bf16[256,512]{1,0:T(8,128)(2,1)S(1)}, u32[]{:S(2)}, u32[]{:S(2)}) collective-permute-start(bf16[256,512]{1,0:T(8,128)(2,1)S(1)} %pad_maximum_fusion), channel_id=1, source_target_pairs={{0,4},{4,0},{8,12},{12,8},{16,24},{20,28},{24,16},{28,20},{1,5},{5... | collective-permute-start | bytes 786440 | tf_op jit(solution)/shard_map/ppermute | solution.py:610
  36.3 7.8 %collective-permute-done.9.pair_y = bf16[256,512]{1,0:T(8,128)(2,1)S(1)} collective-permute-done((bf16[256,512]{1,0:T(8,128)(2,1)S(1)}, bf16[256,512]{1,0:T(8,128)(2,1)S(1)}, u32[]{:S(2)}, u32[]{:S(2)}) %collective-permute-start.9) | collective-permute-done | bytes 262176 | tf_op jit(solution)/shard_map/ppermute | solution.py:610
  44.0 2.4 %shard_map.130 = (f32[2,512,512]{2,1,0:T(8,128)S(1)}, f32[128,1024]{1,0:T(8,128)S(1)}) custom-call(s32[3]{0:T(128)S(1)} %pad_add_fusion.meta, bf16[128,1024]{1,0:T(8,128)(2,1)S(1)} %bitcast.28, bf16[128,512]{1,0:T(8,128)(2,1)S(1)} %pad_maximum_fusion.1.pair, bf16[128,512]{1,0:T(8,128)(2,1)S(1)} %collective-permute-done.4.pair_x, ...), custom_call_target="tpu_custom_call" | custom-call | tf_op jit(solution)/shard_map/pallas_call | solution.py:575
  46.4 7.9 %collective-permute-done.7.refs_3_.refs_6_ = bf16[144,1024]{1,0:T(8,128)(2,1)S(1)} collective-permute-done((bf16[144,1024]{1,0:T(8,128)(2,1)S(1)}, bf16[144,1024]{1,0:T(8,128)(2,1)S(1)}, u32[]{:S(2)}, u32[]{:S(2)}) %collective-permute-start.7) | collective-permute-done | bytes 294944 | tf_op jit(solution)/shard_map/ppermute | solution.py:266
  54.3 5.1 %collective-permute-done.8.refs_4_.refs_7_ = bf16[144,1024]{1,0:T(8,128)(2,1)S(1)} collective-permute-done((bf16[144,1024]{1,0:T(8,128)(2,1)S(1)}, bf16[144,1024]{1,0:T(8,128)(2,1)S(1)}, u32[]{:S(2)}, u32[]{:S(2)}) %collective-permute-start.8) | collective-permute-done | bytes 294944 | tf_op jit(solution)/shard_map/ppermute | solution.py:266
  59.9 1.3 %shard_map.131 = (f32[128,128]{1,0:T(8,128)S(1)}, f32[8,1024]{1,0:T(8,128)S(1)}) custom-call(s32[3]{0:T(128)S(1)} %pad_add_fusion.meta, s32[128,2]{1,0:T(8,128)S(1)} %bitcast.24, bf16[144,1024]{1,0:T(8,128)(2,1)S(1)} %shard_map.129.refs_1_.refs_4_, bf16[144,1024]{1,0:T(8,128)(2,1)S(1)} %collective-permute-done.6.refs_2_.refs_5_, ...), custom_call_target="tpu_custom_call" | custom-call | tf_op jit(solution)/shard_map/pallas_call | solution.py:575
  61.2 2.3 %shard_map.132 = (f32[272,1024]{1,0:T(8,128)S(1)}, bf16[4,272,1024]{2,1,0:T(8,128)(2,1)S(1)}) custom-call(s32[3]{0:T(128)S(1)} %pad_add_fusion.meta, bf16[1024,1024]{1,0:T(8,128)(2,1)S(1)} %copy-done.1, bf16[1024,1024]{1,0:T(8,128)(2,1)S(1)} %collective-permute-done.3.near, bf16[512,1024]{1,0:T(8,128)(2,1)S(1)} %collective-permute-done.5.across, ...), custom_call_target="tpu_custom_call" | custom-call | tf_op jit(solution)/shard_map/pallas_call | solution.py:575
  63.5 1.6 %collective-permute-done.11.across = bf16[512,1024]{1,0:T(8,128)(2,1)S(1)} collective-permute-done((bf16[512,1024]{1,0:T(8,128)(2,1)S(1)}, bf16[512,1024]{1,0:T(8,128)(2,1)S(1)}, u32[]{:S(2)}, u32[]{:S(2)}) %collective-permute-start.11) | collective-permute-done | bytes 1048608 | tf_op jit(solution)/shard_map/ppermute | solution.py:266
  65.1 1.6 %shard_map.133.projected = f32[272,1024]{1,0:T(8,128)S(1)} custom-call(s32[3]{0:T(128)S(1)} %pad_add_fusion.meta, bf16[1024,1024]{1,0:T(8,128)(2,1)S(1)} %collective-permute-done.10.far, bf16[512,1024]{1,0:T(8,128)(2,1)S(1)} %collective-permute-done.11.across, bf16[4,272,1024]{2,1,0:T(8,128)(2,1)S(1)} %get-tuple-element.58.rows, ...), custom_call_target="tpu_custom_call" | custom-call | tf_op jit(solution)/shard_map/pallas_call | solution.py:575
  66.7 2.8 %shard_map.134 = (bf16[128,1024]{1,0:T(8,128)(2,1)}, bf16[16,512]{1,0:T(8,128)(2,1)S(1)}, f32[128,512]{1,0:T(8,128)S(1)}, bf16[144,512]{1,0:T(8,128)(2,1)S(1)}, ...) custom-call(s32[3]{0:T(128)S(1)} %pad_add_fusion.meta, f32[128,128]{1,0:T(8,128)S(1)} %get-tuple-element.73.columns, ...), custom_call_target="tpu_custom_call" | custom-call | tf_op jit(solution)/shard_map/pallas_call | solution.py:575
  69.5 1.1 %collective-permute-start.13 = (bf16[144,512]{1,0:T(8,128)(2,1)S(1)}, bf16[144,512]{1,0:T(8,128)(2,1)S(1)}, u32[]{:S(2)}, u32[]{:S(2)}) collective-permute-start(bf16[144,512]{1,0:T(8,128)(2,1)S(1)} %get-tuple-element.67), channel_id=1, source_target_pairs={{0,8},{4,12},{8,0},{12,4},{16,20},{20,16},{24,28},{28,24},{1,9},{5... | collective-permute-start | bytes 442376 | tf_op jit(solution)/shard_map/ppermute | solution.py:610
  71.1 1.9 %collective-permute-start.15 = (bf16[144,512]{1,0:T(8,128)(2,1)S(1)}, bf16[144,512]{1,0:T(8,128)(2,1)S(1)}, u32[]{:S(2)}, u32[]{:S(2)}) collective-permute-start(bf16[144,512]{1,0:T(8,128)(2,1)S(1)} %get-tuple-element.69), channel_id=1, source_target_pairs={{0,12},{4,8},{8,4},{12,0},{16,28},{20,24},{24,20},{28,16},{1,13},{... | collective-permute-start | bytes 442376 | tf_op jit(solution)/shard_map/ppermute | solution.py:610
  73.0 2.0 %shard_map.136 = bf16[128,4096]{1,0:T(8,128)(2,1)} custom-call(s32[3]{0:T(128)S(1)} %pad_add_fusion.meta, f32[128,128]{1,0:T(8,128)S(1)} %get-tuple-element.73.columns, bf16[128,128]{1,0:T(8,128)(2,1)S(1)} %get-tuple-element.74.place, bf16[128,1024]{1,0:T(8,128)(2,1)S(1)} %bitcast.21, bf16[128,1024]{1,0:T(8,128)(2,1)S(1)} %collective-permute-done.refs_1_, ...), custom_call_target="tpu_custom_call" | custom-call | tf_op jit(solution)/shard_map/pallas_call | solution.py:575
  75.0 1.8 %collective-permute-done.13.t1 = bf16[144,512]{1,0:T(8,128)(2,1)S(1)} collective-permute-done((bf16[144,512]{1,0:T(8,128)(2,1)S(1)}, bf16[144,512]{1,0:T(8,128)(2,1)S(1)}, u32[]{:S(2)}, u32[]{:S(2)}) %collective-permute-start.13) | collective-permute-done | bytes 147488 | tf_op jit(solution)/shard_map/ppermute | solution.py:610
  77.0 2.1 %collective-permute-done.15.t3 = bf16[144,512]{1,0:T(8,128)(2,1)S(1)} collective-permute-done((bf16[144,512]{1,0:T(8,128)(2,1)S(1)}, bf16[144,512]{1,0:T(8,128)(2,1)S(1)}, u32[]{:S(2)}, u32[]{:S(2)}) %collective-permute-start.15) | collective-permute-done | bytes 147488 | tf_op jit(solution)/shard_map/ppermute | solution.py:610
  79.1 1.2 %shard_map.135 = (bf16[128,256]{1,0:T(8,128)(2,1)}, bf16[128,256]{1,0:T(8,128)(2,1)}, f32[4,1024]{1,0:T(4,128)}) custom-call(s32[3]{0:T(128)S(1)} %pad_add_fusion.meta, bf16[16,512]{1,0:T(8,128)(2,1)S(1)} %get-tuple-element.64.router, f32[128,512]{1,0:T(8,128)S(1)} %get-tuple-element.66.own, bf16[144,512]{1,0:T(8,128)(2,1)S(1)} %collective-permute-done.13.t1, ...), custom_call_target="tpu_custom_call" | custom-call | tf_op jit(solution)/shard_map/pallas_call | solution.py:575
  (37 shorter events, 3.4 us)
Async XLA Ops:
  0.6 27.7 %collective-permute-start.3 = (bf16[1024,1024]{1,0:T(8,128)(2,1)}, bf16[1024,1024]{1,0:T(8,128)(2,1)S(1)}, u32[]{:S(2)}, u32[]{:S(2)}) collective-permute-start(bf16[1024,1024]{1,0:T(8,128)(2,1)} %own.1), channel_id=1, source_target_pairs={{0,4},{4,0},{8,12},{12,8},{16,24},{20,28},{24,16},{28,20},{1,5},{5... | collective-permute-start | bytes 6291464 | tf_op jit(solution)/shard_map/ppermute | solution.py:610
  2.2 14.6 %collective-permute-start = (bf16[128,1024]{1,0:T(8,128)(2,1)}, bf16[128,1024]{1,0:T(8,128)(2,1)S(1)}, u32[]{:S(2)}, u32[]{:S(2)}) collective-permute-start(bf16[128,1024]{1,0:T(8,128)(2,1)} %bitcast.16), channel_id=1, source_target_pairs={{0,1},{1,0},{2,3},{3,2},{4,5},{5,4},{6,7},{7,6},{8,9},{9,8},{10,11... | collective-permute-start | bytes 786440 | tf_op jit(solution)/shard_map/ppermute | solution.py:266
  2.6 20.9 %collective-permute-start.1 = (bf16[128,1024]{1,0:T(8,128)(2,1)}, bf16[128,1024]{1,0:T(8,128)(2,1)S(1)}, u32[]{:S(2)}, u32[]{:S(2)}) collective-permute-start(bf16[128,1024]{1,0:T(8,128)(2,1)} %bitcast.17), channel_id=1, source_target_pairs={{0,2},{1,3},{2,0},{3,1},{4,6},{5,7},{6,4},{7,5},{8,10},{9,11},{10,... | collective-permute-start | bytes 786440 | tf_op jit(solution)/shard_map/ppermute | solution.py:266
  5.2 23.1 %collective-permute-start.2 = (bf16[128,1024]{1,0:T(8,128)(2,1)}, bf16[128,1024]{1,0:T(8,128)(2,1)S(1)}, u32[]{:S(2)}, u32[]{:S(2)}) collective-permute-start(bf16[128,1024]{1,0:T(8,128)(2,1)} %bitcast.18), channel_id=1, source_target_pairs={{0,3},{1,2},{2,1},{3,0},{4,7},{5,6},{6,5},{7,4},{8,11},{9,10},{10,... | collective-permute-start | bytes 786440 | tf_op jit(solution)/shard_map/ppermute | solution.py:266
  6.6 10.2 %collective-permute-start.4 = (bf16[128,512]{1,0:T(8,128)(2,1)S(1)}, bf16[128,512]{1,0:T(8,128)(2,1)S(1)}, u32[]{:S(2)}, u32[]{:S(2)}) collective-permute-start(bf16[128,512]{1,0:T(8,128)(2,1)S(1)} %pad_maximum_fusion.1.pair), channel_id=1, source_target_pairs={{0,8},{4,12},{8,0},{12,4},{16,20},{20,16},{24,28},{28,24},{1,9},{5... | collective-permute-start | bytes 393224 | tf_op jit(solution)/shard_map/ppermute | solution.py:610
  10.5 19.5 %copy-start.9 = (bf16[1024,4]{0,1:T(4,128)(2,1)S(1)}, bf16[1024,4]{0,1:T(4,128)(2,1)}, u32[]{:S(2)}) copy-start(bf16[1024,4]{0,1:T(4,128)(2,1)} %param.15) | copy-start | bytes 24580
  10.5 19.5 %copy-start = (bf16[1,128,1024]{2,1,0:T(8,128)(2,1)S(1)}, bf16[1,128,1024]{2,1,0:T(8,128)(2,1)}, u32[]{:S(2)}) copy-start(bf16[1,128,1024]{2,1,0:T(8,128)(2,1)} %param.13) | copy-start | bytes 786436
  12.3 1.2 %copy-start.2 = (bf16[1,128,4096]{2,1,0:T(8,128)(2,1)S(1)}, bf16[1,128,4096]{2,1,0:T(8,128)(2,1)}, u32[]{:S(2)}) copy-start(bf16[1,128,4096]{2,1,0:T(8,128)(2,1)} %param.17) | copy-start | bytes 3145732
  13.6 0.9 %copy-start.3 = (bf16[1,128,1024]{2,1,0:T(8,128)(2,1)S(1)}, bf16[1,128,1024]{2,1,0:T(8,128)(2,1)}, u32[]{:S(2)}) copy-start(bf16[1,128,1024]{2,1,0:T(8,128)(2,1)} %param.12) | copy-start | bytes 786436
  14.5 0.9 %copy-start.6 = (bf16[1024,128]{1,0:T(8,128)(2,1)S(1)}, bf16[1024,128]{1,0:T(8,128)(2,1)}, u32[]{:S(2)}) copy-start(bf16[1024,128]{1,0:T(8,128)(2,1)} %pad.8.router_pad) | copy-start | bytes 786436
  15.5 14.6 %copy-start.4 = (bf16[1,128,1024]{2,1,0:T(8,128)(2,1)S(1)}, bf16[1,128,1024]{2,1,0:T(8,128)(2,1)}, u32[]{:S(2)}) copy-start(bf16[1,128,1024]{2,1,0:T(8,128)(2,1)} %param.12) | copy-start | bytes 786436
  28.3 6.3 %copy-start.7 = (bf16[1,128,256]{2,1,0:T(8,128)(2,1)S(1)}, bf16[1,128,256]{2,1,0:T(8,128)(2,1)}, u32[]{:S(2)}) copy-start(bf16[1,128,256]{2,1,0:T(8,128)(2,1)} %param.11) | copy-start | bytes 196612
  28.3 6.3 %copy-start.8 = (bf16[1,128,256]{2,1,0:T(8,128)(2,1)S(1)}, bf16[1,128,256]{2,1,0:T(8,128)(2,1)}, u32[]{:S(2)}) copy-start(bf16[1,128,256]{2,1,0:T(8,128)(2,1)} %param.10) | copy-start | bytes 196612
  28.4 15.6 %copy-start.5 = (bf16[1,128,1024]{2,1,0:T(8,128)(2,1)S(1)}, bf16[1,128,1024]{2,1,0:T(8,128)(2,1)}, u32[]{:S(2)}) copy-start(bf16[1,128,1024]{2,1,0:T(8,128)(2,1)} %param.9) | copy-start | bytes 786436
  28.4 31.0 %collective-permute-start.5 = (bf16[512,1024]{1,0:T(8,128)(2,1)S(1)}, bf16[512,1024]{1,0:T(8,128)(2,1)S(1)}, u32[]{:S(2)}, u32[]{:S(2)}) collective-permute-start(bf16[512,1024]{1,0:T(8,128)(2,1)S(1)} %constant_dynamic-slice_fusion), channel_id=1, source_target_pairs={{0,8},{4,12},{8,0},{12,4},{16,20},{20,16},{24,28},{28,24},{1,9},{5... | collective-permute-start | bytes 3145736 | tf_op jit(solution)/shard_map/ppermute | solution.py:610
  30.1 31.2 %copy-start.1 = (bf16[1024,1024]{1,0:T(8,128)(2,1)S(1)}, bf16[1024,1024]{1,0:T(8,128)(2,1)}, u32[]{:S(2)}) copy-start(bf16[1024,1024]{1,0:T(8,128)(2,1)} %own.1) | copy-start | bytes 6291460
  31.1 15.3 %collective-permute-start.6 = (bf16[144,1024]{1,0:T(8,128)(2,1)S(1)}, bf16[144,1024]{1,0:T(8,128)(2,1)S(1)}, u32[]{:S(2)}, u32[]{:S(2)}) collective-permute-start(bf16[144,1024]{1,0:T(8,128)(2,1)S(1)} %shard_map.129.refs_1_.refs_4_), channel_id=1, source_target_pairs={{0,1},{1,0},{2,3},{3,2},{4,5},{5,4},{6,7},{7,6},{8,9},{9,8},{10,11... | collective-permute-start | bytes 884744 | tf_op jit(solution)/shard_map/ppermute | solution.py:266
  31.6 22.7 %collective-permute-start.7 = (bf16[144,1024]{1,0:T(8,128)(2,1)S(1)}, bf16[144,1024]{1,0:T(8,128)(2,1)S(1)}, u32[]{:S(2)}, u32[]{:S(2)}) collective-permute-start(bf16[144,1024]{1,0:T(8,128)(2,1)S(1)} %shard_map.129.refs_1_.refs_4_), channel_id=1, source_target_pairs={{0,2},{1,3},{2,0},{3,1},{4,6},{5,7},{6,4},{7,5},{8,10},{9,11},{10,... | collective-permute-start | bytes 884744 | tf_op jit(solution)/shard_map/ppermute | solution.py:266
  34.2 25.2 %collective-permute-start.8 = (bf16[144,1024]{1,0:T(8,128)(2,1)S(1)}, bf16[144,1024]{1,0:T(8,128)(2,1)S(1)}, u32[]{:S(2)}, u32[]{:S(2)}) collective-permute-start(bf16[144,1024]{1,0:T(8,128)(2,1)S(1)} %shard_map.129.refs_1_.refs_4_), channel_id=1, source_target_pairs={{0,3},{1,2},{2,1},{3,0},{4,7},{5,6},{6,5},{7,4},{8,11},{9,10},{10,... | collective-permute-start | bytes 884744 | tf_op jit(solution)/shard_map/ppermute | solution.py:266
  34.7 9.3 %collective-permute-start.9 = (bf16[256,512]{1,0:T(8,128)(2,1)S(1)}, bf16[256,512]{1,0:T(8,128)(2,1)S(1)}, u32[]{:S(2)}, u32[]{:S(2)}) collective-permute-start(bf16[256,512]{1,0:T(8,128)(2,1)S(1)} %pad_maximum_fusion), channel_id=1, source_target_pairs={{0,4},{4,0},{8,12},{12,8},{16,24},{20,28},{24,16},{28,20},{1,5},{5... | collective-permute-start | bytes 786440 | tf_op jit(solution)/shard_map/ppermute | solution.py:610
  59.4 5.7 %collective-permute-start.10 = (bf16[1024,1024]{1,0:T(8,128)(2,1)S(1)}, bf16[1024,1024]{1,0:T(8,128)(2,1)S(1)}, u32[]{:S(2)}, u32[]{:S(2)}) collective-permute-start(bf16[1024,1024]{1,0:T(8,128)(2,1)S(1)} %collective-permute-done.3.near), channel_id=1, source_target_pairs={{0,16},{16,0},{1,17},{17,1},{2,18},{18,2},{3,19},{19,3},{4,20},{20... | collective-permute-start | bytes 6291464 | tf_op jit(solution)/shard_map/ppermute | solution.py:266
  59.4 5.7 %collective-permute-start.11 = (bf16[512,1024]{1,0:T(8,128)(2,1)S(1)}, bf16[512,1024]{1,0:T(8,128)(2,1)S(1)}, u32[]{:S(2)}, u32[]{:S(2)}) collective-permute-start(bf16[512,1024]{1,0:T(8,128)(2,1)S(1)} %collective-permute-done.5.across), channel_id=1, source_target_pairs={{0,16},{16,0},{1,17},{17,1},{2,18},{18,2},{3,19},{19,3},{4,20},{20... | collective-permute-start | bytes 3145736 | tf_op jit(solution)/shard_map/ppermute | solution.py:266
  61.2 5.5 %collective-permute-start.12 = (f32[8,1024]{1,0:T(8,128)S(1)}, f32[8,1024]{1,0:T(8,128)S(1)}, u32[]{:S(2)}, u32[]{:S(2)}) collective-permute-start(f32[8,1024]{1,0:T(8,128)S(1)} %get-tuple-element.60.router_a), channel_id=1, source_target_pairs={{0,16},{16,0},{1,17},{17,1},{2,18},{18,2},{3,19},{19,3},{4,20},{20... | collective-permute-start | bytes 98312 | tf_op jit(solution)/shard_map/ppermute | solution.py:266
  69.5 7.3 %collective-permute-start.13 = (bf16[144,512]{1,0:T(8,128)(2,1)S(1)}, bf16[144,512]{1,0:T(8,128)(2,1)S(1)}, u32[]{:S(2)}, u32[]{:S(2)}) collective-permute-start(bf16[144,512]{1,0:T(8,128)(2,1)S(1)} %get-tuple-element.67), channel_id=1, source_target_pairs={{0,8},{4,12},{8,0},{12,4},{16,20},{20,16},{24,28},{28,24},{1,9},{5... | collective-permute-start | bytes 442376 | tf_op jit(solution)/shard_map/ppermute | solution.py:610
  70.6 6.4 %collective-permute-start.14 = (bf16[144,512]{1,0:T(8,128)(2,1)S(1)}, bf16[144,512]{1,0:T(8,128)(2,1)S(1)}, u32[]{:S(2)}, u32[]{:S(2)}) collective-permute-start(bf16[144,512]{1,0:T(8,128)(2,1)S(1)} %get-tuple-element.68), channel_id=1, source_target_pairs={{0,4},{4,0},{8,12},{12,8},{16,24},{20,28},{24,16},{28,20},{1,5},{5... | collective-permute-start | bytes 442376 | tf_op jit(solution)/shard_map/ppermute | solution.py:610
  71.1 7.9 %collective-permute-start.15 = (bf16[144,512]{1,0:T(8,128)(2,1)S(1)}, bf16[144,512]{1,0:T(8,128)(2,1)S(1)}, u32[]{:S(2)}, u32[]{:S(2)}) collective-permute-start(bf16[144,512]{1,0:T(8,128)(2,1)S(1)} %get-tuple-element.69), channel_id=1, source_target_pairs={{0,12},{4,8},{8,4},{12,0},{16,28},{20,24},{24,20},{28,16},{1,13},{... | collective-permute-start | bytes 442376 | tf_op jit(solution)/shard_map/ppermute | solution.py:610
